TPU v7x, 768 devices: a whole 4x8x12 slice. The times are simulated.
768 devices in a mesh: gx: 64 (over y, x, core), gy: 12 (over z).
Axes of the slice: x: 4, y: 8, z: 12, core: 2. Of those that a mesh axis runs over, the one named last changes fastest.
Arguments:
- density: float32 [512, 96, 128], P('gx', 'gy'), may hold values from 0.05 to 1
- solid: int32 [512, 96, 128], P('gx', 'gy'), may hold values 0 or 1
- void: int32 [512, 96, 128], P('gx', 'gy'), may hold values 0 or 1
- fixed: int32 [3, 512, 96, 128], P(None, 'gx', 'gy'), may hold values 0 or 1
- residual: float32 [3, 512, 96, 128], P(None, 'gx', 'gy'), may hold values from -6 to 6
Outputs:
- update: float32 [3, 512, 96, 128], P(None, 'gx', 'gy')
- next_residual: float32 [3, 512, 96, 128], P(None, 'gx', 'gy')
All inputs are finite; a program needn't handle non-finite values. No bound on the sum of `solid` or of `void` or of `fixed` on one device may be relied on, other than what follows from the above.
Results may differ from a plain program's by a relative error of at most 0.0003.
Values sent between devices are 32-bit elements; how exact they have to be, the bound alone decides.
No kernel may reach another device: no remote copies, remote signals or barrier semaphores. Data moves between devices by JAX's collectives and lax.ppermute only.
A program may use at most 64 MiB of HBM per device.

v0:
```python
import math

import jax
import jax.numpy as jnp
import numpy as np
from jax import lax
from jax.sharding import PartitionSpec as P

LEVELS = 4
COARSE_ITERS = 4


damping = 0.6
void_modulus = 0.001


def with_halo(shard, sides, width):
    for axis, dim in sides:
        peers, length = (lax.axis_size(axis), shard.shape[dim])
        up = [(i, (i + 1) % peers) for i in range(peers - 1)]
        down = [(j, i) for i, j in up]
        last = lax.slice_in_dim(shard, length - width, length, axis=dim)
        initial = lax.slice_in_dim(shard, 0, width, axis=dim)
        before = lax.ppermute(last, axis, up)
        after = lax.ppermute(initial, axis, down)
        shard = jnp.concatenate([before, shard, after], axis=dim)
    return shard


def corner_list():
    return [(a, b, c) for a in (0, 1) for b in (0, 1) for c in (0, 1)]


def element_stiffness():
    poisson = 0.3
    lame_first = poisson / ((1.0 + poisson) * (1.0 - 2.0 * poisson))
    shear = 0.5 / (1.0 + poisson)
    elastic = np.zeros((6, 6))
    elastic[:3, :3] = lame_first
    for i in range(3):
        elastic[i, i] += 2.0 * shear
        elastic[i + 3, i + 3] = shear
    points = [0.5 - 0.5 / math.sqrt(3.0), 0.5 + 0.5 / math.sqrt(3.0)]
    gauss = [(u, v, w) for u in points for v in points for w in points]
    stiffness = np.zeros((24, 24))
    for coord in gauss:
        strain = np.zeros((6, 24))
        for k, corner in enumerate(corner_list()):
            values = [coord[d] if corner[d] else 1.0 - coord[d] for d in range(3)]
            slopes = [2.0 * corner[d] - 1.0 for d in range(3)]
            grad_x = slopes[0] * values[1] * values[2]
            grad_y = values[0] * slopes[1] * values[2]
            grad_z = values[0] * values[1] * slopes[2]
            strain[0, 3 * k] = grad_x
            strain[1, 3 * k + 1] = grad_y
            strain[2, 3 * k + 2] = grad_z
            strain[3, 3 * k] = grad_y
            strain[3, 3 * k + 1] = grad_x
            strain[4, 3 * k + 1] = grad_z
            strain[4, 3 * k + 2] = grad_y
            strain[5, 3 * k] = grad_z
            strain[5, 3 * k + 2] = grad_x
        stiffness += strain.T @ elastic @ strain / 8.0
    return stiffness


def stiffness_diagonal():
    full = element_stiffness()
    return np.array([full[i, i] for i in range(24)])


def pad_last(field):
    return jnp.pad(field, ((0, 0), (0, 0), (0, 0), (1, 1)))


def grow_rims(field):
    return with_halo(field, (("gx", 1), ("gy", 2)), 1)


def grow_row(field):
    rimmed = with_halo(field, (("gx", 1),), 1)
    return jnp.pad(rimmed, ((0, 0), (0, 0), (1, 1), (0, 0)))


def grid_total(value):
    return lax.psum(value, ("gx", "gy"))


def row_total(value):
    return lax.psum(value, "gx")


def element_forces(wide, moduli_ext):
    stiffness = jnp.asarray(element_stiffness(), dtype=jnp.float32)
    nodes_x = wide.shape[1] - 2
    nodes_y = wide.shape[2] - 2
    nodes_z = wide.shape[3] - 2
    pieces = [
        wide[:, a : a + nodes_x + 1, b : b + nodes_y + 1, c : c + nodes_z + 1]
        for a, b, c in corner_list()
    ]
    stacked = jnp.concatenate(pieces, axis=0)
    layout = stacked.shape
    forces = jnp.dot(stiffness, stacked.reshape(24, -1), precision=lax.Precision.HIGHEST).reshape(
        layout
    )
    forces = forces * moduli_ext[None, : nodes_x + 1, : nodes_y + 1, : nodes_z + 1]
    total = jnp.zeros((3, nodes_x, nodes_y, nodes_z), jnp.float32)
    for k, (a, b, c) in enumerate(corner_list()):
        total = (
            total
            + forces[
                3 * k : 3 * k + 3,
                1 - a : 1 - a + nodes_x,
                1 - b : 1 - b + nodes_y,
                1 - c : 1 - c + nodes_z,
            ]
        )
    return total


def apply_operator(field, moduli_ext, free, grow):
    wide = pad_last(grow(field * free))
    return free * element_forces(wide, moduli_ext) + (1.0 - free) * field


def diagonal_of(moduli_ext, free):
    diag_table = stiffness_diagonal()
    nodes_x, nodes_y, nodes_z = (free.shape[1], free.shape[2], free.shape[3])
    total = jnp.zeros(free.shape, jnp.float32)
    for k, (a, b, c) in enumerate(corner_list()):
        entries = jnp.asarray(diag_table[3 * k : 3 * k + 3], dtype=jnp.float32)
        total = (
            total
            + entries[:, None, None, None]
            * moduli_ext[
                None, 1 - a : 1 - a + nodes_x, 1 - b : 1 - b + nodes_y, 1 - c : 1 - c + nodes_z
            ]
        )
    return free * total + (1.0 - free)


def restrict_field(field):
    wide = pad_last(grow_rims(field))
    for axis in (1, 2, 3):
        length = wide.shape[axis] - 2
        centre = lax.slice_in_dim(wide, 1, length + 1, 2, axis)
        lower = lax.slice_in_dim(wide, 0, length, 2, axis)
        upper = lax.slice_in_dim(wide, 2, length + 2, 2, axis)
        wide = centre + 0.5 * (lower + upper)
    return wide


def prolong_field(coarse):
    wide = pad_last(grow_rims(coarse))
    for axis in (1, 2, 3):
        length = wide.shape[axis] - 2
        base = lax.slice_in_dim(wide, 1, length + 1, 1, axis)
        after = lax.slice_in_dim(wide, 2, length + 2, 1, axis)
        middle = 0.5 * (base + after)
        joined = jnp.stack([base, middle], axis=axis + 1)
        target = list(base.shape)
        target[axis] = 2 * length
        wide = joined.reshape(target)
    return wide


def filter_density(density):
    stacked = jnp.stack([density, jnp.ones_like(density)])
    wide = pad_last(grow_rims(stacked))
    size_x, size_y, size_z = density.shape
    numer = jnp.zeros(density.shape, jnp.float32)
    denom = jnp.zeros(density.shape, jnp.float32)
    for dx in (-1, 0, 1):
        for dy in (-1, 0, 1):
            for dz in (-1, 0, 1):
                weight = 2.0 - math.sqrt(dx * dx + dy * dy + dz * dz)
                part = wide[
                    :, 1 + dx : 1 + dx + size_x, 1 + dy : 1 + dy + size_y, 1 + dz : 1 + dz + size_z
                ]
                numer = numer + weight * part[0]
                denom = denom + weight * part[1]
    return numer / denom


def coarsen_moduli(moduli):
    size_x, size_y, size_z = moduli.shape
    grouped = moduli.reshape(size_x // 2, 2, size_y // 2, 2, size_z // 2, 2)
    return 0.25 * jnp.sum(grouped, axis=(1, 3, 5))


def build_levels(moduli, free):
    levels = []
    frees = [free]
    for level in range(LEVELS - 1):
        moduli_ext = pad_last(grow_rims(moduli[None]))[0]
        levels.append((moduli_ext, diagonal_of(moduli_ext, frees[-1])))
        moduli = coarsen_moduli(moduli)
        frees.append(frees[-1][:, ::2, ::2, ::2])
    return (levels, frees, moduli)


def coarse_cg(rhs, moduli, free, grow, total):
    moduli_ext = pad_last(grow(moduli[None]))[0]
    diag = diagonal_of(moduli_ext, free)
    solution = jnp.zeros(rhs.shape, jnp.float32)
    resid = rhs
    precond = resid / diag
    direction = precond
    inner = total(jnp.sum(resid * precond))
    for step in range(COARSE_ITERS):
        image = apply_operator(direction, moduli_ext, free, grow)
        alpha = inner / total(jnp.sum(direction * image))
        solution = solution + alpha * direction
        resid = resid - alpha * image
        if step + 1 < COARSE_ITERS:
            precond = resid / diag
            inner_new = total(jnp.sum(resid * precond))
            direction = precond + inner_new / inner * direction
            inner = inner_new
    return solution


def coarse_solution(rhs, moduli, free):
    size_x, size_y = (rhs.shape[1], rhs.shape[2])
    packed = jnp.concatenate([moduli[None], free, rhs], axis=0)
    rows = lax.all_gather(packed, "gy", axis=2, tiled=True)
    column_start = lax.axis_index("gy") * size_y
    solved = coarse_cg(rows[4:], rows[0], rows[1:4], grow_row, row_total)
    return lax.dynamic_slice_in_dim(solved, column_start, size_y, 2)


def vcycle(level, rhs, levels, frees, coarse_moduli):
    if level == len(levels):
        return coarse_solution(rhs, coarse_moduli, frees[-1])
    moduli_ext, diag = levels[level]
    free = frees[level]
    smooth = damping * rhs / diag
    defect = rhs - apply_operator(smooth, moduli_ext, free, grow_rims)
    coarse_rhs = frees[level + 1] * restrict_field(defect)
    correction = vcycle(level + 1, coarse_rhs, levels, frees, coarse_moduli)
    smooth = smooth + free * prolong_field(correction)
    smooth = smooth + damping * (rhs - apply_operator(smooth, moduli_ext, free, grow_rims)) / diag
    return smooth


def on_device(density, solid, void, fixed, residual):
    free = 1.0 - fixed.astype(jnp.float32)
    filtered = filter_density(density)
    solid_f = solid.astype(jnp.float32)
    void_f = void.astype(jnp.float32)
    physical = (1.0 - void_f) * (solid_f + (1.0 - solid_f) * filtered)
    moduli = void_modulus + (1.0 - void_modulus) * physical**3
    levels, frees, coarse_moduli = build_levels(moduli, free)
    precond = vcycle(0, residual, levels, frees, coarse_moduli)
    image = apply_operator(precond, levels[0][0], free, grow_rims)
    numer = grid_total(jnp.sum(residual * precond))
    denom = grid_total(jnp.sum(precond * image))
    alpha = numer / denom
    return (alpha * precond, residual - alpha * image)


def solution(mesh):
    return jax.shard_map(
        on_device,
        mesh=mesh,
        in_specs=(
            P("gx", "gy", None),
            P("gx", "gy", None),
            P("gx", "gy", None),
            P(None, "gx", "gy", None),
            P(None, "gx", "gy", None),
        ),
        out_specs=(P(None, "gx", "gy", None), P(None, "gx", "gy", None)),
        check_vma=False,
    )
```

profile of v0, /device:TPU:1, one launch (start us, length us, event | category | flops | bytes accessed | tf_op | source)
XLA Modules:
  0.0 1452.1 jit_solution(81783963249095411)
XLA Ops:
  1.3 4.5 collective-permute-start
  5.8 9.2 collective-permute-start.1
  18.5 3.1 collective-permute-done.3
  35.2 3.5 collective-permute-start.6
  40.5 4.4 collective-permute-done.7
  45.3 4.8 collective-permute-start.8
  52.6 3.6 collective-permute-start.28
  58.2 4.8 collective-permute-start.10
  65.0 4.9 collective-permute-start.18
  74.9 3.1 fusion.194
  78.1 3.5 reshape.386
  83.2 4.2 collective-permute-start.12
  92.5 4.4 collective-permute-start.14
  104.7 3.1 collective-permute-start.20
  112.7 3.7 collective-permute-start.22
  117.7 5.5 collective-permute-start.30
  126.1 5.0 collective-permute-start.24
  136.7 5.2 collective-permute-start.26
  148.0 8.3 collective-permute-start.32
  158.3 3.7 collective-permute-done.33
  162.0 4.0 collective-permute-start.34
  167.3 4.3 collective-permute-done.35
  172.7 4.1 collective-permute-start.36
  178.9 3.3 collective-permute-done.37
  182.2 4.6 collective-permute-start.38
  192.4 17.8 %all_gather.3 = f32[7,1,12,16]{3,1,0,2:T(1,128)S(1)} all-gather(f32[7,1,1,16]{3,1,0,2:T(1,128)S(1)} %maximum_bitcast_fusion.3), channel_id=1, replica_groups=mesh['gx'=64,'gy'=12] {'gy'}, dimensions={2}, use_global_device_ids=true | all-gather | bytes 5824 | tf_op jit(solution)/shard_map/all_gather | solution.py:227
  210.3 6.2 collective-permute-start.41
  216.5 5.8 collective-permute-start.40
  225.3 4.2 collective-permute-start.42
  232.4 128.0 %all-reduce.29 = (f32[]{:T(128)}, f32[]{:T(128)}) all-reduce(f32[]{:T(128)} %get-tuple-element.5, f32[]{:T(128)} %get-tuple-element.4), channel_id=1, replica_groups=mesh['gx'=64,'gy'=12] {'gx'}, use_global_device_ids=true, to_apply=%region_5.6 | all-reduce | flops 2 | bytes 16 | tf_op jit(solution)/shard_map/psum | solution.py:90
  362.2 124.2 %psum.72 = f32[]{:T(128)} all-reduce(f32[]{:T(128)} %multiply_reduce_fusion.6), channel_id=1, replica_groups=mesh['gx'=64,'gy'=12] {'gx'}, use_global_device_ids=true, to_apply=%region_9.10 | all-reduce | flops 1 | bytes 8 | tf_op jit(solution)/shard_map/psum | solution.py:90
  496.2 123.5 %psum.73 = f32[]{:T(128)} all-reduce(f32[]{:T(128)} %get-tuple-element.21), channel_id=1, replica_groups=mesh['gx'=64,'gy'=12] {'gx'}, use_global_device_ids=true, to_apply=%region_11.12 | all-reduce | flops 1 | bytes 8 | tf_op jit(solution)/shard_map/psum | solution.py:90
  621.6 125.4 %psum.74 = f32[]{:T(128)} all-reduce(f32[]{:T(128)} %get-tuple-element.19), channel_id=1, replica_groups=mesh['gx'=64,'gy'=12] {'gx'}, use_global_device_ids=true, to_apply=%region_13.14 | all-reduce | flops 1 | bytes 8 | tf_op jit(solution)/shard_map/psum | solution.py:90
  750.8 3.0 collective-permute-start.46
  756.6 123.3 %psum.75 = f32[]{:T(128)} all-reduce(f32[]{:T(128)} %get-tuple-element.15), channel_id=1, replica_groups=mesh['gx'=64,'gy'=12] {'gx'}, use_global_device_ids=true, to_apply=%region_15.16 | all-reduce | flops 1 | bytes 8 | tf_op jit(solution)/shard_map/psum | solution.py:90
  881.8 125.9 %psum.76 = f32[]{:T(128)} all-reduce(f32[]{:T(128)} %multiply_reduce_fusion.2), channel_id=1, replica_groups=mesh['gx'=64,'gy'=12] {'gx'}, use_global_device_ids=true, to_apply=%region_17.18 | all-reduce | flops 1 | bytes 8 | tf_op jit(solution)/shard_map/psum | solution.py:90
  1011.5 3.0 collective-permute-start.48
  1017.4 123.3 %psum.77 = f32[]{:T(128)} all-reduce(f32[]{:T(128)} %fusion.112), channel_id=1, replica_groups=mesh['gx'=64,'gy'=12] {'gx'}, use_global_device_ids=true, to_apply=%region_19.20 | all-reduce | flops 1 | bytes 8 | tf_op jit(solution)/shard_map/psum | solution.py:90
  1142.0 3.7 collective-permute-start.51
  1150.1 4.0 collective-permute-start.52
  1155.5 4.9 collective-permute-start.54
  1165.3 3.9 collective-permute-start.56
  1170.5 3.1 collective-permute-done.57
  1174.7 3.4 collective-permute-start.58
  1186.0 4.0 collective-permute-done.61
  1190.8 3.1 collective-permute-start.62
  1195.9 3.0 collective-permute-done.63
  1198.9 4.8 collective-permute-start.64
  1205.0 3.4 collective-permute-done.65
  1209.8 3.1 collective-permute-start.66
  1214.9 3.0 collective-permute-done.67
  1217.9 3.6 collective-permute-start.68
  1227.7 3.4 collective-permute-start.70
  1233.0 3.1 collective-permute-done.71
  1240.3 3.2 collective-permute-done.73
  1246.5 3.1 fusion.203
  1249.6 3.5 reshape.414
  1255.4 3.4 collective-permute-start.74
  1260.7 3.1 collective-permute-done.75
  1263.8 3.3 collective-permute-start.76
  1268.7 3.2 collective-permute-done.77
  1274.9 3.1 fusion.204
  1278.0 3.5 reshape.416
  1283.8 164.0 %all-reduce.28 = (f32[]{:T(128)}, f32[]{:T(128)}) all-reduce(f32[]{:T(128)} %get-tuple-element.3, f32[]{:T(128)} %get-tuple-element.2), channel_id=1, replica_groups=mesh['gx'=64,'gy'=12] {'gx','gy'}, use_global_device_ids=true, to_apply=%region_21.22 | all-reduce | flops 2 | bytes 16 | tf_op jit(solution)/shard_map/psum | solution.py:86
  (450 shorter events, 161.7 us)
Async XLA Ops:
  1.3 14.5 collective-permute-start
  5.8 10.0 collective-permute-start.1
  25.1 10.1 collective-permute-start.4
  27.0 8.2 collective-permute-start.5
  30.1 33.0 %collective-permute-start.16 = (f32[1,1,4,64]{3,2,1,0:T(4,128)S(1)}, f32[1,1,4,64]{3,2,1,0:T(4,128)S(1)}, u32[]{:S(2)}, u32[]{:S(2)}) collective-permute-start(f32[1,1,4,64]{3,2,1,0:T(4,128)S(1)} %get-tuple-element.106), channel_id=1, source_target_pairs={{0,12},{12,24},{24,36},{36,48},{48,60},{60,72},{72,84},{84,96},{96... | collective-permute-start | bytes 3080 | tf_op jit(solution)/shard_map/ppermute | solution.py:24
  32.9 31.5 %collective-permute-start.17 = (f32[1,1,4,64]{3,2,1,0:T(4,128)S(1)}, f32[1,1,4,64]{3,2,1,0:T(4,128)S(1)}, u32[]{:S(2)}, u32[]{:S(2)}) collective-permute-start(f32[1,1,4,64]{3,2,1,0:T(4,128)S(1)} %get-tuple-element.107), channel_id=1, source_target_pairs={{12,0},{24,12},{36,24},{48,36},{60,48},{72,60},{84,72},{96,84},{10... | collective-permute-start | bytes 3080 | tf_op jit(solution)/shard_map/ppermute | solution.py:25
  35.2 5.3 collective-permute-start.6
  38.7 6.2 collective-permute-start.7
  45.3 11.0 collective-permute-start.8
  50.1 8.1 collective-permute-start.9
  52.6 57.1 %collective-permute-start.28 = (f32[1,1,2,32]{3,2,1,0:T(2,128)}, f32[1,1,2,32]{3,2,1,0:T(2,128)}, u32[]{:S(2)}, u32[]{:S(2)}) collective-permute-start(f32[1,1,2,32]{3,2,1,0:T(2,128)} %get-tuple-element.122), channel_id=1, source_target_pairs={{0,12},{12,24},{24,36},{36,48},{48,60},{60,72},{72,84},{84,96},{96... | collective-permute-start | bytes 776 | tf_op jit(solution)/shard_map/ppermute | solution.py:24
  56.2 53.5 %collective-permute-start.29 = (f32[1,1,2,32]{3,2,1,0:T(2,128)}, f32[1,1,2,32]{3,2,1,0:T(2,128)}, u32[]{:S(2)}, u32[]{:S(2)}) collective-permute-start(f32[1,1,2,32]{3,2,1,0:T(2,128)} %get-tuple-element.123), channel_id=1, source_target_pairs={{12,0},{24,12},{36,24},{48,36},{60,48},{72,60},{84,72},{96,84},{10... | collective-permute-start | bytes 776 | tf_op jit(solution)/shard_map/ppermute | solution.py:25
  58.2 12.3 collective-permute-start.10
  63.1 8.7 collective-permute-start.11
  65.0 22.4 %collective-permute-start.18 = (f32[1,6,1,64]{3,2,1,0:T(1,128)}, f32[1,6,1,64]{3,2,1,0:T(1,128)}, u32[]{:S(2)}, u32[]{:S(2)}) collective-permute-start(f32[1,6,1,64]{3,2,1,0:T(1,128)} %get-tuple-element.102), channel_id=1, source_target_pairs={{0,1},{1,2},{2,3},{3,4},{4,5},{5,6},{6,7},{7,8},{8,9},{9,10},{10,1... | collective-permute-start | bytes 4616 | tf_op jit(solution)/shard_map/ppermute | solution.py:24
  70.5 18.9 %collective-permute-start.19 = (f32[1,6,1,64]{3,2,1,0:T(1,128)}, f32[1,6,1,64]{3,2,1,0:T(1,128)}, u32[]{:S(2)}, u32[]{:S(2)}) collective-permute-start(f32[1,6,1,64]{3,2,1,0:T(1,128)} %get-tuple-element.103), channel_id=1, source_target_pairs={{1,0},{2,1},{3,2},{4,3},{5,4},{6,5},{7,6},{8,7},{9,8},{10,9},{11,1... | collective-permute-start | bytes 4616 | tf_op jit(solution)/shard_map/ppermute | solution.py:25
  83.2 7.0 collective-permute-start.12
  87.5 5.0 collective-permute-start.13
  92.5 7.7 collective-permute-start.14
  96.9 4.8 collective-permute-start.15
  104.7 5.7 collective-permute-start.20
  107.7 4.9 collective-permute-start.21
  112.7 12.0 collective-permute-start.22
  116.4 8.3 collective-permute-start.23
  117.7 15.3 %collective-permute-start.30 = (f32[1,4,1,32]{3,2,1,0:T(1,128)S(1)}, f32[1,4,1,32]{3,2,1,0:T(1,128)S(1)}, u32[]{:S(2)}, u32[]{:S(2)}) collective-permute-start(f32[1,4,1,32]{3,2,1,0:T(1,128)S(1)} %get-tuple-element.118), channel_id=1, source_target_pairs={{0,1},{1,2},{2,3},{3,4},{4,5},{5,6},{6,7},{7,8},{8,9},{9,10},{10,1... | collective-permute-start | bytes 1544 | tf_op jit(solution)/shard_map/ppermute | solution.py:24
  123.2 9.8 collective-permute-start.31
  126.1 7.7 collective-permute-start.24
  131.1 5.6 collective-permute-start.25
  136.7 7.3 collective-permute-start.26
  148.0 10.2 collective-permute-start.32
  156.3 5.6 collective-permute-start.33
  162.0 5.3 collective-permute-start.34
  166.0 5.6 collective-permute-start.35
  172.7 6.2 collective-permute-start.36
  176.8 5.4 collective-permute-start.37
  182.2 6.2 collective-permute-start.38
  210.3 12.1 collective-permute-start.41
  216.5 6.6 collective-permute-start.40
  223.3 6.2 collective-permute-start.43
  225.3 5.1 collective-permute-start.42
  487.7 5.6 collective-permute-start.45
  748.2 5.6 collective-permute-start.47
  1009.0 5.6 collective-permute-start.49
  1142.0 5.7 collective-permute-start.51
  1148.8 5.3 collective-permute-start.53
  1150.1 4.7 collective-permute-start.52
  1155.5 6.8 collective-permute-start.54
  1160.4 4.9 collective-permute-start.55
  1165.3 5.2 collective-permute-start.56
  1174.7 5.3 collective-permute-start.58
  1178.1 4.9 collective-permute-start.59
  1184.7 5.3 collective-permute-start.61
  1190.8 5.0 collective-permute-start.62
  1193.9 4.9 collective-permute-start.63
  1198.9 6.2 collective-permute-start.64
  1209.8 5.0 collective-permute-start.66
  1212.9 4.9 collective-permute-start.67
  1217.9 5.2 collective-permute-start.68
  1227.7 5.3 collective-permute-start.70
  1231.1 5.0 collective-permute-start.71
  1255.4 5.3 collective-permute-start.74
  1258.8 5.0 collective-permute-start.75
  1263.8 4.8 collective-permute-start.76
  1267.1 4.8 collective-permute-start.77
  (39 other events, 373.4 us)
where the time goes:
time: 1460 us; the launch traced here: 1450 us
  blocking collectives  1060 us (73%)
  starting transfers between devices  231 us (16%)
  waiting for transfers between devices  76.8 us (5%)
  local copies, waits for them, and re-layouts  40 us (3%)
  other arithmetic  24 us (2%)
    psum x7, blocking collectives, row_total(): return lax.psum(value, 'gx')  874 us
    psum x1, blocking collectives, grid_total(): return lax.psum(value, ('gx', 'gy'))  164 us
    ppermute x39, starting transfers between devices, with_halo(): before = lax.ppermute(last, axis, up)  150 us
    ppermute x39, starting transfers between devices, with_halo(): after = lax.ppermute(initial, axis, down)  81.3 us
    ppermute x39, waiting for transfers between devices, with_halo(): after = lax.ppermute(initial, axis, down)  70.5 us
  transfers between devices with their start and end apart: 78, of which 30 were waited for; matrix products, arithmetic and copies ran while one was open for 2% of the time, Pallas kernels for 0%

commit v1 on v0

--- a/solution.py
+++ b/solution.py
@@ -77,17 +77,22 @@
     return with_halo(field, (("gx", 1), ("gy", 2)), 1)
 
 
-def grow_row(field):
-    rimmed = with_halo(field, (("gx", 1),), 1)
-    return jnp.pad(rimmed, ((0, 0), (0, 0), (1, 1), (0, 0)))
-
-
-def grid_total(value):
-    return lax.psum(value, ("gx", "gy"))
-
-
-def row_total(value):
-    return lax.psum(value, "gx")
+def pad_sides(field):
+    return jnp.pad(field, ((0, 0), (1, 1), (1, 1), (0, 0)))
+
+
+def spread(row, axis):
+    peers = lax.axis_size(axis)
+    return lax.all_to_all(
+        jnp.broadcast_to(row[None], (peers,) + row.shape), axis, 0, 0, tiled=True
+    )
+
+
+def grid_totals(values):
+    row = jnp.pad(jnp.stack(values), (0, 128 - len(values)))
+    row = jnp.sum(spread(row, "gx"), axis=0)
+    row = jnp.sum(spread(row, "gy"), axis=0)
+    return [row[k] for k in range(len(values))]
 
 
 def element_forces(wide, moduli_ext):
@@ -200,34 +205,37 @@
     return (levels, frees, moduli)
 
 
-def coarse_cg(rhs, moduli, free, grow, total):
-    moduli_ext = pad_last(grow(moduli[None]))[0]
+def coarse_cg(rhs, moduli, free):
+    moduli_ext = pad_last(pad_sides(moduli[None]))[0]
     diag = diagonal_of(moduli_ext, free)
     solution = jnp.zeros(rhs.shape, jnp.float32)
     resid = rhs
     precond = resid / diag
     direction = precond
-    inner = total(jnp.sum(resid * precond))
+    inner = (jnp.sum(resid * precond))
     for step in range(COARSE_ITERS):
-        image = apply_operator(direction, moduli_ext, free, grow)
-        alpha = inner / total(jnp.sum(direction * image))
+        image = apply_operator(direction, moduli_ext, free, pad_sides)
+        alpha = inner / (jnp.sum(direction * image))
         solution = solution + alpha * direction
         resid = resid - alpha * image
         if step + 1 < COARSE_ITERS:
             precond = resid / diag
-            inner_new = total(jnp.sum(resid * precond))
+            inner_new = (jnp.sum(resid * precond))
             direction = precond + inner_new / inner * direction
             inner = inner_new
     return solution
 
 
 def coarse_solution(rhs, moduli, free):
-    size_x, size_y = (rhs.shape[1], rhs.shape[2])
-    packed = jnp.concatenate([moduli[None], free, rhs], axis=0)
-    rows = lax.all_gather(packed, "gy", axis=2, tiled=True)
-    column_start = lax.axis_index("gy") * size_y
-    solved = coarse_cg(rows[4:], rows[0], rows[1:4], grow_row, row_total)
-    return lax.dynamic_slice_in_dim(solved, column_start, size_y, 2)
+    size_x, size_y, size_z = rhs.shape[1:]
+    packed = jnp.concatenate([moduli[None], free, rhs], axis=0).reshape(-1)
+    rows = spread(spread(packed, "gx").reshape(-1), "gy")
+    peers_x, peers_y = (lax.axis_size("gx"), lax.axis_size("gy"))
+    rows = rows.reshape(peers_y, peers_x, 7, size_x, size_y, size_z)
+    rows = rows.transpose(2, 1, 3, 0, 4, 5).reshape(7, peers_x * size_x, peers_y * size_y, size_z)
+    solved = coarse_cg(rows[4:], rows[0], rows[1:4])
+    solved = lax.dynamic_slice_in_dim(solved, lax.axis_index("gx") * size_x, size_x, 1)
+    return lax.dynamic_slice_in_dim(solved, lax.axis_index("gy") * size_y, size_y, 2)
 
 
 def vcycle(level, rhs, levels, frees, coarse_moduli):
@@ -254,8 +262,7 @@
     levels, frees, coarse_moduli = build_levels(moduli, free)
     precond = vcycle(0, residual, levels, frees, coarse_moduli)
     image = apply_operator(precond, levels[0][0], free, grow_rims)
-    numer = grid_total(jnp.sum(residual * precond))
-    denom = grid_total(jnp.sum(precond * image))
+    numer, denom = grid_totals([jnp.sum(residual * precond), jnp.sum(precond * image)])
     alpha = numer / denom
     return (alpha * precond, residual - alpha * image)
 

time: 1460 us -> 709 us (0.49)
  blocking collectives: 1060 us -> 115 us
  local copies, waits for them, and re-layouts: 40 us -> 240 us
  waiting for transfers between devices: 76.8 us -> 31.1 us
    psum x8 -> x0, blocking collectives: 1040 us -> none  [the longest x7 874 us: row_total(): return lax.psum(value, 'gx')]
    all_to_all x0 -> x3, blocking collectives: none -> 115 us  [spread(): lax.all_to_all(jnp.broadcast_to(row[None], (peers,) + row.shape), axis, 0...]
    reshape x11 -> x15, local copies, waits for them, and re-layouts: 12.4 us -> 100 us  [element_forces(): jnp.dot(stiffness, stacked.reshape(24, -1), precision=lax.Precision.HIGHEST)]
    ppermute x39 -> x34, waiting for transfers between devices: 70.5 us -> 0.09 us  [with_halo(): after = lax.ppermute(initial, axis, down)]
    concatenate x11 -> x15, local copies, waits for them, and re-layouts: 0.94 us -> 42.8 us  [element_forces(): stacked = jnp.concatenate(pieces, axis=0)]
    reshape x11, local copies, waits for them, and re-layouts: 6.7 us -> 45.4 us  [element_forces(): stacked.reshape(24, -1)]
    unnamed x128 -> x164, local copies, waits for them, and re-layouts: 4.75 us -> 28.7 us
    all_to_all x0 -> x1, starting transfers between devices: none -> 18.4 us  [spread(): lax.all_to_all(jnp.broadcast_to(row[None], (peers,) + row.shape), axis, 0...]
  transfers between devices with their start and end apart: 78 -> 69, of which waited for: 30 -> 22; matrix products, arithmetic and copies ran while one was open for 2% -> 4% of each run, Pallas kernels for 0% -> 0%
where the time goes in v1:
time: 709 us; the launch traced here: 696 us
  local copies, waits for them, and re-layouts  240 us (34%)
  starting transfers between devices  240 us (34%)
  blocking collectives  115 us (16%)
  other arithmetic  37.9 us (5%)
  waiting for transfers between devices  31.1 us (4%)
  matrix products  18.5 us (3%)
  between operations  14.1 us (2%)
    ppermute x34, starting transfers between devices, with_halo(): before = lax.ppermute(last, axis, up)  152 us
    all_to_all x3, blocking collectives, spread(): lax.all_to_all(jnp.broadcast_to(row[None], (peers,) + row.shape), axis, 0...  115 us
    reshape x15, local copies, waits for them, and re-layouts, element_forces(): jnp.dot(stiffness, stacked.reshape(24, -1), precision=lax.Precision.HIGHEST)  100 us
    ppermute x34, starting transfers between devices, with_halo(): after = lax.ppermute(initial, axis, down)  69 us
    reshape x11, local copies, waits for them, and re-layouts, element_forces(): stacked.reshape(24, -1)  45.4 us
    concatenate x15, local copies, waits for them, and re-layouts, element_forces(): stacked = jnp.concatenate(pieces, axis=0)  42.8 us
    unnamed x164, local copies, waits for them, and re-layouts  28.7 us
    dot_general x11, matrix products, element_forces(): jnp.dot(stiffness, stacked.reshape(24, -1), precision=lax.Precision.HIGHEST)  18.5 us
  transfers between devices with their start and end apart: 69, of which 22 were waited for; matrix products, arithmetic and copies ran while one was open for 4% of the time, Pallas kernels for 0%

profile of v1, /device:TPU:1, one launch (start us, length us, event | category | flops | bytes accessed | tf_op | source)
XLA Modules:
  0.0 696.2 jit_solution(11934148668550802661)
XLA Ops:
  1.3 12.4 %collective-permute-start.1 = (f32[2,1,8,128]{3,2,1,0:T(8,128)S(1)}, f32[2,1,8,128]{3,2,1,0:T(8,128)S(1)}, u32[]{:S(2)}, u32[]{:S(2)}) collective-permute-start(f32[2,1,8,128]{3,2,1,0:T(8,128)S(1)} %get-tuple-element.71), channel_id=1, source_target_pairs={{12,0},{24,12},{36,24},{48,36},{60,48},{72,60},{84,72},{96,84},{10... | collective-permute-start | bytes 24584 | tf_op jit(solution)/shard_map/ppermute | solution.py:25
  18.1 4.0 collective-permute-start.2
  26.4 3.2 collective-permute-start.5
  29.6 3.7 collective-permute-start.4
  35.5 3.6 collective-permute-start.16
  40.9 4.5 collective-permute-start.6
  48.5 3.6 collective-permute-start.8
  54.6 3.6 collective-permute-start.28
  59.6 4.2 collective-permute-start.10
  66.5 4.6 collective-permute-start.18
  74.2 3.1 fusion.229
  77.3 3.5 reshape.332
  84.6 3.5 collective-permute-start.12
  90.2 4.0 collective-permute-start.14
  101.1 4.7 collective-permute-start.20
  107.9 4.0 collective-permute-start.22
  113.2 4.6 collective-permute-start.30
  121.2 5.2 collective-permute-start.24
  128.4 5.1 collective-permute-start.26
  138.0 4.9 collective-permute-start.32
  145.0 5.5 collective-permute-start.34
  154.3 5.0 collective-permute-start.36
  161.4 5.5 collective-permute-start.38
  168.9 52.4 %all_to_all.24 = f32[64,1,112]{2,1,0:T(1,128)S(1)} all-to-all(f32[64,1,112]{2,1,0:T(1,128)S(1)} %broadcast_in_dim.16), channel_id=1, replica_groups=mesh['gx'=64,'gy'=12] {'gx'}, dimensions={0} | all-to-all | bytes 57344 | tf_op jit(solution)/shard_map/all_to_all | solution.py:86
  223.4 18.4 %all-to-all-start.1 = ((f32[12,1,7168]{2,1,0:T(1,128)}), f32[12,1,7168]{2,1,0:T(1,128)S(1)}, u32[]{:S(2)}, u32[]{:S(2)}) async-start(f32[12,1,7168]{2,1,0:T(1,128)} %broadcast_in_dim.18), calls=%async_computation.1 | async-start | bytes 688128 | tf_op jit(solution)/shard_map/all_to_all | solution.py:86
  241.9 17.1 %all-to-all-done.1 = f32[12,1,7168]{2,1,0:T(1,128)S(1)} async-done(((f32[12,1,7168]{2,1,0:T(1,128)}), f32[12,1,7168]{2,1,0:T(1,128)S(1)}, u32[]{:S(2)}, u32[]{:S(2)}) %all-to-all-start.1) | async-done | bytes 344096 | tf_op jit(solution)/shard_map/all_to_all | solution.py:86
  259.8 2.6 reshape.338
  272.4 9.6 %copy.304 = f32[24,65,13,17]{3,2,1,0:T(8,128)} copy(f32[24,65,13,17]{1,3,2,0:T(8,128)} %fusion.1) | data formatting | bytes 2758080 | tf_op jit(solution)/shard_map/concatenate | solution.py:107
  282.1 9.8 %reshape.339 = f32[24,14365]{1,0:T(8,128)S(1)} reshape(f32[24,65,13,17]{3,2,1,0:T(8,128)} %copy.304) | data formatting | bytes 2758080 | tf_op jit(solution)/shard_map/reshape | solution.py:109
  294.2 13.6 %reshape.340 = f32[24,65,13,17]{3,2,1,0:T(8,128)} reshape(f32[24,14365]{1,0:T(8,128)} %fusion.232) | data formatting | bytes 2758080 | tf_op jit(solution)/shard_map/reshape | solution.py:109
  307.8 9.4 %copy.306 = f32[24,65,13,17]{1,3,2,0:T(8,128)} copy(f32[24,65,13,17]{3,2,1,0:T(8,128)} %reshape.340) | data formatting | bytes 2758080 | tf_op jit(solution)/shard_map/reshape | solution.py:109
  317.3 2.4 broadcast_multiply_fusion.3
  331.4 9.6 %copy.307 = f32[24,65,13,17]{3,2,1,0:T(8,128)} copy(f32[24,65,13,17]{1,3,2,0:T(8,128)} %fusion.9) | data formatting | bytes 2758080 | tf_op jit(solution)/shard_map/concatenate | solution.py:107
  341.0 10.0 %reshape.341 = f32[24,14365]{1,0:T(8,128)S(1)} reshape(f32[24,65,13,17]{3,2,1,0:T(8,128)} %copy.307) | data formatting | bytes 2758080 | tf_op jit(solution)/shard_map/reshape | solution.py:109
  353.4 13.6 %reshape.342 = f32[24,65,13,17]{3,2,1,0:T(8,128)} reshape(f32[24,14365]{1,0:T(8,128)} %fusion.233) | data formatting | bytes 2758080 | tf_op jit(solution)/shard_map/reshape | solution.py:109
  366.9 9.4 %copy.308 = f32[24,65,13,17]{1,3,2,0:T(8,128)} copy(f32[24,65,13,17]{3,2,1,0:T(8,128)} %reshape.342) | data formatting | bytes 2758080 | tf_op jit(solution)/shard_map/reshape | solution.py:109
  390.3 9.6 %copy.309 = f32[24,65,13,17]{3,2,1,0:T(8,128)} copy(f32[24,65,13,17]{1,3,2,0:T(8,128)} %fusion.17) | data formatting | bytes 2758080 | tf_op jit(solution)/shard_map/concatenate | solution.py:107
  399.9 9.8 %reshape.343 = f32[24,14365]{1,0:T(8,128)S(1)} reshape(f32[24,65,13,17]{3,2,1,0:T(8,128)} %copy.309) | data formatting | bytes 2758080 | tf_op jit(solution)/shard_map/reshape | solution.py:109
  412.1 13.6 %reshape.344 = f32[24,65,13,17]{3,2,1,0:T(8,128)} reshape(f32[24,14365]{1,0:T(8,128)} %fusion.234) | data formatting | bytes 2758080 | tf_op jit(solution)/shard_map/reshape | solution.py:109
  425.7 9.6 %copy.310 = f32[24,65,13,17]{1,3,2,0:T(8,128)} copy(f32[24,65,13,17]{3,2,1,0:T(8,128)} %reshape.344) | data formatting | bytes 2758080 | tf_op jit(solution)/shard_map/reshape | solution.py:109
  450.1 9.6 %copy.311 = f32[24,65,13,17]{3,2,1,0:T(8,128)} copy(f32[24,65,13,17]{1,3,2,0:T(8,128)} %fusion.25) | data formatting | bytes 2758080 | tf_op jit(solution)/shard_map/concatenate | solution.py:107
  459.7 9.8 %reshape.345 = f32[24,14365]{1,0:T(8,128)S(1)} reshape(f32[24,65,13,17]{3,2,1,0:T(8,128)} %copy.311) | data formatting | bytes 2758080 | tf_op jit(solution)/shard_map/reshape | solution.py:109
  470.8 10.5 %reshape.346 = f32[24,65,13,17]{3,2,1,0:T(8,128)} reshape(f32[24,14365]{1,0:T(8,128)S(1)} %fusion.235) | data formatting | bytes 2758080 | tf_op jit(solution)/shard_map/reshape | solution.py:109
  481.3 9.5 %copy.312 = f32[24,65,13,17]{1,3,2,0:T(8,128)} copy(f32[24,65,13,17]{3,2,1,0:T(8,128)} %reshape.346) | data formatting | bytes 2758080 | tf_op jit(solution)/shard_map/reshape | solution.py:109
  496.4 4.2 collective-permute-start.41
  505.1 5.0 collective-permute-start.42
  513.6 4.8 collective-permute-start.44
  520.5 4.5 collective-permute-start.46
  528.9 5.0 collective-permute-start.48
  536.0 4.5 collective-permute-start.50
  544.0 5.0 collective-permute-start.52
  551.2 4.5 collective-permute-start.54
  559.8 5.0 collective-permute-start.56
  566.9 4.9 collective-permute-start.58
  575.9 5.0 collective-permute-start.60
  583.1 4.9 collective-permute-start.62
  592.0 3.1 fusion.238
  595.1 3.5 reshape.361
  602.8 5.1 collective-permute-start.64
  610.0 5.9 collective-permute-start.66
  619.7 3.1 fusion.239
  622.8 3.5 reshape.363
  629.7 39.6 %all_to_all.25 = f32[64,1,128]{2,1,0:T(1,128)S(1)} all-to-all(f32[64,1,128]{2,1,0:T(1,128)S(1)} %broadcast_in_dim.19), channel_id=1, replica_groups=mesh['gx'=64,'gy'=12] {'gx'}, dimensions={0} | all-to-all | bytes 65536 | tf_op jit(solution)/shard_map/all_to_all | solution.py:86
  669.3 23.1 %all_to_all.26 = f32[12,1,128]{2,1,0:T(1,128)S(1)} all-to-all(f32[12,1,128]{2,1,0:T(1,128)S(1)} %broadcast_in_dim.20), channel_id=1, replica_groups=mesh['gx'=64,'gy'=12] {'gy'}, dimensions={0} | all-to-all | bytes 12288 | tf_op jit(solution)/shard_map/all_to_all | solution.py:86
  (484 shorter events, 171.5 us)
Async XLA Ops:
  1.3 15.1 %collective-permute-start.1 = (f32[2,1,8,128]{3,2,1,0:T(8,128)S(1)}, f32[2,1,8,128]{3,2,1,0:T(8,128)S(1)}, u32[]{:S(2)}, u32[]{:S(2)}) collective-permute-start(f32[2,1,8,128]{3,2,1,0:T(8,128)S(1)} %get-tuple-element.71), channel_id=1, source_target_pairs={{12,0},{24,12},{36,24},{48,36},{60,48},{72,60},{84,72},{96,84},{10... | collective-permute-start | bytes 24584 | tf_op jit(solution)/shard_map/ppermute | solution.py:25
  16.8 5.3 collective-permute-start.3
  26.4 13.1 %collective-permute-start.5 = (f32[1,1,8,128]{3,2,1,0:T(8,128)S(1)}, f32[1,1,8,128]{3,2,1,0:T(8,128)S(1)}, u32[]{:S(2)}, u32[]{:S(2)}) collective-permute-start(f32[1,1,8,128]{3,2,1,0:T(8,128)S(1)} %get-tuple-element.69), channel_id=1, source_target_pairs={{12,0},{24,12},{36,24},{48,36},{60,48},{72,60},{84,72},{96,84},{10... | collective-permute-start | bytes 12296 | tf_op jit(solution)/shard_map/ppermute | solution.py:25
  29.6 9.9 %collective-permute-start.4 = (f32[1,1,8,128]{3,2,1,0:T(8,128)S(1)}, f32[1,1,8,128]{3,2,1,0:T(8,128)S(1)}, u32[]{:S(2)}, u32[]{:S(2)}) collective-permute-start(f32[1,1,8,128]{3,2,1,0:T(8,128)S(1)} %get-tuple-element.68), channel_id=1, source_target_pairs={{0,12},{12,24},{24,36},{36,48},{48,60},{60,72},{72,84},{84,96},{96... | collective-permute-start | bytes 12296 | tf_op jit(solution)/shard_map/ppermute | solution.py:24
  33.6 26.0 %collective-permute-start.17 = (f32[1,1,4,64]{3,2,1,0:T(4,128)S(1)}, f32[1,1,4,64]{3,2,1,0:T(4,128)S(1)}, u32[]{:S(2)}, u32[]{:S(2)}) collective-permute-start(f32[1,1,4,64]{3,2,1,0:T(4,128)S(1)} %get-tuple-element.103), channel_id=1, source_target_pairs={{12,0},{24,12},{36,24},{48,36},{60,48},{72,60},{84,72},{96,84},{10... | collective-permute-start | bytes 3080 | tf_op jit(solution)/shard_map/ppermute | solution.py:25
  35.5 28.4 %collective-permute-start.16 = (f32[1,1,4,64]{3,2,1,0:T(4,128)S(1)}, f32[1,1,4,64]{3,2,1,0:T(4,128)S(1)}, u32[]{:S(2)}, u32[]{:S(2)}) collective-permute-start(f32[1,1,4,64]{3,2,1,0:T(4,128)S(1)} %get-tuple-element.102), channel_id=1, source_target_pairs={{0,12},{12,24},{24,36},{36,48},{48,60},{60,72},{72,84},{84,96},{96... | collective-permute-start | bytes 3080 | tf_op jit(solution)/shard_map/ppermute | solution.py:24
  39.6 6.4 collective-permute-start.7
  46.5 8.1 %collective-permute-start.9 = (f32[3,1,8,128]{3,2,1,0:T(8,128)S(1)}, f32[3,1,8,128]{3,2,1,0:T(8,128)S(1)}, u32[]{:S(2)}, u32[]{:S(2)}) collective-permute-start(f32[3,1,8,128]{3,2,1,0:T(8,128)S(1)} %get-tuple-element.49), channel_id=1, source_target_pairs={{12,0},{24,12},{36,24},{48,36},{60,48},{72,60},{84,72},{96,84},{10... | collective-permute-start | bytes 36872 | tf_op jit(solution)/shard_map/ppermute | solution.py:25
  48.5 9.8 %collective-permute-start.8 = (f32[3,1,8,128]{3,2,1,0:T(8,128)S(1)}, f32[3,1,8,128]{3,2,1,0:T(8,128)S(1)}, u32[]{:S(2)}, u32[]{:S(2)}) collective-permute-start(f32[3,1,8,128]{3,2,1,0:T(8,128)S(1)} %get-tuple-element.48), channel_id=1, source_target_pairs={{0,12},{12,24},{24,36},{36,48},{48,60},{60,72},{72,84},{84,96},{96... | collective-permute-start | bytes 36872 | tf_op jit(solution)/shard_map/ppermute | solution.py:24
  52.7 53.1 %collective-permute-start.29 = (f32[1,1,2,32]{3,2,1,0:T(2,128)}, f32[1,1,2,32]{3,2,1,0:T(2,128)}, u32[]{:S(2)}, u32[]{:S(2)}) collective-permute-start(f32[1,1,2,32]{3,2,1,0:T(2,128)} %get-tuple-element.119), channel_id=1, source_target_pairs={{12,0},{24,12},{36,24},{48,36},{60,48},{72,60},{84,72},{96,84},{10... | collective-permute-start | bytes 776 | tf_op jit(solution)/shard_map/ppermute | solution.py:25
  54.6 51.2 %collective-permute-start.28 = (f32[1,1,2,32]{3,2,1,0:T(2,128)}, f32[1,1,2,32]{3,2,1,0:T(2,128)}, u32[]{:S(2)}, u32[]{:S(2)}) collective-permute-start(f32[1,1,2,32]{3,2,1,0:T(2,128)} %get-tuple-element.118), channel_id=1, source_target_pairs={{0,12},{12,24},{24,36},{36,48},{48,60},{60,72},{72,84},{84,96},{96... | collective-permute-start | bytes 776 | tf_op jit(solution)/shard_map/ppermute | solution.py:24
  58.3 8.2 %collective-permute-start.11 = (f32[3,10,1,128]{3,2,1,0:T(1,128)S(1)}, f32[3,10,1,128]{3,2,1,0:T(1,128)S(1)}, u32[]{:S(2)}, u32[]{:S(2)}) collective-permute-start(f32[3,10,1,128]{3,2,1,0:T(1,128)S(1)} %get-tuple-element.37), channel_id=1, source_target_pairs={{1,0},{2,1},{3,2},{4,3},{5,4},{6,5},{7,6},{8,7},{9,8},{10,9},{11,1... | collective-permute-start | bytes 46088 | tf_op jit(solution)/shard_map/ppermute | solution.py:25
  59.6 11.4 %collective-permute-start.10 = (f32[3,10,1,128]{3,2,1,0:T(1,128)S(1)}, f32[3,10,1,128]{3,2,1,0:T(1,128)S(1)}, u32[]{:S(2)}, u32[]{:S(2)}) collective-permute-start(f32[3,10,1,128]{3,2,1,0:T(1,128)S(1)} %get-tuple-element.36), channel_id=1, source_target_pairs={{0,1},{1,2},{2,3},{3,4},{4,5},{5,6},{6,7},{7,8},{8,9},{9,10},{10,1... | collective-permute-start | bytes 46088 | tf_op jit(solution)/shard_map/ppermute | solution.py:24
  64.5 20.0 %collective-permute-start.19 = (f32[1,6,1,64]{3,2,1,0:T(1,128)}, f32[1,6,1,64]{3,2,1,0:T(1,128)}, u32[]{:S(2)}, u32[]{:S(2)}) collective-permute-start(f32[1,6,1,64]{3,2,1,0:T(1,128)} %get-tuple-element.97), channel_id=1, source_target_pairs={{1,0},{2,1},{3,2},{4,3},{5,4},{6,5},{7,6},{8,7},{9,8},{10,9},{11,1... | collective-permute-start | bytes 4616 | tf_op jit(solution)/shard_map/ppermute | solution.py:25
  66.5 21.6 %collective-permute-start.18 = (f32[1,6,1,64]{3,2,1,0:T(1,128)}, f32[1,6,1,64]{3,2,1,0:T(1,128)}, u32[]{:S(2)}, u32[]{:S(2)}) collective-permute-start(f32[1,6,1,64]{3,2,1,0:T(1,128)} %get-tuple-element.96), channel_id=1, source_target_pairs={{0,1},{1,2},{2,3},{3,4},{4,5},{5,6},{6,7},{7,8},{8,9},{9,10},{10,1... | collective-permute-start | bytes 4616 | tf_op jit(solution)/shard_map/ppermute | solution.py:24
  82.4 6.4 collective-permute-start.13
  88.9 7.3 %collective-permute-start.15 = (f32[3,10,1,128]{3,2,1,0:T(1,128)S(1)}, f32[3,10,1,128]{3,2,1,0:T(1,128)S(1)}, u32[]{:S(2)}, u32[]{:S(2)}) collective-permute-start(f32[3,10,1,128]{3,2,1,0:T(1,128)S(1)} %get-tuple-element.35), channel_id=1, source_target_pairs={{1,0},{2,1},{3,2},{4,3},{5,4},{6,5},{7,6},{8,7},{9,8},{10,9},{11,1... | collective-permute-start | bytes 46088 | tf_op jit(solution)/shard_map/ppermute | solution.py:25
  90.2 6.0 collective-permute-start.14
  99.2 7.4 %collective-permute-start.21 = (f32[3,1,4,64]{3,2,1,0:T(4,128)S(1)}, f32[3,1,4,64]{3,2,1,0:T(4,128)S(1)}, u32[]{:S(2)}, u32[]{:S(2)}) collective-permute-start(f32[3,1,4,64]{3,2,1,0:T(4,128)S(1)} %get-tuple-element.85), channel_id=1, source_target_pairs={{12,0},{24,12},{36,24},{48,36},{60,48},{72,60},{84,72},{96,84},{10... | collective-permute-start | bytes 9224 | tf_op jit(solution)/shard_map/ppermute | solution.py:25
  101.1 5.5 collective-permute-start.20
  106.6 11.2 %collective-permute-start.23 = (f32[3,6,1,64]{3,2,1,0:T(1,128)S(1)}, f32[3,6,1,64]{3,2,1,0:T(1,128)S(1)}, u32[]{:S(2)}, u32[]{:S(2)}) collective-permute-start(f32[3,6,1,64]{3,2,1,0:T(1,128)S(1)} %get-tuple-element.67), channel_id=1, source_target_pairs={{1,0},{2,1},{3,2},{4,3},{5,4},{6,5},{7,6},{8,7},{9,8},{10,9},{11,1... | collective-permute-start | bytes 13832 | tf_op jit(solution)/shard_map/ppermute | solution.py:25
  107.9 10.0 %collective-permute-start.22 = (f32[3,6,1,64]{3,2,1,0:T(1,128)S(1)}, f32[3,6,1,64]{3,2,1,0:T(1,128)S(1)}, u32[]{:S(2)}, u32[]{:S(2)}) collective-permute-start(f32[3,6,1,64]{3,2,1,0:T(1,128)S(1)} %get-tuple-element.66), channel_id=1, source_target_pairs={{0,1},{1,2},{2,3},{3,4},{4,5},{5,6},{6,7},{7,8},{8,9},{9,10},{10,1... | collective-permute-start | bytes 13832 | tf_op jit(solution)/shard_map/ppermute | solution.py:24
  111.9 14.4 %collective-permute-start.31 = (f32[1,4,1,32]{3,2,1,0:T(1,128)S(1)}, f32[1,4,1,32]{3,2,1,0:T(1,128)S(1)}, u32[]{:S(2)}, u32[]{:S(2)}) collective-permute-start(f32[1,4,1,32]{3,2,1,0:T(1,128)S(1)} %get-tuple-element.115), channel_id=1, source_target_pairs={{1,0},{2,1},{3,2},{4,3},{5,4},{6,5},{7,6},{8,7},{9,8},{10,9},{11,1... | collective-permute-start | bytes 1544 | tf_op jit(solution)/shard_map/ppermute | solution.py:25
  113.2 13.1 %collective-permute-start.30 = (f32[1,4,1,32]{3,2,1,0:T(1,128)S(1)}, f32[1,4,1,32]{3,2,1,0:T(1,128)S(1)}, u32[]{:S(2)}, u32[]{:S(2)}) collective-permute-start(f32[1,4,1,32]{3,2,1,0:T(1,128)S(1)} %get-tuple-element.114), channel_id=1, source_target_pairs={{0,1},{1,2},{2,3},{3,4},{4,5},{5,6},{6,7},{7,8},{8,9},{9,10},{10,1... | collective-permute-start | bytes 1544 | tf_op jit(solution)/shard_map/ppermute | solution.py:24
  119.2 7.9 %collective-permute-start.25 = (f32[3,1,4,64]{3,2,1,0:T(4,128)S(1)}, f32[3,1,4,64]{3,2,1,0:T(4,128)S(1)}, u32[]{:S(2)}, u32[]{:S(2)}) collective-permute-start(f32[3,1,4,64]{3,2,1,0:T(4,128)S(1)} %get-tuple-element.83), channel_id=1, source_target_pairs={{12,0},{24,12},{36,24},{48,36},{60,48},{72,60},{84,72},{96,84},{10... | collective-permute-start | bytes 9224 | tf_op jit(solution)/shard_map/ppermute | solution.py:25
  121.2 6.0 collective-permute-start.24
  127.1 7.2 %collective-permute-start.27 = (f32[3,6,1,64]{3,2,1,0:T(1,128)S(1)}, f32[3,6,1,64]{3,2,1,0:T(1,128)S(1)}, u32[]{:S(2)}, u32[]{:S(2)}) collective-permute-start(f32[3,6,1,64]{3,2,1,0:T(1,128)S(1)} %get-tuple-element.65), channel_id=1, source_target_pairs={{1,0},{2,1},{3,2},{4,3},{5,4},{6,5},{7,6},{8,7},{9,8},{10,9},{11,1... | collective-permute-start | bytes 13832 | tf_op jit(solution)/shard_map/ppermute | solution.py:25
  128.4 5.9 collective-permute-start.26
  136.1 6.9 collective-permute-start.33
  138.0 5.7 collective-permute-start.32
  143.7 6.8 collective-permute-start.35
  145.0 6.2 collective-permute-start.34
  152.3 7.2 %collective-permute-start.37 = (f32[3,1,2,32]{3,2,1,0:T(2,128)S(1)}, f32[3,1,2,32]{3,2,1,0:T(2,128)S(1)}, u32[]{:S(2)}, u32[]{:S(2)}) collective-permute-start(f32[3,1,2,32]{3,2,1,0:T(2,128)S(1)} %get-tuple-element.111), channel_id=1, source_target_pairs={{12,0},{24,12},{36,24},{48,36},{60,48},{72,60},{84,72},{96,84},{10... | collective-permute-start | bytes 2312 | tf_op jit(solution)/shard_map/ppermute | solution.py:25
  154.3 5.8 collective-permute-start.36
  160.1 7.2 %collective-permute-start.39 = (f32[3,4,1,32]{3,2,1,0:T(1,128)S(1)}, f32[3,4,1,32]{3,2,1,0:T(1,128)S(1)}, u32[]{:S(2)}, u32[]{:S(2)}) collective-permute-start(f32[3,4,1,32]{3,2,1,0:T(1,128)S(1)} %get-tuple-element.93), channel_id=1, source_target_pairs={{1,0},{2,1},{3,2},{4,3},{5,4},{6,5},{7,6},{8,7},{9,8},{10,9},{11,1... | collective-permute-start | bytes 4616 | tf_op jit(solution)/shard_map/ppermute | solution.py:25
  161.4 6.2 collective-permute-start.38
  223.4 35.6 %all-to-all-start.1 = ((f32[12,1,7168]{2,1,0:T(1,128)}), f32[12,1,7168]{2,1,0:T(1,128)S(1)}, u32[]{:S(2)}, u32[]{:S(2)}) async-start(f32[12,1,7168]{2,1,0:T(1,128)} %broadcast_in_dim.18), calls=%async_computation.1 | async-start | bytes 688128 | tf_op jit(solution)/shard_map/all_to_all | solution.py:86
  496.4 6.4 collective-permute-start.41
  503.8 6.3 collective-permute-start.43
  505.1 5.8 collective-permute-start.42
  511.5 7.0 %collective-permute-start.45 = (f32[3,1,2,32]{3,2,1,0:T(2,128)S(1)}, f32[3,1,2,32]{3,2,1,0:T(2,128)S(1)}, u32[]{:S(2)}, u32[]{:S(2)}) collective-permute-start(f32[3,1,2,32]{3,2,1,0:T(2,128)S(1)} %get-tuple-element.107), channel_id=1, source_target_pairs={{12,0},{24,12},{36,24},{48,36},{60,48},{72,60},{84,72},{96,84},{10... | collective-permute-start | bytes 2312 | tf_op jit(solution)/shard_map/ppermute | solution.py:25
  513.6 5.5 collective-permute-start.44
  519.2 5.8 collective-permute-start.47
  520.5 5.3 collective-permute-start.46
  526.9 7.0 %collective-permute-start.49 = (f32[3,1,2,32]{3,2,1,0:T(2,128)S(1)}, f32[3,1,2,32]{3,2,1,0:T(2,128)S(1)}, u32[]{:S(2)}, u32[]{:S(2)}) collective-permute-start(f32[3,1,2,32]{3,2,1,0:T(2,128)S(1)} %get-tuple-element.105), channel_id=1, source_target_pairs={{12,0},{24,12},{36,24},{48,36},{60,48},{72,60},{84,72},{96,84},{10... | collective-permute-start | bytes 2312 | tf_op jit(solution)/shard_map/ppermute | solution.py:25
  528.9 5.8 collective-permute-start.48
  534.7 5.8 collective-permute-start.51
  536.0 5.3 collective-permute-start.50
  542.1 7.0 %collective-permute-start.53 = (f32[3,1,4,64]{3,2,1,0:T(4,128)S(1)}, f32[3,1,4,64]{3,2,1,0:T(4,128)S(1)}, u32[]{:S(2)}, u32[]{:S(2)}) collective-permute-start(f32[3,1,4,64]{3,2,1,0:T(4,128)S(1)} %get-tuple-element.75), channel_id=1, source_target_pairs={{12,0},{24,12},{36,24},{48,36},{60,48},{72,60},{84,72},{96,84},{10... | collective-permute-start | bytes 9224 | tf_op jit(solution)/shard_map/ppermute | solution.py:25
  544.0 5.8 collective-permute-start.52
  549.9 5.8 collective-permute-start.55
  551.2 5.3 collective-permute-start.54
  557.9 7.0 %collective-permute-start.57 = (f32[3,1,4,64]{3,2,1,0:T(4,128)S(1)}, f32[3,1,4,64]{3,2,1,0:T(4,128)S(1)}, u32[]{:S(2)}, u32[]{:S(2)}) collective-permute-start(f32[3,1,4,64]{3,2,1,0:T(4,128)S(1)} %get-tuple-element.73), channel_id=1, source_target_pairs={{12,0},{24,12},{36,24},{48,36},{60,48},{72,60},{84,72},{96,84},{10... | collective-permute-start | bytes 9224 | tf_op jit(solution)/shard_map/ppermute | solution.py:25
  559.8 5.8 collective-permute-start.56
  565.6 6.3 collective-permute-start.59
  566.9 5.3 collective-permute-start.58
  574.0 7.0 %collective-permute-start.61 = (f32[3,1,8,128]{3,2,1,0:T(8,128)S(1)}, f32[3,1,8,128]{3,2,1,0:T(8,128)S(1)}, u32[]{:S(2)}, u32[]{:S(2)}) collective-permute-start(f32[3,1,8,128]{3,2,1,0:T(8,128)S(1)} %get-tuple-element.41), channel_id=1, source_target_pairs={{12,0},{24,12},{36,24},{48,36},{60,48},{72,60},{84,72},{96,84},{10... | collective-permute-start | bytes 36872 | tf_op jit(solution)/shard_map/ppermute | solution.py:25
  575.9 5.9 collective-permute-start.60
  581.8 6.2 collective-permute-start.63
  583.1 5.8 collective-permute-start.62
  600.9 7.0 %collective-permute-start.65 = (f32[3,1,8,128]{3,2,1,0:T(8,128)S(1)}, f32[3,1,8,128]{3,2,1,0:T(8,128)S(1)}, u32[]{:S(2)}, u32[]{:S(2)}) collective-permute-start(f32[3,1,8,128]{3,2,1,0:T(8,128)S(1)} %get-tuple-element.39), channel_id=1, source_target_pairs={{12,0},{24,12},{36,24},{48,36},{60,48},{72,60},{84,72},{96,84},{10... | collective-permute-start | bytes 36872 | tf_op jit(solution)/shard_map/ppermute | solution.py:25
  602.8 5.9 collective-permute-start.64
  608.7 7.2 %collective-permute-start.67 = (f32[3,10,1,128]{3,2,1,0:T(1,128)S(1)}, f32[3,10,1,128]{3,2,1,0:T(1,128)S(1)}, u32[]{:S(2)}, u32[]{:S(2)}) collective-permute-start(f32[3,10,1,128]{3,2,1,0:T(1,128)S(1)} %get-tuple-element.31), channel_id=1, source_target_pairs={{1,0},{2,1},{3,2},{4,3},{5,4},{6,5},{7,6},{8,7},{9,8},{10,9},{11,1... | collective-permute-start | bytes 46088 | tf_op jit(solution)/shard_map/ppermute | solution.py:25
  610.0 6.6 collective-permute-start.66
  (48 other events, 1446.9 us)

commit v2 on v1

v2 whole, which is shorter than its diff:
```python
import math

import jax
import jax.numpy as jnp
import numpy as np
from jax import lax
from jax.experimental import pallas as pl
from jax.experimental.pallas import tpu as pltpu
from jax.sharding import PartitionSpec as P

COARSE_ITERS = 4
DAMPING = 0.6
VOID_MODULUS = 0.001
F32 = jnp.float32
PARAMS = pltpu.CompilerParams(vmem_limit_bytes=48 * 1024 * 1024)


def corner_list():
    return [(a, b, c) for a in (0, 1) for b in (0, 1) for c in (0, 1)]


def element_stiffness():
    poisson = 0.3
    lame_first = poisson / ((1.0 + poisson) * (1.0 - 2.0 * poisson))
    shear = 0.5 / (1.0 + poisson)
    elastic = np.zeros((6, 6))
    elastic[:3, :3] = lame_first
    for i in range(3):
        elastic[i, i] += 2.0 * shear
        elastic[i + 3, i + 3] = shear
    points = [0.5 - 0.5 / math.sqrt(3.0), 0.5 + 0.5 / math.sqrt(3.0)]
    gauss = [(u, v, w) for u in points for v in points for w in points]
    stiffness = np.zeros((24, 24))
    for coord in gauss:
        strain = np.zeros((6, 24))
        for k, corner in enumerate(corner_list()):
            values = [coord[d] if corner[d] else 1.0 - coord[d] for d in range(3)]
            slopes = [2.0 * corner[d] - 1.0 for d in range(3)]
            grad_x = slopes[0] * values[1] * values[2]
            grad_y = values[0] * slopes[1] * values[2]
            grad_z = values[0] * values[1] * slopes[2]
            strain[0, 3 * k] = grad_x
            strain[1, 3 * k + 1] = grad_y
            strain[2, 3 * k + 2] = grad_z
            strain[3, 3 * k] = grad_y
            strain[3, 3 * k + 1] = grad_x
            strain[4, 3 * k + 1] = grad_z
            strain[4, 3 * k + 2] = grad_y
            strain[5, 3 * k] = grad_z
            strain[5, 3 * k + 2] = grad_x
        stiffness += strain.T @ elastic @ strain / 8.0
    return stiffness


def mode_table():
    corners = corner_list()
    signs = np.array(
        [[math.prod(2 * c[d] - 1 if m[d] else 1 for d in range(3)) for c in corners] for m in corners],
        float,
    )
    wide = np.kron(signs, np.eye(3))
    table = wide @ element_stiffness() @ wide.T / 64.0
    rows = {}
    for i in range(24):
        row = [
            (corners[j // 3], j % 3, float(table[i, j]))
            for j in range(24)
            if abs(table[i, j]) > 1e-12
        ]
        if row:
            rows[(corners[i // 3], i % 3)] = row
    return rows


MODES = mode_table()
DIAG = float(element_stiffness()[0, 0])
PAIRS = ((0, 0), (1, 0), (0, 1), (1, 1))


def flat_modes(field, z_up, y_up):
    after = z_up(field)
    out = {}
    for k, part in ((0, field + after), (1, after - field)):
        after = y_up(part)
        out[(0, k)] = part + after
        out[(1, k)] = after - part
    return [out[p] for p in PAIRS]


def element_modes(low, high, moduli):
    values = {}
    for c in range(3):
        for q, (j, k) in enumerate(PAIRS):
            if (j, k) != (0, 0):
                values[((0, j, k), c)] = low[c][q] + high[c][q]
            values[((1, j, k), c)] = high[c][q] - low[c][q]
    forces = {}
    for key, row in MODES.items():
        total = None
        for mode, c, weight in row:
            term = weight * values[(mode, c)]
            total = term if total is None else total + term
        forces[key] = total * moduli
    to_low, to_high = [], []
    for c in range(3):
        a, b = [], []
        for j, k in PAIRS:
            slope = forces[((1, j, k), c)]
            mean = forces.get(((0, j, k), c))
            a.append(-slope if mean is None else mean - slope)
            b.append(slope if mean is None else mean + slope)
        to_low.append(a)
        to_high.append(b)
    return to_low, to_high


def node_forces(parts, z_down, y_down):
    out = []
    for k in (0, 1):
        mean, slope = (parts[PAIRS.index((0, k))], parts[PAIRS.index((1, k))])
        out.append((mean - slope) + y_down(mean + slope))
    return (out[0] - out[1]) + z_down(out[0] + out[1])


def shift_up(value, axis):
    return pltpu.roll(value, value.shape[axis] - 1, axis)


def shift_down(value, axis):
    return pltpu.roll(value, 1, axis)


def lanes_of(shape):
    return lax.broadcasted_iota(jnp.int32, shape, len(shape) - 1)


def rows_of(shape):
    return lax.broadcasted_iota(jnp.int32, shape, 0)


def z_shifts(full):
    def up(v):
        s = shift_up(v, 1)
        return jnp.where(lanes_of(v.shape) < v.shape[1] - 1, s, 0.0) if full else s

    def down(v):
        s = shift_down(v, 1)
        return jnp.where(lanes_of(v.shape) > 0, s, 0.0) if full else s

    return up, down


def y_up(v):
    return shift_up(v, 0)


def y_down(v):
    return shift_down(v, 0)


def sweep(load, moduli, first, last, full, emit):
    z_up, z_down = z_shifts(full)

    def modes(x):
        return [flat_modes(load(c, x), z_up, y_up) for c in range(3)]

    high = modes(first + 1)
    _, up = element_modes(modes(first), high, moduli(first))

    def body(x, carry):
        low, before = carry
        high = modes(x + 1)
        own, up = element_modes(low, high, moduli(x))
        forces = [
            node_forces([own[c][q] + before[c][q] for q in range(4)], z_down, y_down)
            for c in range(3)
        ]
        emit(x, forces)
        return (high, up)

    lax.fori_loop(first + 1, last + 1, body, (high, up))


def exact_dot(a, b):
    return jnp.dot(a, b, precision=lax.Precision.HIGHEST, preferred_element_type=F32)


def tent(shape, fine, coarse):
    gap = jnp.abs(fine - 2 * coarse)
    return jnp.where(gap == 0, 1.0, jnp.where(gap == 1, 0.5, 0.0)).astype(F32)


def square(kind, period=128):
    shape = (128, 128)
    fine, coarse = (rows_of(shape), lax.rem(lanes_of(shape), period))
    if kind == "restrict":
        return tent(shape, fine, coarse)
    if kind == "pick":
        return jnp.where(fine == 2 * coarse, 1.0, 0.0).astype(F32)
    return jnp.where((fine == 2 * coarse) | (fine == 2 * coarse + 1), 1.0, 0.0).astype(F32)


def prolong_matrix(period=128):
    shape = (128, 128)
    return tent(shape, lanes_of(shape), lax.rem(rows_of(shape), period))


def smooth_rows(v):
    return v + 0.5 * (y_up(v) + y_down(v))


def corner_sum(v, z_down):
    v = v + z_down(v)
    return v + y_down(v)


def scaled(free, inverse):
    return jnp.where(free > 0.0, inverse, DAMPING)


def first_kernel(
    lo_ref, own_ref, hi_ref,
    m_out, f_out, r_out, s_out, w_out, m1_out, f1_out, c1_out, s1_out, w1_out, pack_out,
    t_ref, b_ref, m_ref, f_ref, r_ref, s_ref, w_ref, u_ref, d_ref, v_ref, m1_ref, u1_ref, d1_ref, v2_ref, m2_ref,
):
    pieces = (lo_ref, own_ref, hi_ref)
    slab = (24, 128)
    z_up, z_down = z_shifts(True)
    gx, gy = (lax.axis_index("gx"), lax.axis_index("gy"))
    nodes_x, nodes_y = (8 * lax.axis_size("gx"), 8 * lax.axis_size("gy"))
    w0, w1, w2, w3 = [2.0 - math.sqrt(n) for n in range(4)]

    def each(first, last, body):
        for p, ref in enumerate(pieces):
            a, b = (max(first, 8 * p), min(last, 8 * p + 7))
            if a <= b:
                lax.fori_loop(a - 8 * p, b - 8 * p + 1, lambda i, _, ref=ref, p=p: body(8 * p + i, ref, i), None)

    def gather_flat(x, ref, i):
        own = ref[0, i]
        ring = z_up(own) + z_down(own)
        c1 = y_up(own) + y_down(own) + ring
        c2 = y_up(ring) + y_down(ring)
        b_ref[x] = w0 * own + w1 * c1 + w2 * c2
        t_ref[x] = w1 * own + w2 * c1 + w3 * c2

    each(0, 23, gather_flat)
    row_at = rows_of(slab) + (8 * gy - 8)
    lane_at = lanes_of(slab)
    inside = ((row_at >= 0) & (row_at < nodes_y)).astype(F32)
    ring_y = (row_at > 0).astype(F32) + (row_at < nodes_y - 1).astype(F32)
    ring_z = (lane_at > 0).astype(F32) + (lane_at < 127).astype(F32)
    plain = w0 + w1 * (ring_y + ring_z) + w2 * ring_y * ring_z
    beside = w1 + w2 * (ring_y + ring_z) + w3 * ring_y * ring_z
    inverse_two, inverse_one = (1.0 / (plain + 2.0 * beside), 1.0 / (plain + beside))

    def moduli_of(x, ref, i):
        at = 8 * gx - 8 + x
        edge = (at == 0) | (at == nodes_x - 1)
        inverse = jnp.where(edge, inverse_one, inverse_two)
        filtered = (b_ref[x] + (t_ref[x - 1] + t_ref[x + 1])) * inverse
        solid, void = (ref[1, i], ref[2, i])
        physical = (1.0 - void) * (solid + (1.0 - solid) * filtered)
        value = VOID_MODULUS + (1.0 - VOID_MODULUS) * (physical * physical * physical)
        mask = jnp.where((at >= 0) & (at < nodes_x), inside, 0.0)
        m_ref[x] = value * mask

    each(1, 22, moduli_of)

    def smooth_of(x, ref, i):
        total = corner_sum(m_ref[x] + m_ref[x - 1], z_down)
        inverse = (DAMPING / DIAG) / total
        for c in range(3):
            free, r = (ref[3 + c, i], ref[6 + c, i])
            w = scaled(free, inverse)
            s = w * r
            f_ref[c, x], r_ref[c, x], w_ref[c, x], s_ref[c, x] = (free, r, w, s)
            u_ref[c, x] = free * s

    each(2, 22, smooth_of)

    def defect_of(x, forces):
        for c in range(3):
            free = f_ref[c, x]
            d_ref[c, x] = r_ref[c, x] - (free * forces[c] + (1.0 - free) * s_ref[c, x])

    sweep(lambda c, x: u_ref[c, x], lambda x: m_ref[x], 2, 21, True, defect_of)

    def keep(x, _):
        m_out[x] = m_ref[x + 6, 4:20, :]
        for c in range(3):
            f_out[c, x] = f_ref[c, x + 6, 4:20, :]
            r_out[c, x] = r_ref[c, x + 6, 4:20, :]
            s_out[c, x] = s_ref[c, x + 6, 4:20, :]
            w_out[c, x] = w_ref[c, x + 6, 4:20, :]

    lax.fori_loop(0, 12, keep, None)

    v_ref[:, 24:32, :] = jnp.zeros((64, 8, 128), F32)

    def to_coarse(n, _):
        x = 2 * n + 4
        for c in range(3):
            v = d_ref[c, x] + 0.5 * (d_ref[c, x - 1] + d_ref[c, x + 1])
            v_ref[9 * c + n, 0:24, :] = smooth_rows(v)
            v_ref[27 + 9 * c + n, 0:24, :] = f_ref[c, x]

    lax.fori_loop(0, 9, to_coarse, None)

    def to_coarse_moduli(n, _):
        x = 2 * n + 2
        v = m_ref[x] + m_ref[x + 1]
        v_ref[54 + n, 0:24, :] = v + y_up(v)

    lax.fori_loop(0, 10, to_coarse_moduli, None)

    def half(first, count, matrix):
        v = v_ref[first : first + count, pl.ds(0, 16, stride=2), :]
        return exact_dot(v.reshape(count * 16, 128), matrix).reshape(count, 16, 128)

    restrict, pick, pair = (square("restrict"), square("pick"), square("pair"))
    m1_ref[...] = 0.25 * half(54, 10, pair)
    m1_out[...] = m1_ref[1:10]
    for c in range(3):
        f1_out[c] = half(27 + 9 * c, 9, pick)
        c1_out[c] = f1_out[c] * half(9 * c, 9, restrict)
    _, plain_down = z_shifts(False)

    def smooth1(n, _):
        inverse = (DAMPING / DIAG) / corner_sum(m1_ref[n + 1] + m1_ref[n], plain_down)
        for c in range(3):
            w = scaled(f1_out[c, n], inverse)
            s = w * c1_out[c, n]
            w1_out[c, n], s1_out[c, n] = (w, s)
            u1_ref[c, n] = f1_out[c, n] * s

    lax.fori_loop(0, 9, smooth1, None)

    def defect1(n, forces):
        for c in range(3):
            free = f1_out[c, n]
            d1_ref[c, n] = c1_out[c, n] - (free * forces[c] + (1.0 - free) * s1_out[c, n])

    sweep(lambda c, n: u1_ref[c, n], lambda n: m1_ref[n + 1], 0, 5, False, defect1)

    for n in range(2):
        x = 2 * n + 2
        for c in range(3):
            v2_ref[2 * c + n] = smooth_rows(d1_ref[c, x] + 0.5 * (d1_ref[c, x - 1] + d1_ref[c, x + 1]))
            v2_ref[6 + 2 * c + n] = f1_out[c, x]
    for n in range(3):
        v = m1_ref[2 * n + 1] + m1_ref[2 * n + 2]
        v2_ref[12 + n] = v + y_up(v)
    v2_ref[15] = jnp.zeros((16, 128), F32)

    def half2(first, count, matrix):
        v = v2_ref[first : first + count, pl.ds(0, 8, stride=2), :]
        return exact_dot(v.reshape(count * 8, 128), matrix).reshape(count, 8, 128)

    free2 = half2(6, 6, pick)
    rhs2 = half2(0, 6, restrict) * free2
    m2_ref[...] = 0.25 * half2(12, 4, pair)
    fields = [[m2_ref[1], m2_ref[2]]]
    fields += [[free2[2 * c], free2[2 * c + 1]] for c in range(3)]
    fields += [[rhs2[2 * c], rhs2[2 * c + 1]] for c in range(3)]
    valid = lanes_of((8, 128)) < 32
    inverse = []
    for n in range(2):
        total = corner_sum(m2_ref[n + 1] + m2_ref[n], plain_down)
        inverse.append(jnp.where(total > 0.0, (DAMPING / DIAG) / total, 0.0))
    fields.append(inverse)
    for f, pairs in enumerate(fields):
        row = None
        for n in range(2):
            v = jnp.where(valid, pairs[n], 0.0)
            for y in range(2):
                piece = v[2 + y : 3 + y]
                q = 2 * n + y
                piece = pltpu.roll(piece, 32 * q, 1) if q else piece
                row = piece if row is None else row + piece
        pack_out[f : f + 1, :] = row


def first_call(lo, own, hi):
    big = lambda *s: jax.ShapeDtypeStruct(s + (16, 128), F32)
    s24 = lambda *s: pltpu.VMEM(s + (24, 128), F32)
    return pl.pallas_call(
        first_kernel,
        out_shape=[big(12), big(3, 12), big(3, 12), big(3, 12), big(3, 12)]
        + [big(9), big(3, 9), big(3, 9), big(3, 9), big(3, 9), jax.ShapeDtypeStruct((8, 128), F32)],
        scratch_shapes=[s24(24), s24(24), s24(24)]
        + [s24(3, 24)] * 6
        + [
            pltpu.VMEM((64, 32, 128), F32),
            pltpu.VMEM((10, 16, 128), F32),
            pltpu.VMEM((3, 9, 16, 128), F32),
            pltpu.VMEM((3, 9, 16, 128), F32),
            pltpu.VMEM((16, 16, 128), F32),
            pltpu.VMEM((4, 8, 128), F32),
        ],
        compiler_params=PARAMS,
    )(lo, own, hi)


def second_kernel(lo_ref, own_ref, hi_ref, hi2_ref, l_out, s_out, w_out, pack_out, u_ref, d_ref, v_ref):
    peers = own_ref.shape[0]
    l_out[...] = jnp.zeros(l_out.shape, F32)
    valid = lanes_of((peers, 128)) < 32
    for ref, base, count in ((lo_ref, 0, 2), (own_ref, 2, 2), (hi_ref, 4, 2), (hi2_ref, 6, 1)):
        for f in range(8):
            rows = ref[:, f, :]
            for n in range(count):
                for y in range(2):
                    q = 2 * n + y
                    v = pltpu.roll(rows, 128 - 32 * q, 1) if q else rows
                    l_out[f, base + n, pl.ds(y, peers, stride=2), :] = jnp.where(valid, v, 0.0)

    def smooth(n, _):
        inverse = l_out[7, n]
        for c in range(3):
            w = scaled(l_out[1 + c, n], inverse)
            s = w * l_out[4 + c, n]
            w_out[c, n], s_out[c, n] = (w, s)
            u_ref[c, n] = l_out[1 + c, n] * s

    lax.fori_loop(0, 7, smooth, None)

    def defect(n, forces):
        for c in range(3):
            free = l_out[1 + c, n]
            d_ref[c, n] = l_out[4 + c, n] - (free * forces[c] + (1.0 - free) * s_out[c, n])

    sweep(lambda c, n: u_ref[c, n], lambda n: l_out[0, n], 0, 3, False, defect)
    for c in range(3):
        v_ref[c] = smooth_rows(d_ref[c, 2] + 0.5 * (d_ref[c, 1] + d_ref[c, 3]))
        v_ref[3 + c] = l_out[1 + c, 2]
    v = l_out[0, 2] + l_out[0, 3]
    v_ref[6] = v + y_up(v)

    def half(first, count, matrix):
        v = v_ref[first : first + count, pl.ds(0, 16, stride=2), :]
        return exact_dot(v.reshape(count * 16, 128), matrix).reshape(count, 16, 128)

    free = half(3, 3, square("pick", 16))
    rhs = half(0, 3, square("restrict", 16)) * free
    moduli = 0.25 * half(6, 1, square("pair", 16))
    shape = (8, 128)
    own_lane = (lanes_of(shape) // 16) == rows_of(shape)
    for f, v in enumerate([moduli[0], free[0], free[1], free[2], rhs[0], rhs[1], rhs[2]]):
        for h in range(2):
            part = jnp.where(own_lane, v[8 * h : 8 * h + 8], 0.0)
            pack_out[f : f + 1, 128 * h : 128 * h + 128] = jnp.sum(part, axis=0, keepdims=True)
    pack_out[7:8, :] = jnp.zeros((1, 256), F32)


def second_call(lo, own, hi, hi2):
    big = lambda *s: jax.ShapeDtypeStruct(s + (32, 128), F32)
    vmem = lambda *s: pltpu.VMEM(s + (32, 128), F32)
    return pl.pallas_call(
        second_kernel,
        out_shape=[big(8, 7), big(3, 7), big(3, 7), jax.ShapeDtypeStruct((8, 256), F32)],
        scratch_shapes=[vmem(3, 7), vmem(3, 7), vmem(7)],
        compiler_params=PARAMS,
    )(lo, own, hi, hi2)


def coarse_solve(rows_ref):
    peers = rows_ref.shape[0]
    shape = (peers + 8, 256)

    def field(f):
        v = rows_ref[:, 256 * f : 256 * f + 256]
        return jnp.concatenate([v, jnp.zeros((8, 256), F32)], axis=0)

    depth = lanes_of(shape) & 15
    z_up = lambda v: jnp.where(depth < 15, shift_up(v, 1), 0.0)
    z_down = lambda v: jnp.where(depth > 0, shift_down(v, 1), 0.0)
    side_up = lambda v: pltpu.roll(v, 240, 1)
    side_down = lambda v: pltpu.roll(v, 16, 1)
    moduli = field(0)
    free = [field(1 + c) for c in range(3)]
    resid = [field(4 + c) for c in range(3)]
    total = moduli + z_down(moduli)
    total = total + side_down(total)
    total = DIAG * (total + shift_down(total, 0))
    inverse = [1.0 / jnp.where(f > 0.0, total, 1.0) for f in free]

    def dot(a, b):
        return jnp.sum(a[0] * b[0] + a[1] * b[1] + a[2] * b[2], keepdims=True)

    def operator(v):
        low = [flat_modes(v[c] * free[c], z_up, side_up) for c in range(3)]
        high = [[shift_up(p, 0) for p in low[c]] for c in range(3)]
        own, up = element_modes(low, high, moduli)
        out = []
        for c in range(3):
            parts = [own[c][q] + shift_down(up[c][q], 0) for q in range(4)]
            forces = node_forces(parts, z_down, side_down)
            out.append(free[c] * forces + (1.0 - free[c]) * v[c])
        return out

    precond = [r * i for r, i in zip(resid, inverse)]
    direction = precond
    inner = dot(resid, precond)
    answer = None
    for step in range(COARSE_ITERS):
        image = operator(direction)
        alpha = inner / dot(direction, image)
        moved = [alpha * d for d in direction]
        answer = moved if answer is None else [s + m for s, m in zip(answer, moved)]
        if step + 1 < COARSE_ITERS:
            resid = [r - alpha * q for r, q in zip(resid, image)]
            precond = [r * i for r, i in zip(resid, inverse)]
            inner_new = dot(resid, precond)
            ratio = inner_new / inner
            direction = [z + ratio * d for z, d in zip(precond, direction)]
            inner = inner_new
    return answer


def third_kernel(
    rows_ref, l2_ref, s2_ref, w2_ref, m1_ref, f1_ref, c1_ref, s1_ref, w1_ref, m_ref, f_ref, r_ref, s_ref, w_ref,
    p_out, q_out, sum_out,
    a_ref, z3_ref, p2_ref, u2_ref, y2_ref, v2_ref, p1_ref, u1_ref, y1_ref, v1_ref, p0_ref, u0_ref, y0_ref,
):
    gx, gy = (lax.axis_index("gx"), lax.axis_index("gy"))
    peers = rows_ref.shape[0]
    answer = coarse_solve(rows_ref)
    for c in range(3):
        a_ref[c, 0:8, :] = jnp.zeros((8, 256), F32)
        a_ref[c, 8 : 16 + peers, :] = answer[c]

    spread3 = prolong_matrix(16)
    shape = (8, 128)
    own_lane = (lanes_of(shape) // 16) == rows_of(shape)
    for c in range(3):
        for i in range(4):
            row = a_ref[c, pl.ds(gx + 7 + i, 1), :]
            halves = [
                jnp.where(own_lane, jnp.broadcast_to(row[:, 128 * h : 128 * h + 128], shape), 0.0)
                for h in range(2)
            ]
            w = exact_dot(jnp.concatenate(halves, axis=0), spread3)
            z3_ref[i, pl.ds(0, 16, stride=2), :] = w
            z3_ref[i, pl.ds(1, 16, stride=2), :] = 0.5 * (w + y_up(w))
        for n in range(7):
            i = n // 2
            p = z3_ref[i] if n % 2 == 0 else 0.5 * (z3_ref[i] + z3_ref[i + 1])
            free = l2_ref[1 + c, n]
            s = s2_ref[c, n] + free * p
            y2_ref[c, n] = s
            u2_ref[c, n] = free * s

    v2_ref[...] = jnp.zeros(v2_ref.shape, F32)

    def level2(n, forces):
        for c in range(3):
            free, s = (l2_ref[1 + c, n], y2_ref[c, n])
            image = free * forces[c] + (1.0 - free) * s
            v2_ref[c, n - 1, 8:40, :] = s + w2_ref[c, n] * (l2_ref[4 + c, n] - image)

    sweep(lambda c, n: u2_ref[c, n], lambda n: l2_ref[0, n], 0, 5, False, level2)

    spread = prolong_matrix()
    for c in range(3):
        for i in range(5):
            w = exact_dot(v2_ref[c, i, pl.ds(2 * gy + 6, 16), :], spread)
            p1_ref[c, i, pl.ds(0, 8, stride=2), :] = w[0:8]
            p1_ref[c, i, pl.ds(1, 8, stride=2), :] = 0.5 * (w[0:8] + w[1:9])
        for n in range(9):
            i = n // 2
            p = p1_ref[c, i] if n % 2 == 0 else 0.5 * (p1_ref[c, i] + p1_ref[c, i + 1])
            free = f1_ref[c, n]
            s = s1_ref[c, n] + free * p
            y1_ref[c, n] = s
            u1_ref[c, n] = free * s

    def level1(n, forces):
        for c in range(3):
            free, s = (f1_ref[c, n], y1_ref[c, n])
            image = free * forces[c] + (1.0 - free) * s
            v1_ref[c, n - 1] = s + w1_ref[c, n] * (c1_ref[c, n] - image)

    sweep(lambda c, n: u1_ref[c, n], lambda n: m1_ref[n], 0, 7, False, level1)

    for c in range(3):
        w = exact_dot(v1_ref[c].reshape(7 * 16, 128), spread).reshape(7, 16, 128)
        for i in range(7):
            p0_ref[c, i, pl.ds(0, 8, stride=2), :] = w[i, 2:10]
            p0_ref[c, i, pl.ds(1, 8, stride=2), :] = 0.5 * (w[i, 2:10] + w[i, 3:11])
        for n in range(12):
            i = n // 2
            p = p0_ref[c, i] if n % 2 == 0 else 0.5 * (p0_ref[c, i] + p0_ref[c, i + 1])
            free = f_ref[c, n]
            s = s_ref[c, n] + free * p
            y0_ref[c, n] = s
            u0_ref[c, n] = free * s

    def level0(n, forces):
        for c in range(3):
            free, s = (f_ref[c, n], y0_ref[c, n])
            image = free * forces[c] + (1.0 - free) * s
            y0_ref[c, n] = s + w_ref[c, n] * (r_ref[c, n] - image)

    sweep(lambda c, n: u0_ref[c, n], lambda n: m_ref[n], 0, 10, True, level0)
    sum_out[...] = jnp.zeros((8, 128), F32)

    def last(n, forces):
        one = two = None
        for c in range(3):
            free, v = (f_ref[c, n], y0_ref[c, n])
            image = (free * forces[c] + (1.0 - free) * v)[4:12]
            v = v[4:12]
            p_out[c, n - 2] = v
            q_out[c, n - 2] = image
            a, b = (r_ref[c, n, 4:12, :] * v, v * image)
            one, two = ((a, b) if one is None else (one + a, two + b))
        sum_out[0:1, :] = sum_out[0:1, :] + jnp.sum(one, axis=0, keepdims=True)
        sum_out[1:2, :] = sum_out[1:2, :] + jnp.sum(two, axis=0, keepdims=True)

    sweep(lambda c, n: f_ref[c, n] * y0_ref[c, n], lambda n: m_ref[n], 1, 9, True, last)
    lane = lanes_of((1, 128))
    one = jnp.sum(sum_out[0:1, :], keepdims=True)
    two = jnp.sum(sum_out[1:2, :], keepdims=True)
    sum_out[0:1, :] = jnp.where(lane == 0, one, jnp.where(lane == 1, two, 0.0))


def third_call(rows, level2, level1, level0):
    own = jax.ShapeDtypeStruct((3, 8, 8, 128), F32)
    peers = rows.shape[0]
    return pl.pallas_call(
        third_kernel,
        out_shape=[own, own, jax.ShapeDtypeStruct((8, 128), F32)],
        scratch_shapes=[
            pltpu.VMEM((3, peers + 16, 256), F32),
            pltpu.VMEM((4, 32, 128), F32),
            pltpu.VMEM((1, 8, 128), F32),
            pltpu.VMEM((3, 7, 32, 128), F32),
            pltpu.VMEM((3, 7, 32, 128), F32),
            pltpu.VMEM((3, 5, 48, 128), F32),
            pltpu.VMEM((3, 5, 16, 128), F32),
            pltpu.VMEM((3, 9, 16, 128), F32),
            pltpu.VMEM((3, 9, 16, 128), F32),
            pltpu.VMEM((3, 7, 16, 128), F32),
            pltpu.VMEM((3, 7, 16, 128), F32),
            pltpu.VMEM((3, 12, 16, 128), F32),
            pltpu.VMEM((3, 12, 16, 128), F32),
        ],
        compiler_params=PARAMS,
    )(rows, *level2, *level1, *level0)


def from_peer(value, axis, step):
    peers = lax.axis_size(axis)
    return lax.ppermute(value, axis, [(i + step, i) for i in range(peers) if 0 <= i + step < peers])


def spread_all(row, axis):
    peers = lax.axis_size(axis)
    return lax.all_to_all(
        jnp.broadcast_to(row[None], (peers,) + row.shape), axis, 0, 0, tiled=True
    )


def on_device(density, solid, void, fixed, residual):
    packed = jnp.concatenate(
        [
            density[None],
            solid.astype(F32)[None],
            void.astype(F32)[None],
            1.0 - fixed.astype(F32),
            residual,
        ],
        axis=0,
    )
    own = jnp.concatenate([from_peer(packed, "gy", -1), packed, from_peer(packed, "gy", 1)], axis=2)
    first = first_call(from_peer(own, "gx", -1), own, from_peer(own, "gx", 1))
    level0, level1, piece = (first[0:5], first[5:10], first[10])
    columns = spread_all(piece, "gy")
    second = second_call(
        from_peer(columns, "gx", -1), columns, from_peer(columns, "gx", 1), from_peer(columns, "gx", 2)
    )
    rows = spread_all(second[3].reshape(-1), "gx")
    precond, image, sums = third_call(rows, second[0:3], level1, level0)
    sums = jnp.sum(spread_all(sums[0], "gx"), axis=0)
    sums = jnp.sum(spread_all(sums, "gy"), axis=0)
    alpha = sums[0] / sums[1]
    return (alpha * precond, residual - alpha * image)


def solution(mesh):
    return jax.shard_map(
        on_device,
        mesh=mesh,
        in_specs=(
            P("gx", "gy", None),
            P("gx", "gy", None),
            P("gx", "gy", None),
            P(None, "gx", "gy", None),
            P(None, "gx", "gy", None),
        ),
        out_specs=(P(None, "gx", "gy", None), P(None, "gx", "gy", None)),
        check_vma=False,
    )
```

time: 709 us -> 161 us (0.23); the launches traced: 696 us -> 160 us
  local copies, waits for them, and re-layouts: 240 us -> 2.75 us
  starting transfers between devices: 240 us -> 30.4 us
  other arithmetic: 37.9 us -> 1.59 us
  blocking collectives: 115 us -> 80.7 us
  Pallas kernels: 0 us -> 27.8 us
  matrix products: 18.5 us -> 0 us
  waiting for transfers between devices: 31.1 us -> 14.7 us
  between operations: 14.1 us -> 2.14 us
    ppermute x68 -> x7, starting transfers between devices: 221 us -> 30.4 us  [from_peer(): lax.ppermute(value, axis, [(i + step, i) for i in range(peers) if 0 <= i...]
    reshape x32 -> x0, local copies, waits for them, and re-layouts: 153 us -> none  [the longest x15 100 us: element_forces(): jnp.dot(stiffness, stacked.reshape(24, -1), precision=lax.Precision.HIGHEST)]
    concatenate x15 -> x1, local copies, waits for them, and re-layouts: 42.8 us -> 0.01 us  [on_device(): jnp.concatenate([density[None], solid.astype(F32)[None], void.astype(F32)...]
    all_to_all x3 -> x4, blocking collectives: 115 us -> 80.7 us  [spread_all(): lax.all_to_all(jnp.broadcast_to(row[None], (peers,) + row.shape), axis, 0...]
    pallas_call x0 -> x3, Pallas kernels: none -> 27.8 us  [the longest x1 13.9 us: third_call(): pl.pallas_call(third_kernel, out_shape=[own, own, jax.ShapeDtypeStruct((8...]
    unnamed x164 -> x9, local copies, waits for them, and re-layouts: 28.7 us -> 1.85 us
    dot_general x11 -> x0, matrix products: 18.5 us -> none  [element_forces(): jnp.dot(stiffness, stacked.reshape(24, -1), precision=lax.Precision.HIGHEST)]
    all_to_all x1 -> x0, starting transfers between devices: 18.4 us -> none  [spread(): lax.all_to_all(jnp.broadcast_to(row[None], (peers,) + row.shape), axis, 0...]
  transfers between devices with their start and end apart: 69 -> 7, of which waited for: 22 -> 5; matrix products, arithmetic and copies ran while one was open for 4% -> 0% of each run, Pallas kernels for 0% -> 0%
where the time goes in v2:
time: 161 us; the launch traced here: 160 us
  blocking collectives  80.7 us (50%)
  starting transfers between devices  30.4 us (19%)
  Pallas kernels  27.8 us (17%)
  waiting for transfers between devices  14.7 us (9%)
  local copies, waits for them, and re-layouts  2.75 us (2%)
  between operations  2.14 us (1%)
    all_to_all x4, blocking collectives, spread_all(): lax.all_to_all(jnp.broadcast_to(row[None], (peers,) + row.shape), axis, 0...  80.7 us
    ppermute x7, starting transfers between devices, from_peer(): lax.ppermute(value, axis, [(i + step, i) for i in range(peers) if 0 <= i...  30.4 us
    ppermute x7, waiting for transfers between devices, from_peer(): lax.ppermute(value, axis, [(i + step, i) for i in range(peers) if 0 <= i...  14.7 us
    pallas_call x1, Pallas kernels, third_call(): pl.pallas_call(third_kernel, out_shape=[own, own, jax.ShapeDtypeStruct((8...  13.9 us
    pallas_call x1, Pallas kernels, first_call(): pl.pallas_call(first_kernel, out_shape=[big(12), big(3, 12), big(3, 12),...  12.2 us
  transfers between devices with their start and end apart: 7, of which 5 were waited for; matrix products, arithmetic and copies ran while one was open for 0% of the time, Pallas kernels for 0%

profile of v2, /device:TPU:1, one launch (start us, length us, event | category | flops | bytes accessed | tf_op | source)
XLA Modules:
  0.0 160.1 jit_solution(12179343628795626134)
XLA Ops:
  0.6 0.0 copy-start.2
  0.6 0.0 copy-start.1
  0.6 0.8 bitcast_dynamic-update-slice_fusion.2
  1.4 0.0 copy-done.2
  1.5 0.8 bitcast_dynamic-update-slice_fusion
  2.2 0.0 copy-done.1
  2.2 0.0 copy-start
  2.2 0.9 copy-done
  3.1 1.3 collective-permute-start.1
  4.4 5.5 %collective-permute-start = (f32[9,8,8,128]{3,2,1,0:T(8,128)S(1)}, f32[9,8,8,128]{3,2,1,0:T(8,128)S(1)}, u32[]{:S(2)}, u32[]{:S(2)}) collective-permute-start(f32[9,8,8,128]{3,2,1,0:T(8,128)S(1)} %constant_dynamic-update-slice_fusion), channel_id=1, source_target_pairs={{0,1},{1,2},{2,3},{3,4},{4,5},{5,6},{6,7},{7,8},{8,9},{9,10},{10,1... | collective-permute-start | bytes 884744 | tf_op jit(solution)/shard_map/ppermute | solution.py:655
  9.9 2.2 %collective-permute-done.1 = f32[9,8,8,128]{3,2,1,0:T(8,128)S(1)} collective-permute-done((f32[9,8,8,128]{3,2,1,0:T(8,128)S(1)}, f32[9,8,8,128]{3,2,1,0:T(8,128)S(1)}, u32[]{:S(2)}, u32[]{:S(2)}) %collective-permute-start.1) | collective-permute-done | bytes 294944 | tf_op jit(solution)/shard_map/ppermute | solution.py:655
  12.1 1.5 collective-permute-done
  13.5 0.1 pad_maximum_fusion.own_ref
  13.6 12.1 %collective-permute-start.3 = (f32[9,8,24,128]{3,2,1,0:T(8,128)S(1)}, f32[9,8,24,128]{3,2,1,0:T(8,128)S(1)}, u32[]{:S(2)}, u32[]{:S(2)}) collective-permute-start(f32[9,8,24,128]{3,2,1,0:T(8,128)S(1)} %pad_maximum_fusion.own_ref), channel_id=1, source_target_pairs={{12,0},{24,12},{36,24},{48,36},{60,48},{72,60},{84,72},{96,84},{10... | collective-permute-start | bytes 2654216 | tf_op jit(solution)/shard_map/ppermute | solution.py:655
  25.7 1.9 %collective-permute-start.2 = (f32[9,8,24,128]{3,2,1,0:T(8,128)S(1)}, f32[9,8,24,128]{3,2,1,0:T(8,128)S(1)}, u32[]{:S(2)}, u32[]{:S(2)}) collective-permute-start(f32[9,8,24,128]{3,2,1,0:T(8,128)S(1)} %pad_maximum_fusion.own_ref), channel_id=1, source_target_pairs={{0,12},{12,24},{24,36},{36,48},{48,60},{60,72},{72,84},{84,96},{96... | collective-permute-start | bytes 2654216 | tf_op jit(solution)/shard_map/ppermute | solution.py:655
  27.6 3.3 %collective-permute-done.3.hi_ref = f32[9,8,24,128]{3,2,1,0:T(8,128)S(1)} collective-permute-done((f32[9,8,24,128]{3,2,1,0:T(8,128)S(1)}, f32[9,8,24,128]{3,2,1,0:T(8,128)S(1)}, u32[]{:S(2)}, u32[]{:S(2)}) %collective-permute-start.3) | collective-permute-done | bytes 884768 | tf_op jit(solution)/shard_map/ppermute | solution.py:655
  30.9 6.7 %collective-permute-done.2.lo_ref = f32[9,8,24,128]{3,2,1,0:T(8,128)S(1)} collective-permute-done((f32[9,8,24,128]{3,2,1,0:T(8,128)S(1)}, f32[9,8,24,128]{3,2,1,0:T(8,128)S(1)}, u32[]{:S(2)}, u32[]{:S(2)}) %collective-permute-start.2) | collective-permute-done | bytes 884768 | tf_op jit(solution)/shard_map/ppermute | solution.py:655
  37.6 12.2 %shard_map.68 = (f32[12,16,128]{2,1,0:T(8,128)S(1)}, f32[3,12,16,128]{3,2,1,0:T(8,128)S(1)}, f32[3,12,16,128]{3,2,1,0:T(8,128)S(1)}, f32[3,12,16,128]{3,2,1,0:T(...) custom-call(f32[9,8,24,128]{3,2,1,0:T(8,128)S(1)} %collective-permut, ...), custom_call_target="tpu_custom_call" | custom-call | tf_op jit(solution)/shard_map/pallas_call | solution.py:387
  49.9 20.4 %all_to_all.25.own_ref = f32[12,8,128]{2,1,0:T(8,128)S(1)} all-to-all(f32[12,8,128]{2,1,0:T(8,128)S(1)} %broadcast_in_dim.36), channel_id=1, replica_groups=mesh['gx'=64,'gy'=12] {'gy'}, dimensions={0} | all-to-all | bytes 98304 | tf_op jit(solution)/shard_map/all_to_all | solution.py:660
  70.3 1.3 collective-permute-start.6
  71.6 1.9 %collective-permute-start.5 = (f32[12,8,128]{2,1,0:T(8,128)S(1)}, f32[12,8,128]{2,1,0:T(8,128)S(1)}, u32[]{:S(2)}, u32[]{:S(2)}) collective-permute-start(f32[12,8,128]{2,1,0:T(8,128)S(1)} %all_to_all.25.own_ref), channel_id=1, source_target_pairs={{12,0},{24,12},{36,24},{48,36},{60,48},{72,60},{84,72},{96,84},{10... | collective-permute-start | bytes 147464 | tf_op jit(solution)/shard_map/ppermute | solution.py:655
  73.5 6.4 %collective-permute-start.4 = (f32[12,8,128]{2,1,0:T(8,128)S(1)}, f32[12,8,128]{2,1,0:T(8,128)S(1)}, u32[]{:S(2)}, u32[]{:S(2)}) collective-permute-start(f32[12,8,128]{2,1,0:T(8,128)S(1)} %all_to_all.25.own_ref), channel_id=1, source_target_pairs={{0,12},{12,24},{24,36},{36,48},{48,60},{60,72},{72,84},{84,96},{96... | collective-permute-start | bytes 147464 | tf_op jit(solution)/shard_map/ppermute | solution.py:655
  80.0 0.0 collective-permute-done.6.hi2_ref
  80.0 0.0 collective-permute-done.5.hi_ref
  80.0 1.1 collective-permute-done.4.lo_ref
  81.1 1.7 %shard_map.69 = (f32[8,7,32,128]{3,2,1,0:T(8,128)S(1)}, f32[3,7,32,128]{3,2,1,0:T(8,128)S(1)}, f32[3,7,32,128]{3,2,1,0:T(8,128)S(1)}, f32[8,256]{1,0:T(8,128)S(1)}) custom-call(f32[12,8,128]{2,1,0:T(8,128)S(1)} %collective-permute-done.4.lo_ref, f32[12,8,128]{2,1,0:T(8,128)S(1)} %all_to_all.25.own_ref, f32[12,8,128]{2,1,0:T(8,128)S(1)} %collective-permute-done.5.hi_ref, ...), custom_call_target="tpu_custom_call" | custom-call | tf_op jit(solution)/shard_map/pallas_call | solution.py:459
  82.9 0.3 broadcast_in_dim.38
  83.1 33.9 %all_to_all.26 = f32[64,1,2048]{2,1,0:T(1,128)S(1)} all-to-all(f32[64,1,2048]{2,1,0:T(1,128)S(1)} %broadcast_in_dim.38), channel_id=1, replica_groups=mesh['gx'=64,'gy'=12] {'gx'}, dimensions={0} | all-to-all | bytes 1048576 | tf_op jit(solution)/shard_map/all_to_all | solution.py:660
  117.1 0.2 copy.11
  117.2 13.9 %shard_map.70 = (f32[3,8,8,128]{3,2,1,0:T(8,128)S(1)}, f32[3,8,8,128]{3,2,1,0:T(8,128)S(1)}, f32[8,128]{1,0:T(8,128)S(1)}) custom-call(f32[64,2048]{1,0:T(8,128)S(1)} %bitcast.15, f32[8,7,32,128]{3,2,1,0:T(8,128)S(1)} %get-tuple-element.22.l2_ref, f32[3,7,32,128]{3,2,1,0:T(8,128)S(1)} %get-tuple-element.23.s2_ref, ...), custom_call_target="tpu_custom_call" | custom-call | tf_op jit(solution)/shard_map/pallas_call | solution.py:631
  131.1 14.9 %all_to_all.27 = f32[64,1,128]{2,1,0:T(1,128)S(1)} all-to-all(f32[64,1,128]{2,1,0:T(1,128)S(1)} %broadcast_in_dim.39), channel_id=1, replica_groups=mesh['gx'=64,'gy'=12] {'gx'}, dimensions={0} | all-to-all | bytes 65536 | tf_op jit(solution)/shard_map/all_to_all | solution.py:660
  146.1 11.4 %all_to_all.28 = f32[12,1,128]{2,1,0:T(1,128)S(1)} all-to-all(f32[12,1,128]{2,1,0:T(1,128)S(1)} %broadcast_in_dim.40), channel_id=1, replica_groups=mesh['gx'=64,'gy'=12] {'gy'}, dimensions={0} | all-to-all | bytes 12288 | tf_op jit(solution)/shard_map/all_to_all | solution.py:660
  157.5 0.6 fusion
  159.4 0.7 multiply_subtract_fusion
  (10 shorter events, 0.1 us)
Async XLA Ops:
  0.6 0.8 copy-start.2
  0.6 1.6 copy-start.1
  2.2 0.9 copy-start
  3.1 8.9 %collective-permute-start.1 = (f32[9,8,8,128]{3,2,1,0:T(8,128)S(1)}, f32[9,8,8,128]{3,2,1,0:T(8,128)S(1)}, u32[]{:S(2)}, u32[]{:S(2)}) collective-permute-start(f32[9,8,8,128]{3,2,1,0:T(8,128)S(1)} %constant_dynamic-update-slice_fusion), channel_id=1, source_target_pairs={{1,0},{2,1},{3,2},{4,3},{5,4},{6,5},{7,6},{8,7},{9,8},{10,9},{11,1... | collective-permute-start | bytes 884744 | tf_op jit(solution)/shard_map/ppermute | solution.py:655
  4.4 9.1 %collective-permute-start = (f32[9,8,8,128]{3,2,1,0:T(8,128)S(1)}, f32[9,8,8,128]{3,2,1,0:T(8,128)S(1)}, u32[]{:S(2)}, u32[]{:S(2)}) collective-permute-start(f32[9,8,8,128]{3,2,1,0:T(8,128)S(1)} %constant_dynamic-update-slice_fusion), channel_id=1, source_target_pairs={{0,1},{1,2},{2,3},{3,4},{4,5},{5,6},{6,7},{7,8},{8,9},{9,10},{10,1... | collective-permute-start | bytes 884744 | tf_op jit(solution)/shard_map/ppermute | solution.py:655
  13.6 17.3 %collective-permute-start.3 = (f32[9,8,24,128]{3,2,1,0:T(8,128)S(1)}, f32[9,8,24,128]{3,2,1,0:T(8,128)S(1)}, u32[]{:S(2)}, u32[]{:S(2)}) collective-permute-start(f32[9,8,24,128]{3,2,1,0:T(8,128)S(1)} %pad_maximum_fusion.own_ref), channel_id=1, source_target_pairs={{12,0},{24,12},{36,24},{48,36},{60,48},{72,60},{84,72},{96,84},{10... | collective-permute-start | bytes 2654216 | tf_op jit(solution)/shard_map/ppermute | solution.py:655
  25.7 11.9 %collective-permute-start.2 = (f32[9,8,24,128]{3,2,1,0:T(8,128)S(1)}, f32[9,8,24,128]{3,2,1,0:T(8,128)S(1)}, u32[]{:S(2)}, u32[]{:S(2)}) collective-permute-start(f32[9,8,24,128]{3,2,1,0:T(8,128)S(1)} %pad_maximum_fusion.own_ref), channel_id=1, source_target_pairs={{0,12},{12,24},{24,36},{36,48},{48,60},{60,72},{72,84},{84,96},{96... | collective-permute-start | bytes 2654216 | tf_op jit(solution)/shard_map/ppermute | solution.py:655
  70.3 9.7 %collective-permute-start.6 = (f32[12,8,128]{2,1,0:T(8,128)S(1)}, f32[12,8,128]{2,1,0:T(8,128)S(1)}, u32[]{:S(2)}, u32[]{:S(2)}) collective-permute-start(f32[12,8,128]{2,1,0:T(8,128)S(1)} %all_to_all.25.own_ref), channel_id=1, source_target_pairs={{24,0},{36,12},{48,24},{60,36},{72,48},{84,60},{96,72},{108,84},{1... | collective-permute-start | bytes 147464 | tf_op jit(solution)/shard_map/ppermute | solution.py:655
  71.6 8.4 %collective-permute-start.5 = (f32[12,8,128]{2,1,0:T(8,128)S(1)}, f32[12,8,128]{2,1,0:T(8,128)S(1)}, u32[]{:S(2)}, u32[]{:S(2)}) collective-permute-start(f32[12,8,128]{2,1,0:T(8,128)S(1)} %all_to_all.25.own_ref), channel_id=1, source_target_pairs={{12,0},{24,12},{36,24},{48,36},{60,48},{72,60},{84,72},{96,84},{10... | collective-permute-start | bytes 147464 | tf_op jit(solution)/shard_map/ppermute | solution.py:655
  73.5 7.6 %collective-permute-start.4 = (f32[12,8,128]{2,1,0:T(8,128)S(1)}, f32[12,8,128]{2,1,0:T(8,128)S(1)}, u32[]{:S(2)}, u32[]{:S(2)}) collective-permute-start(f32[12,8,128]{2,1,0:T(8,128)S(1)} %all_to_all.25.own_ref), channel_id=1, source_target_pairs={{0,12},{12,24},{24,36},{36,48},{48,60},{60,72},{72,84},{84,96},{96... | collective-permute-start | bytes 147464 | tf_op jit(solution)/shard_map/ppermute | solution.py:655

commit v3 on v2

--- a/solution.py
+++ b/solution.py
@@ -158,7 +158,7 @@
     return shift_down(v, 0)
 
 
-def sweep(load, moduli, first, last, full, emit):
+def sweep(load, moduli, first, last, full, emit, unroll=True):
     z_up, z_down = z_shifts(full)
 
     def modes(x):
@@ -178,7 +178,7 @@
         emit(x, forces)
         return (high, up)
 
-    lax.fori_loop(first + 1, last + 1, body, (high, up))
+    lax.fori_loop(first + 1, last + 1, body, (high, up), unroll=unroll)
 
 
 def exact_dot(a, b):
@@ -234,7 +234,7 @@
         for p, ref in enumerate(pieces):
             a, b = (max(first, 8 * p), min(last, 8 * p + 7))
             if a <= b:
-                lax.fori_loop(a - 8 * p, b - 8 * p + 1, lambda i, _, ref=ref, p=p: body(8 * p + i, ref, i), None)
+                lax.fori_loop(a - 8 * p, b - 8 * p + 1, lambda i, _, ref=ref, p=p: body(8 * p + i, ref, i), None, unroll=True)
 
     def gather_flat(x, ref, i):
         own = ref[0, i]
@@ -294,7 +294,7 @@
             s_out[c, x] = s_ref[c, x + 6, 4:20, :]
             w_out[c, x] = w_ref[c, x + 6, 4:20, :]
 
-    lax.fori_loop(0, 12, keep, None)
+    lax.fori_loop(0, 12, keep, None, unroll=2)
 
     v_ref[:, 24:32, :] = jnp.zeros((64, 8, 128), F32)
 
@@ -305,14 +305,14 @@
             v_ref[9 * c + n, 0:24, :] = smooth_rows(v)
             v_ref[27 + 9 * c + n, 0:24, :] = f_ref[c, x]
 
-    lax.fori_loop(0, 9, to_coarse, None)
+    lax.fori_loop(0, 9, to_coarse, None, unroll=3)
 
     def to_coarse_moduli(n, _):
         x = 2 * n + 2
         v = m_ref[x] + m_ref[x + 1]
         v_ref[54 + n, 0:24, :] = v + y_up(v)
 
-    lax.fori_loop(0, 10, to_coarse_moduli, None)
+    lax.fori_loop(0, 10, to_coarse_moduli, None, unroll=5)
 
     def half(first, count, matrix):
         v = v_ref[first : first + count, pl.ds(0, 16, stride=2), :]
@@ -334,7 +334,7 @@
             w1_out[c, n], s1_out[c, n] = (w, s)
             u1_ref[c, n] = f1_out[c, n] * s
 
-    lax.fori_loop(0, 9, smooth1, None)
+    lax.fori_loop(0, 9, smooth1, None, unroll=True)
 
     def defect1(n, forces):
         for c in range(3):
@@ -423,7 +423,7 @@
             w_out[c, n], s_out[c, n] = (w, s)
             u_ref[c, n] = l_out[1 + c, n] * s
 
-    lax.fori_loop(0, 7, smooth, None)
+    lax.fori_loop(0, 7, smooth, None, unroll=True)
 
     def defect(n, forces):
         for c in range(3):
@@ -446,11 +446,16 @@
     moduli = 0.25 * half(6, 1, square("pair", 16))
     shape = (8, 128)
     own_lane = (lanes_of(shape) // 16) == rows_of(shape)
-    for f, v in enumerate([moduli[0], free[0], free[1], free[2], rhs[0], rhs[1], rhs[2]]):
-        for h in range(2):
-            part = jnp.where(own_lane, v[8 * h : 8 * h + 8], 0.0)
-            pack_out[f : f + 1, 128 * h : 128 * h + 128] = jnp.sum(part, axis=0, keepdims=True)
-    pack_out[7:8, :] = jnp.zeros((1, 256), F32)
+    fields = []
+    for v in (moduli[0], free[0], free[1], free[2], rhs[0], rhs[1], rhs[2]):
+        fields.append(
+            [
+                jnp.sum(jnp.where(own_lane, v[8 * h : 8 * h + 8], 0.0), axis=0, keepdims=True)
+                for h in range(2)
+            ]
+        )
+    for t, v in enumerate(pack_rows(fields)):
+        pack_out[:, 128 * t : 128 * t + 128] = v
 
 
 def second_call(lo, own, hi, hi2):
@@ -458,18 +463,43 @@
     vmem = lambda *s: pltpu.VMEM(s + (32, 128), F32)
     return pl.pallas_call(
         second_kernel,
-        out_shape=[big(8, 7), big(3, 7), big(3, 7), jax.ShapeDtypeStruct((8, 256), F32)],
+        out_shape=[big(8, 7), big(3, 7), big(3, 7), jax.ShapeDtypeStruct((1, 1408), F32)],
         scratch_shapes=[vmem(3, 7), vmem(3, 7), vmem(7)],
         compiler_params=PARAMS,
     )(lo, own, hi, hi2)
 
 
+def pack_rows(fields):
+    out = []
+    low = lanes_of(fields[0][0].shape) < 64
+    turn = lambda v: pltpu.roll(v, 64, 1)
+    for k in range(0, 6, 2):
+        (a0, a1), (b0, b1) = (fields[k], fields[k + 1])
+        middle = turn(b0)
+        out += [a0, jnp.where(low, a1, middle), jnp.where(low, middle, turn(b1))]
+    return out + fields[6]
+
+
+def unpack_rows(tiles):
+    out = []
+    low = lanes_of(tiles[0].shape) < 64
+    turn = lambda v: pltpu.roll(v, 64, 1)
+    for k in range(0, 9, 3):
+        t0, t1, t2 = tiles[k : k + 3]
+        r1, r2 = (turn(t1), turn(t2))
+        out.append([t0, jnp.where(low, t1, 0.0)])
+        out.append([jnp.where(low, r1, r2), jnp.where(low, r2, 0.0)])
+    return out + [tiles[9:11]]
+
+
 def coarse_solve(rows_ref):
     peers = rows_ref.shape[0]
     shape = (peers + 8, 256)
 
+    fields = unpack_rows([rows_ref[:, 128 * t : 128 * t + 128] for t in range(11)])
+
     def field(f):
-        v = rows_ref[:, 256 * f : 256 * f + 256]
+        v = jnp.concatenate(fields[f], axis=1)
         return jnp.concatenate([v, jnp.zeros((8, 256), F32)], axis=0)
 
     depth = lanes_of(shape) & 15
@@ -650,6 +680,22 @@
     )(rows, *level2, *level1, *level0)
 
 
+def pack_kernel(density_ref, solid_ref, void_ref, fixed_ref, residual_ref, out_ref):
+    out_ref[0] = density_ref[...]
+    out_ref[1] = solid_ref[...].astype(F32)
+    out_ref[2] = void_ref[...].astype(F32)
+    out_ref[3:6] = 1.0 - fixed_ref[...].astype(F32)
+    out_ref[6:9] = residual_ref[...]
+
+
+def last_kernel(sums_ref, precond_ref, image_ref, residual_ref, update_ref, next_ref):
+    total = jnp.sum(sums_ref[...], axis=0, keepdims=True)
+    alpha = total[:, 0:1] / total[:, 1:2]
+    for c in range(3):
+        update_ref[c] = alpha * precond_ref[c]
+        next_ref[c] = residual_ref[c] - alpha * image_ref[c]
+
+
 def from_peer(value, axis, step):
     peers = lax.axis_size(axis)
     return lax.ppermute(value, axis, [(i + step, i) for i in range(peers) if 0 <= i + step < peers])
@@ -663,16 +709,11 @@
 
 
 def on_device(density, solid, void, fixed, residual):
-    packed = jnp.concatenate(
-        [
-            density[None],
-            solid.astype(F32)[None],
-            void.astype(F32)[None],
-            1.0 - fixed.astype(F32),
-            residual,
-        ],
-        axis=0,
-    )
+    packed = pl.pallas_call(
+        pack_kernel,
+        out_shape=jax.ShapeDtypeStruct((9,) + density.shape, F32),
+        compiler_params=PARAMS,
+    )(density, solid, void, fixed, residual)
     own = jnp.concatenate([from_peer(packed, "gy", -1), packed, from_peer(packed, "gy", 1)], axis=2)
     first = first_call(from_peer(own, "gx", -1), own, from_peer(own, "gx", 1))
     level0, level1, piece = (first[0:5], first[5:10], first[10])
@@ -683,9 +724,12 @@
     rows = spread_all(second[3].reshape(-1), "gx")
     precond, image, sums = third_call(rows, second[0:3], level1, level0)
     sums = jnp.sum(spread_all(sums[0], "gx"), axis=0)
-    sums = jnp.sum(spread_all(sums, "gy"), axis=0)
-    alpha = sums[0] / sums[1]
-    return (alpha * precond, residual - alpha * image)
+    block = jax.ShapeDtypeStruct(residual.shape, F32)
+    return tuple(
+        pl.pallas_call(last_kernel, out_shape=[block, block], compiler_params=PARAMS)(
+            spread_all(sums, "gy"), precond, image, residual
+        )
+    )
 
 
 def solution(mesh):

time: 161 us -> 148 us (0.919)
  Pallas kernels: 27.8 us -> 16 us
  local copies, waits for them, and re-layouts: 2.75 us -> 8.18 us
  blocking collectives: 80.7 us -> 77.3 us
    pallas_call x1, Pallas kernels: 12.2 us -> 4.9 us  [first_call(): pl.pallas_call(first_kernel, out_shape=[big(12), big(3, 12), big(3, 12),...]
    unnamed x9 -> x30, local copies, waits for them, and re-layouts: 1.85 us -> 7.96 us
    pallas_call x1, Pallas kernels: 13.9 us -> 9.11 us  [third_call(): pl.pallas_call(third_kernel, out_shape=[own, own, jax.ShapeDtypeStruct((8...]
    all_to_all x4, blocking collectives: 80.7 us -> 77.3 us  [spread_all(): lax.all_to_all(jnp.broadcast_to(row[None], (peers,) + row.shape), axis, 0...]
where the time goes in v3:
time: 148 us
  blocking collectives  77.3 us (52%)
  starting transfers between devices  30.4 us (21%)
  Pallas kernels  16 us (11%)
  waiting for transfers between devices  14.7 us (10%)
  local copies, waits for them, and re-layouts  8.18 us (6%)
    all_to_all x4, blocking collectives, spread_all(): lax.all_to_all(jnp.broadcast_to(row[None], (peers,) + row.shape), axis, 0...  77.3 us
    ppermute x7, starting transfers between devices, from_peer(): lax.ppermute(value, axis, [(i + step, i) for i in range(peers) if 0 <= i...  30.4 us
    ppermute x7, waiting for transfers between devices, from_peer(): lax.ppermute(value, axis, [(i + step, i) for i in range(peers) if 0 <= i...  14.7 us
    pallas_call x1, Pallas kernels, third_call(): pl.pallas_call(third_kernel, out_shape=[own, own, jax.ShapeDtypeStruct((8...  9.11 us
    unnamed x30, local copies, waits for them, and re-layouts  7.96 us
    pallas_call x1, Pallas kernels, first_call(): pl.pallas_call(first_kernel, out_shape=[big(12), big(3, 12), big(3, 12),...  4.9 us
  transfers between devices with their start and end apart: 7, of which 5 were waited for; matrix products, arithmetic and copies ran while one was open for 0% of the time, Pallas kernels for 0%

profile of v3, /device:TPU:1, one launch (start us, length us, event | category | flops | bytes accessed | tf_op | source)
XLA Modules:
  0.0 147.5 jit_solution(10840601313707281804)
XLA Ops:
  0.6 0.0 copy-start
  0.6 0.9 copy-done
  1.5 0.0 copy-start.4
  1.5 0.9 copy-done.4
  2.4 0.0 copy-start.11
  2.4 0.8 copy-done.11
  3.2 0.0 copy-start.12
  3.2 0.8 copy-done.12
  3.9 0.0 copy-start.13
  3.9 0.8 copy-done.13
  4.7 1.3 collective-permute-start.1
  6.0 5.5 %collective-permute-start = (f32[9,8,8,128]{3,2,1,0:T(8,128)S(1)}, f32[9,8,8,128]{3,2,1,0:T(8,128)S(1)}, u32[]{:S(2)}, u32[]{:S(2)}) collective-permute-start(f32[9,8,8,128]{3,2,1,0:T(8,128)S(1)} %shard_map.68), channel_id=1, source_target_pairs={{0,1},{1,2},{2,3},{3,4},{4,5},{5,6},{6,7},{7,8},{8,9},{9,10},{10,1... | collective-permute-start | bytes 884744 | tf_op jit(solution)/shard_map/ppermute | solution.py:701
  11.5 2.2 %collective-permute-done.1 = f32[9,8,8,128]{3,2,1,0:T(8,128)S(1)} collective-permute-done((f32[9,8,8,128]{3,2,1,0:T(8,128)S(1)}, f32[9,8,8,128]{3,2,1,0:T(8,128)S(1)}, u32[]{:S(2)}, u32[]{:S(2)}) %collective-permute-start.1) | collective-permute-done | bytes 294944 | tf_op jit(solution)/shard_map/ppermute | solution.py:701
  13.7 1.5 %collective-permute-done = f32[9,8,8,128]{3,2,1,0:T(8,128)S(1)} collective-permute-done((f32[9,8,8,128]{3,2,1,0:T(8,128)S(1)}, f32[9,8,8,128]{3,2,1,0:T(8,128)S(1)}, u32[]{:S(2)}, u32[]{:S(2)}) %collective-permute-start) | collective-permute-done | bytes 294944 | tf_op jit(solution)/shard_map/ppermute | solution.py:701
  15.1 0.1 pad_maximum_fusion.own_ref
  15.2 12.1 %collective-permute-start.3 = (f32[9,8,24,128]{3,2,1,0:T(8,128)S(1)}, f32[9,8,24,128]{3,2,1,0:T(8,128)S(1)}, u32[]{:S(2)}, u32[]{:S(2)}) collective-permute-start(f32[9,8,24,128]{3,2,1,0:T(8,128)S(1)} %pad_maximum_fusion.own_ref), channel_id=1, source_target_pairs={{12,0},{24,12},{36,24},{48,36},{60,48},{72,60},{84,72},{96,84},{10... | collective-permute-start | bytes 2654216 | tf_op jit(solution)/shard_map/ppermute | solution.py:701
  27.3 1.9 %collective-permute-start.2 = (f32[9,8,24,128]{3,2,1,0:T(8,128)S(1)}, f32[9,8,24,128]{3,2,1,0:T(8,128)S(1)}, u32[]{:S(2)}, u32[]{:S(2)}) collective-permute-start(f32[9,8,24,128]{3,2,1,0:T(8,128)S(1)} %pad_maximum_fusion.own_ref), channel_id=1, source_target_pairs={{0,12},{12,24},{24,36},{36,48},{48,60},{60,72},{72,84},{84,96},{96... | collective-permute-start | bytes 2654216 | tf_op jit(solution)/shard_map/ppermute | solution.py:701
  29.2 3.3 %collective-permute-done.3.hi_ref = f32[9,8,24,128]{3,2,1,0:T(8,128)S(1)} collective-permute-done((f32[9,8,24,128]{3,2,1,0:T(8,128)S(1)}, f32[9,8,24,128]{3,2,1,0:T(8,128)S(1)}, u32[]{:S(2)}, u32[]{:S(2)}) %collective-permute-start.3) | collective-permute-done | bytes 884768 | tf_op jit(solution)/shard_map/ppermute | solution.py:701
  32.5 6.7 %collective-permute-done.2.lo_ref = f32[9,8,24,128]{3,2,1,0:T(8,128)S(1)} collective-permute-done((f32[9,8,24,128]{3,2,1,0:T(8,128)S(1)}, f32[9,8,24,128]{3,2,1,0:T(8,128)S(1)}, u32[]{:S(2)}, u32[]{:S(2)}) %collective-permute-start.2) | collective-permute-done | bytes 884768 | tf_op jit(solution)/shard_map/ppermute | solution.py:701
  39.2 4.9 %shard_map.69 = (f32[12,16,128]{2,1,0:T(8,128)S(1)}, f32[3,12,16,128]{3,2,1,0:T(8,128)S(1)}, f32[3,12,16,128]{3,2,1,0:T(8,128)S(1)}, f32[3,12,16,128]{3,2,1,0:T(...) custom-call(f32[9,8,24,128]{3,2,1,0:T(8,128)S(1)} %collective-permut, ...), custom_call_target="tpu_custom_call" | custom-call | tf_op jit(solution)/shard_map/pallas_call | solution.py:387
  44.1 0.0 copy-start.2
  44.1 0.7 copy-done.2
  44.8 0.0 copy-start.7
  44.8 0.6 copy-done.7
  45.4 0.0 copy-start.9
  45.4 20.4 %all_to_all.27.own_ref = f32[12,8,128]{2,1,0:T(8,128)S(1)} all-to-all(f32[12,8,128]{2,1,0:T(8,128)S(1)} %broadcast_in_dim.8), channel_id=1, replica_groups=mesh['gx'=64,'gy'=12] {'gy'}, dimensions={0} | all-to-all | bytes 98304 | tf_op jit(solution)/shard_map/all_to_all | solution.py:706
  65.9 0.0 copy-done.9
  65.9 1.3 collective-permute-start.6
  67.2 1.9 %collective-permute-start.5 = (f32[12,8,128]{2,1,0:T(8,128)S(1)}, f32[12,8,128]{2,1,0:T(8,128)S(1)}, u32[]{:S(2)}, u32[]{:S(2)}) collective-permute-start(f32[12,8,128]{2,1,0:T(8,128)S(1)} %all_to_all.27.own_ref), channel_id=1, source_target_pairs={{12,0},{24,12},{36,24},{48,36},{60,48},{72,60},{84,72},{96,84},{10... | collective-permute-start | bytes 147464 | tf_op jit(solution)/shard_map/ppermute | solution.py:701
  69.1 6.4 %collective-permute-start.4 = (f32[12,8,128]{2,1,0:T(8,128)S(1)}, f32[12,8,128]{2,1,0:T(8,128)S(1)}, u32[]{:S(2)}, u32[]{:S(2)}) collective-permute-start(f32[12,8,128]{2,1,0:T(8,128)S(1)} %all_to_all.27.own_ref), channel_id=1, source_target_pairs={{0,12},{12,24},{24,36},{36,48},{48,60},{60,72},{72,84},{84,96},{96... | collective-permute-start | bytes 147464 | tf_op jit(solution)/shard_map/ppermute | solution.py:701
  75.5 0.0 collective-permute-done.6.hi2_ref
  75.5 0.0 collective-permute-done.5.hi_ref
  75.6 1.1 collective-permute-done.4.lo_ref
  76.7 1.2 shard_map.70
  77.9 0.2 broadcast_in_dim.9
  78.1 30.7 %all_to_all.28 = f32[64,1,1408]{2,1,0:T(1,128)S(1)} all-to-all(f32[64,1,1408]{2,1,0:T(1,128)S(1)} %broadcast_in_dim.9), channel_id=1, replica_groups=mesh['gx'=64,'gy'=12] {'gx'}, dimensions={0} | all-to-all | bytes 720896 | tf_op jit(solution)/shard_map/all_to_all | solution.py:706
  108.8 0.0 copy-start.3
  108.8 0.0 copy-start.8
  108.8 0.0 copy-start.10
  108.8 0.9 copy-done.3
  109.7 0.1 copy-done.8
  109.8 0.0 copy-done.10
  109.9 9.1 %shard_map.71 = (f32[3,8,8,128]{3,2,1,0:T(8,128)S(1)}, f32[3,8,8,128]{3,2,1,0:T(8,128)S(1)}, f32[8,128]{1,0:T(8,128)S(1)}) custom-call(f32[64,1408]{1,0:T(8,128)S(1)} %bitcast.9, f32[8,7,32,128]{3,2,1,0:T(8,128)S(1)} %get-tuple-element.22.l2_ref, f32[3,7,32,128]{3,2,1,0:T(8,128)S(1)} %get-tuple-element.23.s2_ref, ...), custom_call_target="tpu_custom_call" | custom-call | tf_op jit(solution)/shard_map/pallas_call | solution.py:661
  119.0 0.0 copy-start.5
  119.0 0.6 copy-done.5
  119.6 0.0 copy-start.1
  119.6 14.7 %all_to_all.29 = f32[64,1,128]{2,1,0:T(1,128)S(1)} all-to-all(f32[64,1,128]{2,1,0:T(1,128)S(1)} %broadcast_in_dim.10), channel_id=1, replica_groups=mesh['gx'=64,'gy'=12] {'gx'}, dimensions={0} | all-to-all | bytes 65536 | tf_op jit(solution)/shard_map/all_to_all | solution.py:706
  134.4 11.4 %all_to_all.30 = f32[12,1,128]{2,1,0:T(1,128)S(1)} all-to-all(f32[12,1,128]{2,1,0:T(1,128)S(1)} %broadcast_in_dim.11), channel_id=1, replica_groups=mesh['gx'=64,'gy'=12] {'gy'}, dimensions={0} | all-to-all | bytes 12288 | tf_op jit(solution)/shard_map/all_to_all | solution.py:706
  145.8 0.0 copy-done.1
  145.8 0.0 copy-start.6
  145.8 0.9 copy-done.6
  146.7 0.8 shard_map.72
  (9 shorter events, 0.1 us)
Async XLA Ops:
  0.6 0.9 copy-start
  1.5 0.9 copy-start.4
  2.4 0.8 copy-start.11
  3.2 0.8 copy-start.12
  3.9 0.8 copy-start.13
  4.7 8.9 %collective-permute-start.1 = (f32[9,8,8,128]{3,2,1,0:T(8,128)S(1)}, f32[9,8,8,128]{3,2,1,0:T(8,128)S(1)}, u32[]{:S(2)}, u32[]{:S(2)}) collective-permute-start(f32[9,8,8,128]{3,2,1,0:T(8,128)S(1)} %shard_map.68), channel_id=1, source_target_pairs={{1,0},{2,1},{3,2},{4,3},{5,4},{6,5},{7,6},{8,7},{9,8},{10,9},{11,1... | collective-permute-start | bytes 884744 | tf_op jit(solution)/shard_map/ppermute | solution.py:701
  6.0 9.1 %collective-permute-start = (f32[9,8,8,128]{3,2,1,0:T(8,128)S(1)}, f32[9,8,8,128]{3,2,1,0:T(8,128)S(1)}, u32[]{:S(2)}, u32[]{:S(2)}) collective-permute-start(f32[9,8,8,128]{3,2,1,0:T(8,128)S(1)} %shard_map.68), channel_id=1, source_target_pairs={{0,1},{1,2},{2,3},{3,4},{4,5},{5,6},{6,7},{7,8},{8,9},{9,10},{10,1... | collective-permute-start | bytes 884744 | tf_op jit(solution)/shard_map/ppermute | solution.py:701
  15.2 17.3 %collective-permute-start.3 = (f32[9,8,24,128]{3,2,1,0:T(8,128)S(1)}, f32[9,8,24,128]{3,2,1,0:T(8,128)S(1)}, u32[]{:S(2)}, u32[]{:S(2)}) collective-permute-start(f32[9,8,24,128]{3,2,1,0:T(8,128)S(1)} %pad_maximum_fusion.own_ref), channel_id=1, source_target_pairs={{12,0},{24,12},{36,24},{48,36},{60,48},{72,60},{84,72},{96,84},{10... | collective-permute-start | bytes 2654216 | tf_op jit(solution)/shard_map/ppermute | solution.py:701
  27.3 11.9 %collective-permute-start.2 = (f32[9,8,24,128]{3,2,1,0:T(8,128)S(1)}, f32[9,8,24,128]{3,2,1,0:T(8,128)S(1)}, u32[]{:S(2)}, u32[]{:S(2)}) collective-permute-start(f32[9,8,24,128]{3,2,1,0:T(8,128)S(1)} %pad_maximum_fusion.own_ref), channel_id=1, source_target_pairs={{0,12},{12,24},{24,36},{36,48},{48,60},{60,72},{72,84},{84,96},{96... | collective-permute-start | bytes 2654216 | tf_op jit(solution)/shard_map/ppermute | solution.py:701
  44.1 0.7 copy-start.2
  44.8 0.6 copy-start.7
  45.4 20.4 %copy-start.9 = (f32[9,16,128]{2,1,0:T(8,128)}, f32[9,16,128]{2,1,0:T(8,128)S(1)}, u32[]{:S(2)}) copy-start(f32[9,16,128]{2,1,0:T(8,128)S(1)} %get-tuple-element.25.m1_ref) | copy-start | bytes 221188
  65.9 9.7 %collective-permute-start.6 = (f32[12,8,128]{2,1,0:T(8,128)S(1)}, f32[12,8,128]{2,1,0:T(8,128)S(1)}, u32[]{:S(2)}, u32[]{:S(2)}) collective-permute-start(f32[12,8,128]{2,1,0:T(8,128)S(1)} %all_to_all.27.own_ref), channel_id=1, source_target_pairs={{24,0},{36,12},{48,24},{60,36},{72,48},{84,60},{96,72},{108,84},{1... | collective-permute-start | bytes 147464 | tf_op jit(solution)/shard_map/ppermute | solution.py:701
  67.2 8.4 %collective-permute-start.5 = (f32[12,8,128]{2,1,0:T(8,128)S(1)}, f32[12,8,128]{2,1,0:T(8,128)S(1)}, u32[]{:S(2)}, u32[]{:S(2)}) collective-permute-start(f32[12,8,128]{2,1,0:T(8,128)S(1)} %all_to_all.27.own_ref), channel_id=1, source_target_pairs={{12,0},{24,12},{36,24},{48,36},{60,48},{72,60},{84,72},{96,84},{10... | collective-permute-start | bytes 147464 | tf_op jit(solution)/shard_map/ppermute | solution.py:701
  69.1 7.6 %collective-permute-start.4 = (f32[12,8,128]{2,1,0:T(8,128)S(1)}, f32[12,8,128]{2,1,0:T(8,128)S(1)}, u32[]{:S(2)}, u32[]{:S(2)}) collective-permute-start(f32[12,8,128]{2,1,0:T(8,128)S(1)} %all_to_all.27.own_ref), channel_id=1, source_target_pairs={{0,12},{12,24},{24,36},{36,48},{48,60},{60,72},{72,84},{84,96},{96... | collective-permute-start | bytes 147464 | tf_op jit(solution)/shard_map/ppermute | solution.py:701
  108.8 0.9 copy-start.3
  108.8 1.0 copy-start.8
  108.8 1.0 copy-start.10
  119.0 0.6 copy-start.5
  119.6 26.2 %copy-start.1 = (f32[3,8,8,128]{3,2,1,0:T(8,128)S(1)}, f32[3,8,8,128]{3,2,1,0:T(8,128)}, u32[]{:S(2)}) copy-start(f32[3,8,8,128]{3,2,1,0:T(8,128)} %residual_ref.3) | copy-start | bytes 294916
  145.8 0.9 copy-start.6

commit v4 on v3

--- a/solution.py
+++ b/solution.py
@@ -12,7 +12,7 @@
 DAMPING = 0.6
 VOID_MODULUS = 0.001
 F32 = jnp.float32
-PARAMS = pltpu.CompilerParams(vmem_limit_bytes=48 * 1024 * 1024)
+PARAMS = pltpu.CompilerParams(vmem_limit_bytes=16 * 1024 * 1024)
 
 
 def corner_list():
@@ -220,8 +220,8 @@
 
 def first_kernel(
     lo_ref, own_ref, hi_ref,
-    m_out, f_out, r_out, s_out, w_out, m1_out, f1_out, c1_out, s1_out, w1_out, pack_out,
-    t_ref, b_ref, m_ref, f_ref, r_ref, s_ref, w_ref, u_ref, d_ref, v_ref, m1_ref, u1_ref, d1_ref, v2_ref, m2_ref,
+    m_out, i_out, f_out, r_out, m1_out, i1_out, f1_out, c1_out, pack_out,
+    t_ref, b_ref, m_ref, i_ref, f_ref, r_ref, s_ref, u_ref, d_ref, v_ref, m1_ref, s1_ref, u1_ref, d1_ref, v2_ref,
 ):
     pieces = (lo_ref, own_ref, hi_ref)
     slab = (24, 128)
@@ -270,11 +270,11 @@
     def smooth_of(x, ref, i):
         total = corner_sum(m_ref[x] + m_ref[x - 1], z_down)
         inverse = (DAMPING / DIAG) / total
+        i_ref[x] = inverse
         for c in range(3):
             free, r = (ref[3 + c, i], ref[6 + c, i])
-            w = scaled(free, inverse)
-            s = w * r
-            f_ref[c, x], r_ref[c, x], w_ref[c, x], s_ref[c, x] = (free, r, w, s)
+            s = scaled(free, inverse) * r
+            f_ref[c, x], r_ref[c, x], s_ref[c, x] = (free, r, s)
             u_ref[c, x] = free * s
 
     each(2, 22, smooth_of)
@@ -288,11 +288,10 @@
 
     def keep(x, _):
         m_out[x] = m_ref[x + 6, 4:20, :]
+        i_out[x] = i_ref[x + 6, 4:20, :]
         for c in range(3):
             f_out[c, x] = f_ref[c, x + 6, 4:20, :]
             r_out[c, x] = r_ref[c, x + 6, 4:20, :]
-            s_out[c, x] = s_ref[c, x + 6, 4:20, :]
-            w_out[c, x] = w_ref[c, x + 6, 4:20, :]
 
     lax.fori_loop(0, 12, keep, None, unroll=2)
 
@@ -328,10 +327,10 @@
 
     def smooth1(n, _):
         inverse = (DAMPING / DIAG) / corner_sum(m1_ref[n + 1] + m1_ref[n], plain_down)
-        for c in range(3):
-            w = scaled(f1_out[c, n], inverse)
-            s = w * c1_out[c, n]
-            w1_out[c, n], s1_out[c, n] = (w, s)
+        i1_out[n] = inverse
+        for c in range(3):
+            s = scaled(f1_out[c, n], inverse) * c1_out[c, n]
+            s1_ref[c, n] = s
             u1_ref[c, n] = f1_out[c, n] * s
 
     lax.fori_loop(0, 9, smooth1, None, unroll=True)
@@ -339,46 +338,46 @@
     def defect1(n, forces):
         for c in range(3):
             free = f1_out[c, n]
-            d1_ref[c, n] = c1_out[c, n] - (free * forces[c] + (1.0 - free) * s1_out[c, n])
-
-    sweep(lambda c, n: u1_ref[c, n], lambda n: m1_ref[n + 1], 0, 5, False, defect1)
-
-    for n in range(2):
+            d1_ref[c, n] = c1_out[c, n] - (free * forces[c] + (1.0 - free) * s1_ref[c, n])
+
+    sweep(lambda c, n: u1_ref[c, n], lambda n: m1_ref[n + 1], 0, 7, False, defect1)
+
+    for n in range(3):
         x = 2 * n + 2
         for c in range(3):
-            v2_ref[2 * c + n] = smooth_rows(d1_ref[c, x] + 0.5 * (d1_ref[c, x - 1] + d1_ref[c, x + 1]))
-            v2_ref[6 + 2 * c + n] = f1_out[c, x]
-    for n in range(3):
+            v2_ref[3 * c + n] = smooth_rows(d1_ref[c, x] + 0.5 * (d1_ref[c, x - 1] + d1_ref[c, x + 1]))
+            v2_ref[9 + 3 * c + n] = f1_out[c, x]
+    for n in range(4):
         v = m1_ref[2 * n + 1] + m1_ref[2 * n + 2]
-        v2_ref[12 + n] = v + y_up(v)
-    v2_ref[15] = jnp.zeros((16, 128), F32)
+        v2_ref[18 + n] = v + y_up(v)
 
     def half2(first, count, matrix):
         v = v2_ref[first : first + count, pl.ds(0, 8, stride=2), :]
         return exact_dot(v.reshape(count * 8, 128), matrix).reshape(count, 8, 128)
 
-    free2 = half2(6, 6, pick)
-    rhs2 = half2(0, 6, restrict) * free2
-    m2_ref[...] = 0.25 * half2(12, 4, pair)
-    fields = [[m2_ref[1], m2_ref[2]]]
-    fields += [[free2[2 * c], free2[2 * c + 1]] for c in range(3)]
-    fields += [[rhs2[2 * c], rhs2[2 * c + 1]] for c in range(3)]
+    free2 = half2(9, 9, pick)
+    rhs2 = half2(0, 9, restrict) * free2
+    moduli2 = 0.25 * half2(18, 4, pair)
+    fields = [[moduli2[1 + n] for n in range(3)]]
+    fields += [[free2[3 * c + n] for n in range(3)] for c in range(3)]
+    fields += [[rhs2[3 * c + n] for n in range(3)] for c in range(3)]
     valid = lanes_of((8, 128)) < 32
     inverse = []
-    for n in range(2):
-        total = corner_sum(m2_ref[n + 1] + m2_ref[n], plain_down)
+    for n in range(3):
+        total = corner_sum(moduli2[n + 1] + moduli2[n], plain_down)
         inverse.append(jnp.where(total > 0.0, (DAMPING / DIAG) / total, 0.0))
     fields.append(inverse)
-    for f, pairs in enumerate(fields):
-        row = None
-        for n in range(2):
-            v = jnp.where(valid, pairs[n], 0.0)
+    for f, slabs in enumerate(fields):
+        rows = [None, None]
+        for n in range(3):
+            v = jnp.where(valid, slabs[n], 0.0)
             for y in range(2):
                 piece = v[2 + y : 3 + y]
-                q = 2 * n + y
+                q = 2 * (n % 2) + y
                 piece = pltpu.roll(piece, 32 * q, 1) if q else piece
-                row = piece if row is None else row + piece
-        pack_out[f : f + 1, :] = row
+                rows[n // 2] = piece if rows[n // 2] is None else rows[n // 2] + piece
+        pack_out[f : f + 1, 0:128] = rows[0]
+        pack_out[f : f + 1, 128:256] = rows[1]
 
 
 def first_call(lo, own, hi):
@@ -386,49 +385,49 @@
     s24 = lambda *s: pltpu.VMEM(s + (24, 128), F32)
     return pl.pallas_call(
         first_kernel,
-        out_shape=[big(12), big(3, 12), big(3, 12), big(3, 12), big(3, 12)]
-        + [big(9), big(3, 9), big(3, 9), big(3, 9), big(3, 9), jax.ShapeDtypeStruct((8, 128), F32)],
-        scratch_shapes=[s24(24), s24(24), s24(24)]
-        + [s24(3, 24)] * 6
+        out_shape=[big(12), big(12), big(3, 12), big(3, 12)]
+        + [big(9), big(9), big(3, 9), big(3, 9), jax.ShapeDtypeStruct((8, 256), F32)],
+        scratch_shapes=[s24(24)] * 4
+        + [s24(3, 24)] * 5
         + [
             pltpu.VMEM((64, 32, 128), F32),
             pltpu.VMEM((10, 16, 128), F32),
             pltpu.VMEM((3, 9, 16, 128), F32),
             pltpu.VMEM((3, 9, 16, 128), F32),
-            pltpu.VMEM((16, 16, 128), F32),
-            pltpu.VMEM((4, 8, 128), F32),
+            pltpu.VMEM((3, 9, 16, 128), F32),
+            pltpu.VMEM((22, 16, 128), F32),
         ],
         compiler_params=PARAMS,
     )(lo, own, hi)
 
 
-def second_kernel(lo_ref, own_ref, hi_ref, hi2_ref, l_out, s_out, w_out, pack_out, u_ref, d_ref, v_ref):
+def second_kernel(lo_ref, own_ref, hi_ref, l_out, pack_out, s_ref, u_ref, d_ref, v_ref):
     peers = own_ref.shape[0]
     l_out[...] = jnp.zeros(l_out.shape, F32)
     valid = lanes_of((peers, 128)) < 32
-    for ref, base, count in ((lo_ref, 0, 2), (own_ref, 2, 2), (hi_ref, 4, 2), (hi2_ref, 6, 1)):
+    for ref, base, count in ((lo_ref, 0, 2), (own_ref, 2, 2), (hi_ref, 4, 3)):
         for f in range(8):
-            rows = ref[:, f, :]
-            for n in range(count):
-                for y in range(2):
-                    q = 2 * n + y
-                    v = pltpu.roll(rows, 128 - 32 * q, 1) if q else rows
-                    l_out[f, base + n, pl.ds(y, peers, stride=2), :] = jnp.where(valid, v, 0.0)
+            for h in range((count + 1) // 2):
+                rows = ref[:, f, 128 * h : 128 * h + 128]
+                for n in range(2 * h, min(2 * h + 2, count)):
+                    for y in range(2):
+                        q = 2 * (n % 2) + y
+                        v = pltpu.roll(rows, 128 - 32 * q, 1) if q else rows
+                        l_out[f, base + n, pl.ds(y, peers, stride=2), :] = jnp.where(valid, v, 0.0)
 
     def smooth(n, _):
         inverse = l_out[7, n]
         for c in range(3):
-            w = scaled(l_out[1 + c, n], inverse)
-            s = w * l_out[4 + c, n]
-            w_out[c, n], s_out[c, n] = (w, s)
+            s = scaled(l_out[1 + c, n], inverse) * l_out[4 + c, n]
+            s_ref[c, n] = s
             u_ref[c, n] = l_out[1 + c, n] * s
 
-    lax.fori_loop(0, 7, smooth, None, unroll=True)
+    lax.fori_loop(0, 5, smooth, None, unroll=True)
 
     def defect(n, forces):
         for c in range(3):
             free = l_out[1 + c, n]
-            d_ref[c, n] = l_out[4 + c, n] - (free * forces[c] + (1.0 - free) * s_out[c, n])
+            d_ref[c, n] = l_out[4 + c, n] - (free * forces[c] + (1.0 - free) * s_ref[c, n])
 
     sweep(lambda c, n: u_ref[c, n], lambda n: l_out[0, n], 0, 3, False, defect)
     for c in range(3):
@@ -458,15 +457,15 @@
         pack_out[:, 128 * t : 128 * t + 128] = v
 
 
-def second_call(lo, own, hi, hi2):
+def second_call(lo, own, hi):
     big = lambda *s: jax.ShapeDtypeStruct(s + (32, 128), F32)
     vmem = lambda *s: pltpu.VMEM(s + (32, 128), F32)
     return pl.pallas_call(
         second_kernel,
-        out_shape=[big(8, 7), big(3, 7), big(3, 7), jax.ShapeDtypeStruct((1, 1408), F32)],
-        scratch_shapes=[vmem(3, 7), vmem(3, 7), vmem(7)],
+        out_shape=[big(8, 7), jax.ShapeDtypeStruct((1, 1408), F32)],
+        scratch_shapes=[vmem(3, 5), vmem(3, 5), vmem(3, 4), vmem(7)],
         compiler_params=PARAMS,
-    )(lo, own, hi, hi2)
+    )(lo, own, hi)
 
 
 def pack_rows(fields):
@@ -549,9 +548,9 @@
 
 
 def third_kernel(
-    rows_ref, l2_ref, s2_ref, w2_ref, m1_ref, f1_ref, c1_ref, s1_ref, w1_ref, m_ref, f_ref, r_ref, s_ref, w_ref,
+    rows_ref, l2_ref, m1_ref, i1_ref, f1_ref, c1_ref, m_ref, i_ref, f_ref, r_ref,
     p_out, q_out, sum_out,
-    a_ref, z3_ref, p2_ref, u2_ref, y2_ref, v2_ref, p1_ref, u1_ref, y1_ref, v1_ref, p0_ref, u0_ref, y0_ref,
+    a_ref, z3_ref, u2_ref, y2_ref, v2_ref, p1_ref, u1_ref, y1_ref, v1_ref, p0_ref, u0_ref, y0_ref,
 ):
     gx, gy = (lax.axis_index("gx"), lax.axis_index("gy"))
     peers = rows_ref.shape[0]
@@ -577,7 +576,7 @@
             i = n // 2
             p = z3_ref[i] if n % 2 == 0 else 0.5 * (z3_ref[i] + z3_ref[i + 1])
             free = l2_ref[1 + c, n]
-            s = s2_ref[c, n] + free * p
+            s = scaled(free, l2_ref[7, n]) * l2_ref[4 + c, n] + free * p
             y2_ref[c, n] = s
             u2_ref[c, n] = free * s
 
@@ -587,7 +586,7 @@
         for c in range(3):
             free, s = (l2_ref[1 + c, n], y2_ref[c, n])
             image = free * forces[c] + (1.0 - free) * s
-            v2_ref[c, n - 1, 8:40, :] = s + w2_ref[c, n] * (l2_ref[4 + c, n] - image)
+            v2_ref[c, n - 1, 8:40, :] = s + scaled(free, l2_ref[7, n]) * (l2_ref[4 + c, n] - image)
 
     sweep(lambda c, n: u2_ref[c, n], lambda n: l2_ref[0, n], 0, 5, False, level2)
 
@@ -601,7 +600,7 @@
             i = n // 2
             p = p1_ref[c, i] if n % 2 == 0 else 0.5 * (p1_ref[c, i] + p1_ref[c, i + 1])
             free = f1_ref[c, n]
-            s = s1_ref[c, n] + free * p
+            s = scaled(free, i1_ref[n]) * c1_ref[c, n] + free * p
             y1_ref[c, n] = s
             u1_ref[c, n] = free * s
 
@@ -609,7 +608,7 @@
         for c in range(3):
             free, s = (f1_ref[c, n], y1_ref[c, n])
             image = free * forces[c] + (1.0 - free) * s
-            v1_ref[c, n - 1] = s + w1_ref[c, n] * (c1_ref[c, n] - image)
+            v1_ref[c, n - 1] = s + scaled(free, i1_ref[n]) * (c1_ref[c, n] - image)
 
     sweep(lambda c, n: u1_ref[c, n], lambda n: m1_ref[n], 0, 7, False, level1)
 
@@ -622,7 +621,7 @@
             i = n // 2
             p = p0_ref[c, i] if n % 2 == 0 else 0.5 * (p0_ref[c, i] + p0_ref[c, i + 1])
             free = f_ref[c, n]
-            s = s_ref[c, n] + free * p
+            s = scaled(free, i_ref[n]) * r_ref[c, n] + free * p
             y0_ref[c, n] = s
             u0_ref[c, n] = free * s
 
@@ -630,7 +629,7 @@
         for c in range(3):
             free, s = (f_ref[c, n], y0_ref[c, n])
             image = free * forces[c] + (1.0 - free) * s
-            y0_ref[c, n] = s + w_ref[c, n] * (r_ref[c, n] - image)
+            y0_ref[c, n] = s + scaled(free, i_ref[n]) * (r_ref[c, n] - image)
 
     sweep(lambda c, n: u0_ref[c, n], lambda n: m_ref[n], 0, 10, True, level0)
     sum_out[...] = jnp.zeros((8, 128), F32)
@@ -664,7 +663,6 @@
         scratch_shapes=[
             pltpu.VMEM((3, peers + 16, 256), F32),
             pltpu.VMEM((4, 32, 128), F32),
-            pltpu.VMEM((1, 8, 128), F32),
             pltpu.VMEM((3, 7, 32, 128), F32),
             pltpu.VMEM((3, 7, 32, 128), F32),
             pltpu.VMEM((3, 5, 48, 128), F32),
@@ -677,23 +675,35 @@
             pltpu.VMEM((3, 12, 16, 128), F32),
         ],
         compiler_params=PARAMS,
-    )(rows, *level2, *level1, *level0)
-
-
-def pack_kernel(density_ref, solid_ref, void_ref, fixed_ref, residual_ref, out_ref):
-    out_ref[0] = density_ref[...]
-    out_ref[1] = solid_ref[...].astype(F32)
-    out_ref[2] = void_ref[...].astype(F32)
-    out_ref[3:6] = 1.0 - fixed_ref[...].astype(F32)
-    out_ref[6:9] = residual_ref[...]
-
-
-def last_kernel(sums_ref, precond_ref, image_ref, residual_ref, update_ref, next_ref):
+    )(rows, level2, *level1, *level0)
+
+
+def pack_kernel(density_ref, solid_ref, void_ref, fixed_ref, residual_ref, out_ref, flags_ref, fixed_to, sems):
+    copies = [
+        pltpu.make_async_copy(solid_ref, flags_ref.at[0], sems.at[0]),
+        pltpu.make_async_copy(void_ref, flags_ref.at[1], sems.at[1]),
+        pltpu.make_async_copy(fixed_ref, fixed_to, sems.at[2]),
+        pltpu.make_async_copy(density_ref, out_ref.at[0], sems.at[3]),
+        pltpu.make_async_copy(residual_ref, out_ref.at[pl.ds(6, 3)], sems.at[4]),
+    ]
+    for copy in copies:
+        copy.start()
+    copies[0].wait()
+    out_ref[1] = flags_ref[0].astype(F32)
+    copies[1].wait()
+    out_ref[2] = flags_ref[1].astype(F32)
+    copies[2].wait()
+    out_ref[3:6] = 1.0 - fixed_to[...].astype(F32)
+    copies[3].wait()
+    copies[4].wait()
+
+
+def last_kernel(sums_ref, precond_ref, image_ref, packed_ref, update_ref, next_ref):
     total = jnp.sum(sums_ref[...], axis=0, keepdims=True)
     alpha = total[:, 0:1] / total[:, 1:2]
     for c in range(3):
         update_ref[c] = alpha * precond_ref[c]
-        next_ref[c] = residual_ref[c] - alpha * image_ref[c]
+        next_ref[c] = packed_ref[6 + c] - alpha * image_ref[c]
 
 
 def from_peer(value, axis, step):
@@ -712,22 +722,28 @@
     packed = pl.pallas_call(
         pack_kernel,
         out_shape=jax.ShapeDtypeStruct((9,) + density.shape, F32),
-        compiler_params=PARAMS,
+        in_specs=[pl.BlockSpec(memory_space=pltpu.HBM)] * 5,
+        scratch_shapes=[
+            pltpu.VMEM((2,) + solid.shape, jnp.int32),
+            pltpu.VMEM(fixed.shape, jnp.int32),
+            pltpu.SemaphoreType.DMA((5,)),
+        ],
+        compiler_params=pltpu.CompilerParams(vmem_limit_bytes=60 * 1024 * 1024),
     )(density, solid, void, fixed, residual)
     own = jnp.concatenate([from_peer(packed, "gy", -1), packed, from_peer(packed, "gy", 1)], axis=2)
     first = first_call(from_peer(own, "gx", -1), own, from_peer(own, "gx", 1))
-    level0, level1, piece = (first[0:5], first[5:10], first[10])
+    level0, level1, piece = (first[0:4], first[4:8], first[8])
     columns = spread_all(piece, "gy")
     second = second_call(
-        from_peer(columns, "gx", -1), columns, from_peer(columns, "gx", 1), from_peer(columns, "gx", 2)
+        from_peer(columns, "gx", -1), columns, from_peer(columns, "gx", 1)
     )
-    rows = spread_all(second[3].reshape(-1), "gx")
-    precond, image, sums = third_call(rows, second[0:3], level1, level0)
+    rows = spread_all(second[1].reshape(-1), "gx")
+    precond, image, sums = third_call(rows, second[0], level1, level0)
     sums = jnp.sum(spread_all(sums[0], "gx"), axis=0)
     block = jax.ShapeDtypeStruct(residual.shape, F32)
     return tuple(
         pl.pallas_call(last_kernel, out_shape=[block, block], compiler_params=PARAMS)(
-            spread_all(sums, "gy"), precond, image, residual
+            spread_all(sums, "gy"), precond, image, packed
         )
     )
 

time: 148 us -> 142 us (0.959)
  local copies, waits for them, and re-layouts: 8.18 us -> 0.26 us
  Pallas kernels: 16 us -> 17.8 us
  starting transfers between devices: 30.4 us -> 28.9 us
    unnamed x30 -> x4, local copies, waits for them, and re-layouts: 7.96 us -> 0.03 us
    pallas_call x1, Pallas kernels: 0.02 us -> 1.75 us  [on_device(): pl.pallas_call(pack_kernel, out_shape=jax.ShapeDtypeStruct((9,) + density...]
    ppermute x7 -> x6, starting transfers between devices: 30.4 us -> 28.9 us  [from_peer(): lax.ppermute(value, axis, [(i + step, i) for i in range(peers) if 0 <= i...]
    ppermute x7 -> x6, waiting for transfers between devices: 14.7 us -> 15.5 us  [from_peer(): lax.ppermute(value, axis, [(i + step, i) for i in range(peers) if 0 <= i...]
  transfers between devices with their start and end apart: 7 -> 6, of which waited for: 5 -> 6; matrix products, arithmetic and copies ran while one was open for 0% -> 0% of each run, Pallas kernels for 0% -> 0%
where the time goes in v4:
time: 142 us
  blocking collectives  77.6 us (55%)
  starting transfers between devices  28.9 us (20%)
  Pallas kernels  17.8 us (13%)
  waiting for transfers between devices  15.5 us (11%)
    all_to_all x4, blocking collectives, spread_all(): lax.all_to_all(jnp.broadcast_to(row[None], (peers,) + row.shape), axis, 0...  77.6 us
    ppermute x6, starting transfers between devices, from_peer(): lax.ppermute(value, axis, [(i + step, i) for i in range(peers) if 0 <= i...  28.9 us
    ppermute x6, waiting for transfers between devices, from_peer(): lax.ppermute(value, axis, [(i + step, i) for i in range(peers) if 0 <= i...  15.5 us
    pallas_call x1, Pallas kernels, third_call(): pl.pallas_call(third_kernel, out_shape=[own, own, jax.ShapeDtypeStruct((8...  9.11 us
    pallas_call x1, Pallas kernels, first_call(): pl.pallas_call(first_kernel, out_shape=[big(12), big(12), big(3, 12), big...  4.99 us
  transfers between devices with their start and end apart: 6, of which 6 were waited for; matrix products, arithmetic and copies ran while one was open for 0% of the time, Pallas kernels for 0%

profile of v4, /device:TPU:1, one launch (start us, length us, event | category | flops | bytes accessed | tf_op | source)
XLA Modules:
  0.0 141.8 jit_solution(9121144208075985681)
XLA Ops:
  0.6 1.8 %shard_map.68.packed_ref = f32[9,8,8,128]{3,2,1,0:T(8,128)} custom-call(f32[8,8,128]{2,1,0:T(8,128)} %density_ref.1, s32[8,8,128]{2,1,0:T(8,128)} %solid_ref.1, s32[8,8,128]{2,1,0:T(8,128)} %void_ref.1, s32[3,8,8,128]{3,2,1,0:T(8,128)} %fixed_ref.1, f32[3,8,8,128]{3,2,1,0:T(8,128)} %residual_ref.1), custom_call_target="tpu_custom_call" | custom-call | tf_op jit(solution)/shard_map/pallas_call | solution.py:722
  2.4 1.3 collective-permute-start.1
  3.7 5.5 %collective-permute-start = (f32[9,8,8,128]{3,2,1,0:T(8,128)}, f32[9,8,8,128]{3,2,1,0:T(8,128)S(1)}, u32[]{:S(2)}, u32[]{:S(2)}) collective-permute-start(f32[9,8,8,128]{3,2,1,0:T(8,128)} %shard_map.68.packed_ref), channel_id=1, source_target_pairs={{0,1},{1,2},{2,3},{3,4},{4,5},{5,6},{6,7},{7,8},{8,9},{9,10},{10,1... | collective-permute-start | bytes 884744 | tf_op jit(solution)/shard_map/ppermute | solution.py:711
  9.2 2.4 %collective-permute-done.1 = f32[9,8,8,128]{3,2,1,0:T(8,128)S(1)} collective-permute-done((f32[9,8,8,128]{3,2,1,0:T(8,128)}, f32[9,8,8,128]{3,2,1,0:T(8,128)S(1)}, u32[]{:S(2)}, u32[]{:S(2)}) %collective-permute-start.1) | collective-permute-done | bytes 294944 | tf_op jit(solution)/shard_map/ppermute | solution.py:711
  11.5 1.6 %collective-permute-done = f32[9,8,8,128]{3,2,1,0:T(8,128)S(1)} collective-permute-done((f32[9,8,8,128]{3,2,1,0:T(8,128)}, f32[9,8,8,128]{3,2,1,0:T(8,128)S(1)}, u32[]{:S(2)}, u32[]{:S(2)}) %collective-permute-start) | collective-permute-done | bytes 294944 | tf_op jit(solution)/shard_map/ppermute | solution.py:711
  13.1 1.0 pad_maximum_fusion.own_ref
  14.1 12.1 %collective-permute-start.3 = (f32[9,8,24,128]{3,2,1,0:T(8,128)S(1)}, f32[9,8,24,128]{3,2,1,0:T(8,128)S(1)}, u32[]{:S(2)}, u32[]{:S(2)}) collective-permute-start(f32[9,8,24,128]{3,2,1,0:T(8,128)S(1)} %pad_maximum_fusion.own_ref), channel_id=1, source_target_pairs={{12,0},{24,12},{36,24},{48,36},{60,48},{72,60},{84,72},{96,84},{10... | collective-permute-start | bytes 2654216 | tf_op jit(solution)/shard_map/ppermute | solution.py:711
  26.2 1.9 %collective-permute-start.2 = (f32[9,8,24,128]{3,2,1,0:T(8,128)S(1)}, f32[9,8,24,128]{3,2,1,0:T(8,128)S(1)}, u32[]{:S(2)}, u32[]{:S(2)}) collective-permute-start(f32[9,8,24,128]{3,2,1,0:T(8,128)S(1)} %pad_maximum_fusion.own_ref), channel_id=1, source_target_pairs={{0,12},{12,24},{24,36},{36,48},{48,60},{60,72},{72,84},{84,96},{96... | collective-permute-start | bytes 2654216 | tf_op jit(solution)/shard_map/ppermute | solution.py:711
  28.2 3.3 %collective-permute-done.3.hi_ref = f32[9,8,24,128]{3,2,1,0:T(8,128)S(1)} collective-permute-done((f32[9,8,24,128]{3,2,1,0:T(8,128)S(1)}, f32[9,8,24,128]{3,2,1,0:T(8,128)S(1)}, u32[]{:S(2)}, u32[]{:S(2)}) %collective-permute-start.3) | collective-permute-done | bytes 884768 | tf_op jit(solution)/shard_map/ppermute | solution.py:711
  31.4 6.7 %collective-permute-done.2.lo_ref = f32[9,8,24,128]{3,2,1,0:T(8,128)S(1)} collective-permute-done((f32[9,8,24,128]{3,2,1,0:T(8,128)S(1)}, f32[9,8,24,128]{3,2,1,0:T(8,128)S(1)}, u32[]{:S(2)}, u32[]{:S(2)}) %collective-permute-start.2) | collective-permute-done | bytes 884768 | tf_op jit(solution)/shard_map/ppermute | solution.py:711
  38.1 5.0 %shard_map.69 = (f32[12,16,128]{2,1,0:T(8,128)S(1)}, f32[12,16,128]{2,1,0:T(8,128)S(1)}, f32[3,12,16,128]{3,2,1,0:T(8,128)S(1)}, f32[3,12,16,128]{3,2,1,0:T(8,12...) custom-call(f32[9,8,24,128]{3,2,1,0:T(8,128)S(1)} %collective-permut, ...), custom_call_target="tpu_custom_call" | custom-call | tf_op jit(solution)/shard_map/pallas_call | solution.py:386
  43.1 20.7 %all_to_all.27.own_ref = f32[12,8,256]{2,1,0:T(8,128)S(1)} all-to-all(f32[12,8,256]{2,1,0:T(8,128)S(1)} %broadcast_in_dim.8), channel_id=1, replica_groups=mesh['gx'=64,'gy'=12] {'gy'}, dimensions={0} | all-to-all | bytes 196608 | tf_op jit(solution)/shard_map/all_to_all | solution.py:716
  63.9 1.9 %collective-permute-start.5 = (f32[12,8,256]{2,1,0:T(8,128)S(1)}, f32[12,8,256]{2,1,0:T(8,128)S(1)}, u32[]{:S(2)}, u32[]{:S(2)}) collective-permute-start(f32[12,8,256]{2,1,0:T(8,128)S(1)} %all_to_all.27.own_ref), channel_id=1, source_target_pairs={{12,0},{24,12},{36,24},{48,36},{60,48},{72,60},{84,72},{96,84},{10... | collective-permute-start | bytes 294920 | tf_op jit(solution)/shard_map/ppermute | solution.py:711
  65.8 6.2 %collective-permute-start.4 = (f32[12,8,256]{2,1,0:T(8,128)S(1)}, f32[12,8,256]{2,1,0:T(8,128)S(1)}, u32[]{:S(2)}, u32[]{:S(2)}) collective-permute-start(f32[12,8,256]{2,1,0:T(8,128)S(1)} %all_to_all.27.own_ref), channel_id=1, source_target_pairs={{0,12},{12,24},{24,36},{36,48},{48,60},{60,72},{72,84},{84,96},{96... | collective-permute-start | bytes 294920 | tf_op jit(solution)/shard_map/ppermute | solution.py:711
  72.0 0.4 collective-permute-done.5.hi_ref
  72.4 1.3 collective-permute-done.4.lo_ref
  73.6 1.1 shard_map.70
  74.8 0.2 broadcast_in_dim.9
  75.0 30.8 %all_to_all.28 = f32[64,1,1408]{2,1,0:T(1,128)S(1)} all-to-all(f32[64,1,1408]{2,1,0:T(1,128)S(1)} %broadcast_in_dim.9), channel_id=1, replica_groups=mesh['gx'=64,'gy'=12] {'gx'}, dimensions={0} | all-to-all | bytes 720896 | tf_op jit(solution)/shard_map/all_to_all | solution.py:716
  105.8 0.0 copy-start
  105.8 9.1 %shard_map.71 = (f32[3,8,8,128]{3,2,1,0:T(8,128)S(1)}, f32[3,8,8,128]{3,2,1,0:T(8,128)S(1)}, f32[8,128]{1,0:T(8,128)S(1)}) custom-call(f32[64,1408]{1,0:T(8,128)S(1)} %bitcast.9, f32[8,7,32,128]{3,2,1,0:T(8,128)S(1)} %get-tuple-element.18.l2_ref, f32[9,16,128]{2,1,0:T(8,128)S(1)} %get-tuple-element.19.m1_ref, f32[9,16,128]{2,1,0:T(8,128)S(1)} %get-tuple-element.20.i1_ref, ...), custom_call_target="tpu_custom_call" | custom-call | tf_op jit(solution)/shard_map/pallas_call | solution.py:660
  115.0 14.6 %all_to_all.29 = f32[64,1,128]{2,1,0:T(1,128)S(1)} all-to-all(f32[64,1,128]{2,1,0:T(1,128)S(1)} %broadcast_in_dim.10), channel_id=1, replica_groups=mesh['gx'=64,'gy'=12] {'gx'}, dimensions={0} | all-to-all | bytes 65536 | tf_op jit(solution)/shard_map/all_to_all | solution.py:716
  129.6 11.4 %all_to_all.30 = f32[12,1,128]{2,1,0:T(1,128)S(1)} all-to-all(f32[12,1,128]{2,1,0:T(1,128)S(1)} %broadcast_in_dim.11), channel_id=1, replica_groups=mesh['gx'=64,'gy'=12] {'gy'}, dimensions={0} | all-to-all | bytes 12288 | tf_op jit(solution)/shard_map/all_to_all | solution.py:716
  141.0 0.0 copy-done
  141.0 0.8 shard_map.72
  (8 shorter events, 0.1 us)
Async XLA Ops:
  2.4 9.1 %collective-permute-start.1 = (f32[9,8,8,128]{3,2,1,0:T(8,128)}, f32[9,8,8,128]{3,2,1,0:T(8,128)S(1)}, u32[]{:S(2)}, u32[]{:S(2)}) collective-permute-start(f32[9,8,8,128]{3,2,1,0:T(8,128)} %shard_map.68.packed_ref), channel_id=1, source_target_pairs={{1,0},{2,1},{3,2},{4,3},{5,4},{6,5},{7,6},{8,7},{9,8},{10,9},{11,1... | collective-permute-start | bytes 884744 | tf_op jit(solution)/shard_map/ppermute | solution.py:711
  3.7 9.4 %collective-permute-start = (f32[9,8,8,128]{3,2,1,0:T(8,128)}, f32[9,8,8,128]{3,2,1,0:T(8,128)S(1)}, u32[]{:S(2)}, u32[]{:S(2)}) collective-permute-start(f32[9,8,8,128]{3,2,1,0:T(8,128)} %shard_map.68.packed_ref), channel_id=1, source_target_pairs={{0,1},{1,2},{2,3},{3,4},{4,5},{5,6},{6,7},{7,8},{8,9},{9,10},{10,1... | collective-permute-start | bytes 884744 | tf_op jit(solution)/shard_map/ppermute | solution.py:711
  14.1 17.3 %collective-permute-start.3 = (f32[9,8,24,128]{3,2,1,0:T(8,128)S(1)}, f32[9,8,24,128]{3,2,1,0:T(8,128)S(1)}, u32[]{:S(2)}, u32[]{:S(2)}) collective-permute-start(f32[9,8,24,128]{3,2,1,0:T(8,128)S(1)} %pad_maximum_fusion.own_ref), channel_id=1, source_target_pairs={{12,0},{24,12},{36,24},{48,36},{60,48},{72,60},{84,72},{96,84},{10... | collective-permute-start | bytes 2654216 | tf_op jit(solution)/shard_map/ppermute | solution.py:711
  26.2 11.9 %collective-permute-start.2 = (f32[9,8,24,128]{3,2,1,0:T(8,128)S(1)}, f32[9,8,24,128]{3,2,1,0:T(8,128)S(1)}, u32[]{:S(2)}, u32[]{:S(2)}) collective-permute-start(f32[9,8,24,128]{3,2,1,0:T(8,128)S(1)} %pad_maximum_fusion.own_ref), channel_id=1, source_target_pairs={{0,12},{12,24},{24,36},{36,48},{48,60},{60,72},{72,84},{84,96},{96... | collective-permute-start | bytes 2654216 | tf_op jit(solution)/shard_map/ppermute | solution.py:711
  63.9 8.5 %collective-permute-start.5 = (f32[12,8,256]{2,1,0:T(8,128)S(1)}, f32[12,8,256]{2,1,0:T(8,128)S(1)}, u32[]{:S(2)}, u32[]{:S(2)}) collective-permute-start(f32[12,8,256]{2,1,0:T(8,128)S(1)} %all_to_all.27.own_ref), channel_id=1, source_target_pairs={{12,0},{24,12},{36,24},{48,36},{60,48},{72,60},{84,72},{96,84},{10... | collective-permute-start | bytes 294920 | tf_op jit(solution)/shard_map/ppermute | solution.py:711
  65.8 7.8 %collective-permute-start.4 = (f32[12,8,256]{2,1,0:T(8,128)S(1)}, f32[12,8,256]{2,1,0:T(8,128)S(1)}, u32[]{:S(2)}, u32[]{:S(2)}) collective-permute-start(f32[12,8,256]{2,1,0:T(8,128)S(1)} %all_to_all.27.own_ref), channel_id=1, source_target_pairs={{0,12},{12,24},{24,36},{36,48},{48,60},{60,72},{72,84},{84,96},{96... | collective-permute-start | bytes 294920 | tf_op jit(solution)/shard_map/ppermute | solution.py:711
  105.8 35.2 %copy-start = (f32[9,8,8,128]{3,2,1,0:T(8,128)S(1)}, f32[9,8,8,128]{3,2,1,0:T(8,128)}, u32[]{:S(2)}) copy-start(f32[9,8,8,128]{3,2,1,0:T(8,128)} %shard_map.68.packed_ref) | copy-start | bytes 884740

commit v5 on v4

--- a/solution.py
+++ b/solution.py
@@ -12,6 +12,7 @@
 DAMPING = 0.6
 VOID_MODULUS = 0.001
 F32 = jnp.float32
+GX = ("chip", "core")
 PARAMS = pltpu.CompilerParams(vmem_limit_bytes=16 * 1024 * 1024)
 
 
@@ -226,8 +227,8 @@
     pieces = (lo_ref, own_ref, hi_ref)
     slab = (24, 128)
     z_up, z_down = z_shifts(True)
-    gx, gy = (lax.axis_index("gx"), lax.axis_index("gy"))
-    nodes_x, nodes_y = (8 * lax.axis_size("gx"), 8 * lax.axis_size("gy"))
+    gx, gy = (lax.axis_index(GX), lax.axis_index("gy"))
+    nodes_x, nodes_y = (8 * lax.axis_size(GX), 8 * lax.axis_size("gy"))
     w0, w1, w2, w3 = [2.0 - math.sqrt(n) for n in range(4)]
 
     def each(first, last, body):
@@ -401,14 +402,21 @@
     )(lo, own, hi)
 
 
-def second_kernel(lo_ref, own_ref, hi_ref, l_out, pack_out, s_ref, u_ref, d_ref, v_ref):
-    peers = own_ref.shape[0]
+def second_kernel(pair_ref, far_ref, l_out, pack_out, s_ref, u_ref, d_ref, v_ref):
+    peers = far_ref.shape[0]
+    first = lax.axis_index("core") == 0
     l_out[...] = jnp.zeros(l_out.shape, F32)
     valid = lanes_of((peers, 128)) < 32
-    for ref, base, count in ((lo_ref, 0, 2), (own_ref, 2, 2), (hi_ref, 4, 3)):
+    for piece, (base, count) in enumerate(((0, 2), (2, 2), (4, 3))):
         for f in range(8):
             for h in range((count + 1) // 2):
-                rows = ref[:, f, 128 * h : 128 * h + 128]
+                lanes = slice(128 * h, 128 * h + 128)
+                sides = [
+                    far_ref[:, f, lanes],
+                    pair_ref[0:peers, f, lanes],
+                    pair_ref[peers : 2 * peers, f, lanes],
+                ]
+                rows = jnp.where(first, sides[piece], sides[(piece + 1) % 3])
                 for n in range(2 * h, min(2 * h + 2, count)):
                     for y in range(2):
                         q = 2 * (n % 2) + y
@@ -457,7 +465,7 @@
         pack_out[:, 128 * t : 128 * t + 128] = v
 
 
-def second_call(lo, own, hi):
+def second_call(pair, far):
     big = lambda *s: jax.ShapeDtypeStruct(s + (32, 128), F32)
     vmem = lambda *s: pltpu.VMEM(s + (32, 128), F32)
     return pl.pallas_call(
@@ -465,7 +473,7 @@
         out_shape=[big(8, 7), jax.ShapeDtypeStruct((1, 1408), F32)],
         scratch_shapes=[vmem(3, 5), vmem(3, 5), vmem(3, 4), vmem(7)],
         compiler_params=PARAMS,
-    )(lo, own, hi)
+    )(pair, far)
 
 
 def pack_rows(fields):
@@ -552,7 +560,7 @@
     p_out, q_out, sum_out,
     a_ref, z3_ref, u2_ref, y2_ref, v2_ref, p1_ref, u1_ref, y1_ref, v1_ref, p0_ref, u0_ref, y0_ref,
 ):
-    gx, gy = (lax.axis_index("gx"), lax.axis_index("gy"))
+    gx, gy = (lax.axis_index(GX), lax.axis_index("gy"))
     peers = rows_ref.shape[0]
     answer = coarse_solve(rows_ref)
     for c in range(3):
@@ -728,18 +736,20 @@
             pltpu.VMEM(fixed.shape, jnp.int32),
             pltpu.SemaphoreType.DMA((5,)),
         ],
-        compiler_params=pltpu.CompilerParams(vmem_limit_bytes=60 * 1024 * 1024),
-    )(density, solid, void, fixed, residual)
+        compiler_params=PARAMS,
+    )(*[pltpu.with_memory_space_constraint(v, pltpu.HBM) for v in (density, solid, void, fixed, residual)])
     own = jnp.concatenate([from_peer(packed, "gy", -1), packed, from_peer(packed, "gy", 1)], axis=2)
-    first = first_call(from_peer(own, "gx", -1), own, from_peer(own, "gx", 1))
+    first = first_call(from_peer(own, GX, -1), own, from_peer(own, GX, 1))
     level0, level1, piece = (first[0:4], first[4:8], first[8])
-    columns = spread_all(piece, "gy")
-    second = second_call(
-        from_peer(columns, "gx", -1), columns, from_peer(columns, "gx", 1)
-    )
-    rows = spread_all(second[1].reshape(-1), "gx")
+    columns = spread_all(piece, ("core", "gy"))
+    count = lax.axis_size("gy")
+    own = jnp.where(lax.axis_index("core") == 0, columns[:count], columns[count:])
+    devices = lax.axis_size(GX)
+    meet = [(i, i + 1) for i in range(1, devices - 1, 2)]
+    second = second_call(columns, lax.ppermute(own, GX, meet + [(j, i) for i, j in meet]))
+    rows = spread_all(second[1].reshape(-1), GX)
     precond, image, sums = third_call(rows, second[0], level1, level0)
-    sums = jnp.sum(spread_all(sums[0], "gx"), axis=0)
+    sums = jnp.sum(spread_all(sums[0], GX), axis=0)
     block = jax.ShapeDtypeStruct(residual.shape, F32)
     return tuple(
         pl.pallas_call(last_kernel, out_shape=[block, block], compiler_params=PARAMS)(
@@ -749,16 +759,18 @@
 
 
 def solution(mesh):
+    chips, side = (mesh.devices.shape[0] // 2, mesh.devices.shape[1])
+    split = jax.sharding.Mesh(mesh.devices.reshape(chips, 2, side), ("chip", "core", "gy"))
     return jax.shard_map(
         on_device,
-        mesh=mesh,
+        mesh=split,
         in_specs=(
-            P("gx", "gy", None),
-            P("gx", "gy", None),
-            P("gx", "gy", None),
-            P(None, "gx", "gy", None),
-            P(None, "gx", "gy", None),
+            P(("chip", "core"), "gy", None),
+            P(("chip", "core"), "gy", None),
+            P(("chip", "core"), "gy", None),
+            P(None, ("chip", "core"), "gy", None),
+            P(None, ("chip", "core"), "gy", None),
         ),
-        out_specs=(P(None, "gx", "gy", None), P(None, "gx", "gy", None)),
+        out_specs=(P(None, ("chip", "core"), "gy", None), P(None, ("chip", "core"), "gy", None)),
         check_vma=False,
     )

time: 142 us -> 145 us (1.021)
  blocking collectives: 77.6 us -> 56.6 us
  waiting for transfers between devices: 15.5 us -> 33.9 us
  starting transfers between devices: 28.9 us -> 35 us
    all_to_all x4 -> x3, blocking collectives: 77.6 us -> 56.6 us  [spread_all(): lax.all_to_all(jnp.broadcast_to(row[None], (peers,) + row.shape), axis, 0...]
    all_to_all x0 -> x1, starting transfers between devices: none -> 15 us  [spread_all(): lax.all_to_all(jnp.broadcast_to(row[None], (peers,) + row.shape), axis, 0...]
    all_to_all x0 -> x1, waiting for transfers between devices: none -> 13.9 us  [spread_all(): lax.all_to_all(jnp.broadcast_to(row[None], (peers,) + row.shape), axis, 0...]
    ppermute x6 -> x4, starting transfers between devices: 28.9 us -> 16.9 us  [from_peer(): lax.ppermute(value, axis, [(i + step, i) for i in range(peers) if 0 <= i...]
    ppermute x0 -> x1, starting transfers between devices: none -> 3.17 us  [on_device(): lax.ppermute(own, GX, meet + [(j, i) for i, j in meet])]
    ppermute x0 -> x1, waiting for transfers between devices: none -> 2.76 us  [on_device(): lax.ppermute(own, GX, meet + [(j, i) for i, j in meet])]
    ppermute x6 -> x4, waiting for transfers between devices: 15.5 us -> 17.2 us  [from_peer(): lax.ppermute(value, axis, [(i + step, i) for i in range(peers) if 0 <= i...]
where the time goes in v5:
time: 145 us; the launch traced here: 144 us
  blocking collectives  56.6 us (39%)
  starting transfers between devices  35 us (24%)
  waiting for transfers between devices  33.9 us (23%)
  Pallas kernels  17.1 us (12%)
    all_to_all x3, blocking collectives, spread_all(): lax.all_to_all(jnp.broadcast_to(row[None], (peers,) + row.shape), axis, 0...  56.6 us
    ppermute x4, waiting for transfers between devices, from_peer(): lax.ppermute(value, axis, [(i + step, i) for i in range(peers) if 0 <= i...  17.2 us
    ppermute x4, starting transfers between devices, from_peer(): lax.ppermute(value, axis, [(i + step, i) for i in range(peers) if 0 <= i...  16.9 us
    all_to_all x1, starting transfers between devices, spread_all(): lax.all_to_all(jnp.broadcast_to(row[None], (peers,) + row.shape), axis, 0...  15 us
    all_to_all x1, waiting for transfers between devices, spread_all(): lax.all_to_all(jnp.broadcast_to(row[None], (peers,) + row.shape), axis, 0...  13.9 us
    pallas_call x1, Pallas kernels, third_call(): pl.pallas_call(third_kernel, out_shape=[own, own, jax.ShapeDtypeStruct((8...  9.11 us
    pallas_call x1, Pallas kernels, first_call(): pl.pallas_call(first_kernel, out_shape=[big(12), big(12), big(3, 12), big...  4.98 us
    ppermute x1, starting transfers between devices, on_device(): lax.ppermute(own, GX, meet + [(j, i) for i, j in meet])  3.17 us
  transfers between devices with their start and end apart: 6, of which 6 were waited for; matrix products, arithmetic and copies ran while one was open for 0% of the time, Pallas kernels for 0%

profile of v5, /device:TPU:1, one launch (start us, length us, event | category | flops | bytes accessed | tf_op | source)
XLA Modules:
  0.0 144.5 jit_solution(16400135270351739318)
XLA Ops:
  0.6 1.0 shard_map.68.packed_ref
  1.7 4.8 %collective-permute-start = (f32[9,8,8,128]{3,2,1,0:T(8,128)S(1)}, f32[9,8,8,128]{3,2,1,0:T(8,128)S(1)}, u32[]{:S(2)}, u32[]{:S(2)}) collective-permute-start(f32[9,8,8,128]{3,2,1,0:T(8,128)S(1)} %shard_map.68.packed_ref), channel_id=1, source_target_pairs={{0,1},{1,2},{2,3},{3,4},{4,5},{5,6},{6,7},{7,8},{8,9},{9,10},{10,1... | collective-permute-start | bytes 884744 | tf_op jit(solution)/shard_map/ppermute | solution.py:719
  6.5 1.3 collective-permute-start.1
  7.8 2.3 %collective-permute-done = f32[9,8,8,128]{3,2,1,0:T(8,128)S(1)} collective-permute-done((f32[9,8,8,128]{3,2,1,0:T(8,128)S(1)}, f32[9,8,8,128]{3,2,1,0:T(8,128)S(1)}, u32[]{:S(2)}, u32[]{:S(2)}) %collective-permute-start) | collective-permute-done | bytes 294944 | tf_op jit(solution)/shard_map/ppermute | solution.py:719
  10.2 4.5 %collective-permute-done.1 = f32[9,8,8,128]{3,2,1,0:T(8,128)S(1)} collective-permute-done((f32[9,8,8,128]{3,2,1,0:T(8,128)S(1)}, f32[9,8,8,128]{3,2,1,0:T(8,128)S(1)}, u32[]{:S(2)}, u32[]{:S(2)}) %collective-permute-start.1) | collective-permute-done | bytes 294944 | tf_op jit(solution)/shard_map/ppermute | solution.py:719
  14.6 0.1 pad_maximum_fusion.own_ref
  14.7 6.9 %collective-permute-start.2 = (f32[9,8,24,128]{3,2,1,0:T(8,128)S(1)}, f32[9,8,24,128]{3,2,1,0:T(8,128)S(1)}, u32[]{:S(2)}, u32[]{:S(2)}) collective-permute-start(f32[9,8,24,128]{3,2,1,0:T(8,128)S(1)} %pad_maximum_fusion.own_ref), channel_id=1, source_target_pairs={{0,12},{12,24},{24,36},{36,48},{48,60},{60,72},{72,84},{84,96},{96... | collective-permute-start | bytes 2654216 | tf_op jit(solution)/shard_map/ppermute | solution.py:719
  21.6 3.9 %collective-permute-start.3 = (f32[9,8,24,128]{3,2,1,0:T(8,128)S(1)}, f32[9,8,24,128]{3,2,1,0:T(8,128)S(1)}, u32[]{:S(2)}, u32[]{:S(2)}) collective-permute-start(f32[9,8,24,128]{3,2,1,0:T(8,128)S(1)} %pad_maximum_fusion.own_ref), channel_id=1, source_target_pairs={{12,0},{24,12},{36,24},{48,36},{60,48},{72,60},{84,72},{96,84},{10... | collective-permute-start | bytes 2654216 | tf_op jit(solution)/shard_map/ppermute | solution.py:719
  25.5 6.1 %collective-permute-done.2.lo_ref = f32[9,8,24,128]{3,2,1,0:T(8,128)S(1)} collective-permute-done((f32[9,8,24,128]{3,2,1,0:T(8,128)S(1)}, f32[9,8,24,128]{3,2,1,0:T(8,128)S(1)}, u32[]{:S(2)}, u32[]{:S(2)}) %collective-permute-start.2) | collective-permute-done | bytes 884768 | tf_op jit(solution)/shard_map/ppermute | solution.py:719
  31.5 4.4 %collective-permute-done.3.hi_ref = f32[9,8,24,128]{3,2,1,0:T(8,128)S(1)} collective-permute-done((f32[9,8,24,128]{3,2,1,0:T(8,128)S(1)}, f32[9,8,24,128]{3,2,1,0:T(8,128)S(1)}, u32[]{:S(2)}, u32[]{:S(2)}) %collective-permute-start.3) | collective-permute-done | bytes 884768 | tf_op jit(solution)/shard_map/ppermute | solution.py:719
  35.9 5.0 %shard_map.69 = (f32[12,16,128]{2,1,0:T(8,128)S(1)}, f32[12,16,128]{2,1,0:T(8,128)S(1)}, f32[3,12,16,128]{3,2,1,0:T(8,128)S(1)}, f32[3,12,16,128]{3,2,1,0:T(8,12...) custom-call(f32[9,8,24,128]{3,2,1,0:T(8,128)S(1)} %collective-permut, ...), custom_call_target="tpu_custom_call" | custom-call | tf_op jit(solution)/shard_map/pallas_call | solution.py:387
  40.9 0.7 broadcast_in_dim.8
  41.6 15.0 %all-to-all-start = ((f32[24,8,256]{2,1,0:T(8,128)}), f32[24,8,256]{2,1,0:T(8,128)S(1)}, u32[]{:S(2)}, u32[]{:S(2)}) async-start(f32[24,8,256]{2,1,0:T(8,128)} %broadcast_in_dim.8), calls=%async_computation | async-start | bytes 393216 | tf_op jit(solution)/shard_map/all_to_all | solution.py:724
  56.6 13.9 %all-to-all-done.pair_ref = f32[24,8,256]{2,1,0:T(8,128)S(1)} async-done(((f32[24,8,256]{2,1,0:T(8,128)}), f32[24,8,256]{2,1,0:T(8,128)S(1)}, u32[]{:S(2)}, u32[]{:S(2)}) %all-to-all-start) | async-done | bytes 196640 | tf_op jit(solution)/shard_map/all_to_all | solution.py:724
  70.5 3.2 %collective-permute-start.4 = (f32[12,8,256]{2,1,0:T(8,128)S(1)}, f32[12,8,256]{2,1,0:T(8,128)S(1)}, u32[]{:S(2)}, u32[]{:S(2)}) collective-permute-start(f32[12,8,256]{2,1,0:T(8,128)S(1)} %slice_select_fusion), channel_id=1, source_target_pairs={{12,24},{36,48},{60,72},{84,96},{108,120},{132,144},{156,168},{180... | collective-permute-start | bytes 294920 | tf_op jit(solution)/shard_map/ppermute | solution.py:749
  73.7 2.8 %collective-permute-done.4.far_ref = f32[12,8,256]{2,1,0:T(8,128)S(1)} collective-permute-done((f32[12,8,256]{2,1,0:T(8,128)S(1)}, f32[12,8,256]{2,1,0:T(8,128)S(1)}, u32[]{:S(2)}, u32[]{:S(2)}) %collective-permute-start.4) | collective-permute-done | bytes 98336 | tf_op jit(solution)/shard_map/ppermute | solution.py:749
  76.5 1.2 shard_map.70
  77.7 0.2 broadcast_in_dim.9
  77.8 29.9 %all_to_all.27 = f32[64,1,1408]{2,1,0:T(1,128)S(1)} all-to-all(f32[64,1,1408]{2,1,0:T(1,128)S(1)} %broadcast_in_dim.9), channel_id=1, replica_groups=mesh['chip'=32,'core'=2,'gy'=12] {'chip','core'}, dimensions={0} | all-to-all | bytes 720896 | tf_op jit(solution)/shard_map/all_to_all | solution.py:724
  107.8 9.1 %shard_map.71 = (f32[3,8,8,128]{3,2,1,0:T(8,128)S(1)}, f32[3,8,8,128]{3,2,1,0:T(8,128)S(1)}, f32[8,128]{1,0:T(8,128)S(1)}) custom-call(f32[64,1408]{1,0:T(8,128)S(1)} %bitcast.9, f32[8,7,32,128]{3,2,1,0:T(8,128)S(1)} %get-tuple-element.18.l2_ref, f32[9,16,128]{2,1,0:T(8,128)S(1)} %get-tuple-element.19.m1_ref, f32[9,16,128]{2,1,0:T(8,128)S(1)} %get-tuple-element.20.i1_ref, ...), custom_call_target="tpu_custom_call" | custom-call | tf_op jit(solution)/shard_map/pallas_call | solution.py:668
  116.9 14.6 %all_to_all.28 = f32[64,1,128]{2,1,0:T(1,128)S(1)} all-to-all(f32[64,1,128]{2,1,0:T(1,128)S(1)} %broadcast_in_dim.10), channel_id=1, replica_groups=mesh['chip'=32,'core'=2,'gy'=12] {'chip','core'}, dimensions={0} | all-to-all | bytes 65536 | tf_op jit(solution)/shard_map/all_to_all | solution.py:724
  131.6 12.1 %all_to_all.29 = f32[12,1,128]{2,1,0:T(1,128)S(1)} all-to-all(f32[12,1,128]{2,1,0:T(1,128)S(1)} %broadcast_in_dim.11), channel_id=1, replica_groups=mesh['chip'=32,'core'=2,'gy'=12] {'gy'}, dimensions={0} | all-to-all | bytes 12288 | tf_op jit(solution)/shard_map/all_to_all | solution.py:724
  143.7 0.8 shard_map.72
  (8 shorter events, 0.1 us)
Async XLA Ops:
  1.7 8.5 %collective-permute-start = (f32[9,8,8,128]{3,2,1,0:T(8,128)S(1)}, f32[9,8,8,128]{3,2,1,0:T(8,128)S(1)}, u32[]{:S(2)}, u32[]{:S(2)}) collective-permute-start(f32[9,8,8,128]{3,2,1,0:T(8,128)S(1)} %shard_map.68.packed_ref), channel_id=1, source_target_pairs={{0,1},{1,2},{2,3},{3,4},{4,5},{5,6},{6,7},{7,8},{8,9},{9,10},{10,1... | collective-permute-start | bytes 884744 | tf_op jit(solution)/shard_map/ppermute | solution.py:719
  6.5 8.1 %collective-permute-start.1 = (f32[9,8,8,128]{3,2,1,0:T(8,128)S(1)}, f32[9,8,8,128]{3,2,1,0:T(8,128)S(1)}, u32[]{:S(2)}, u32[]{:S(2)}) collective-permute-start(f32[9,8,8,128]{3,2,1,0:T(8,128)S(1)} %shard_map.68.packed_ref), channel_id=1, source_target_pairs={{1,0},{2,1},{3,2},{4,3},{5,4},{6,5},{7,6},{8,7},{9,8},{10,9},{11,1... | collective-permute-start | bytes 884744 | tf_op jit(solution)/shard_map/ppermute | solution.py:719
  14.7 16.8 %collective-permute-start.2 = (f32[9,8,24,128]{3,2,1,0:T(8,128)S(1)}, f32[9,8,24,128]{3,2,1,0:T(8,128)S(1)}, u32[]{:S(2)}, u32[]{:S(2)}) collective-permute-start(f32[9,8,24,128]{3,2,1,0:T(8,128)S(1)} %pad_maximum_fusion.own_ref), channel_id=1, source_target_pairs={{0,12},{12,24},{24,36},{36,48},{48,60},{60,72},{72,84},{84,96},{96... | collective-permute-start | bytes 2654216 | tf_op jit(solution)/shard_map/ppermute | solution.py:719
  21.6 14.4 %collective-permute-start.3 = (f32[9,8,24,128]{3,2,1,0:T(8,128)S(1)}, f32[9,8,24,128]{3,2,1,0:T(8,128)S(1)}, u32[]{:S(2)}, u32[]{:S(2)}) collective-permute-start(f32[9,8,24,128]{3,2,1,0:T(8,128)S(1)} %pad_maximum_fusion.own_ref), channel_id=1, source_target_pairs={{12,0},{24,12},{36,24},{48,36},{60,48},{72,60},{84,72},{96,84},{10... | collective-permute-start | bytes 2654216 | tf_op jit(solution)/shard_map/ppermute | solution.py:719
  41.6 28.9 %all-to-all-start = ((f32[24,8,256]{2,1,0:T(8,128)}), f32[24,8,256]{2,1,0:T(8,128)S(1)}, u32[]{:S(2)}, u32[]{:S(2)}) async-start(f32[24,8,256]{2,1,0:T(8,128)} %broadcast_in_dim.8), calls=%async_computation | async-start | bytes 393216 | tf_op jit(solution)/shard_map/all_to_all | solution.py:724
  70.5 5.9 %collective-permute-start.4 = (f32[12,8,256]{2,1,0:T(8,128)S(1)}, f32[12,8,256]{2,1,0:T(8,128)S(1)}, u32[]{:S(2)}, u32[]{:S(2)}) collective-permute-start(f32[12,8,256]{2,1,0:T(8,128)S(1)} %slice_select_fusion), channel_id=1, source_target_pairs={{12,24},{36,48},{60,72},{84,96},{108,120},{132,144},{156,168},{180... | collective-permute-start | bytes 294920 | tf_op jit(solution)/shard_map/ppermute | solution.py:749

commit v6 on v5

--- a/solution.py
+++ b/solution.py
@@ -706,6 +706,11 @@
     copies[4].wait()
 
 
+def own_kernel(pair_ref, out_ref):
+    count = out_ref.shape[0]
+    out_ref[...] = jnp.where(lax.axis_index("core") == 0, pair_ref[:count], pair_ref[count:])
+
+
 def last_kernel(sums_ref, precond_ref, image_ref, packed_ref, update_ref, next_ref):
     total = jnp.sum(sums_ref[...], axis=0, keepdims=True)
     alpha = total[:, 0:1] / total[:, 1:2]
@@ -742,11 +747,11 @@
     first = first_call(from_peer(own, GX, -1), own, from_peer(own, GX, 1))
     level0, level1, piece = (first[0:4], first[4:8], first[8])
     columns = spread_all(piece, ("core", "gy"))
-    count = lax.axis_size("gy")
-    own = jnp.where(lax.axis_index("core") == 0, columns[:count], columns[count:])
+    half = jax.ShapeDtypeStruct((lax.axis_size("gy"),) + piece.shape, F32)
+    columns_own = pl.pallas_call(own_kernel, out_shape=half, compiler_params=PARAMS)(columns)
     devices = lax.axis_size(GX)
     meet = [(i, i + 1) for i in range(1, devices - 1, 2)]
-    second = second_call(columns, lax.ppermute(own, GX, meet + [(j, i) for i, j in meet]))
+    second = second_call(columns, lax.ppermute(columns_own, GX, meet + [(j, i) for i, j in meet]))
     rows = spread_all(second[1].reshape(-1), GX)
     precond, image, sums = third_call(rows, second[0], level1, level0)
     sums = jnp.sum(spread_all(sums[0], GX), axis=0)

time: 145 us -> 142 us (0.979)
  blocking collectives: 56.6 us -> 82.1 us
  waiting for transfers between devices: 33.9 us -> 15.9 us
  starting transfers between devices: 35 us -> 25.2 us
    all_to_all x3 -> x4, blocking collectives: 56.6 us -> 82.1 us  [spread_all(): lax.all_to_all(jnp.broadcast_to(row[None], (peers,) + row.shape), axis, 0...]
    all_to_all x1 -> x0, starting transfers between devices: 15 us -> none  [spread_all(): lax.all_to_all(jnp.broadcast_to(row[None], (peers,) + row.shape), axis, 0...]
    all_to_all x1 -> x0, waiting for transfers between devices: 13.9 us -> none  [spread_all(): lax.all_to_all(jnp.broadcast_to(row[None], (peers,) + row.shape), axis, 0...]
    ppermute x4, starting transfers between devices: 16.9 us -> 20.8 us  [from_peer(): lax.ppermute(value, axis, [(i + step, i) for i in range(peers) if 0 <= i...]
    ppermute x4, waiting for transfers between devices: 17.2 us -> 13.6 us  [from_peer(): lax.ppermute(value, axis, [(i + step, i) for i in range(peers) if 0 <= i...]
  transfers between devices with their start and end apart: 6 -> 5, of which waited for: 6 -> 5; matrix products, arithmetic and copies ran while one was open for 0% -> 0% of each run, Pallas kernels for 0% -> 0%
where the time goes in v6:
time: 142 us; the launch traced here: 141 us
  blocking collectives  82.1 us (58%)
  starting transfers between devices  25.2 us (18%)
  Pallas kernels  17.2 us (12%)
  waiting for transfers between devices  15.9 us (11%)
    all_to_all x4, blocking collectives, spread_all(): lax.all_to_all(jnp.broadcast_to(row[None], (peers,) + row.shape), axis, 0...  82.1 us
    ppermute x4, starting transfers between devices, from_peer(): lax.ppermute(value, axis, [(i + step, i) for i in range(peers) if 0 <= i...  20.8 us
    ppermute x4, waiting for transfers between devices, from_peer(): lax.ppermute(value, axis, [(i + step, i) for i in range(peers) if 0 <= i...  13.6 us
    pallas_call x1, Pallas kernels, third_call(): pl.pallas_call(third_kernel, out_shape=[own, own, jax.ShapeDtypeStruct((8...  9.11 us
    pallas_call x1, Pallas kernels, first_call(): pl.pallas_call(first_kernel, out_shape=[big(12), big(12), big(3, 12), big...  4.98 us
    ppermute x1, starting transfers between devices, on_device(): lax.ppermute(columns_own, GX, meet + [(j, i) for i, j in meet])  4.44 us
  transfers between devices with their start and end apart: 5, of which 5 were waited for; matrix products, arithmetic and copies ran while one was open for 0% of the time, Pallas kernels for 0%

profile of v6, /device:TPU:1, one launch (start us, length us, event | category | flops | bytes accessed | tf_op | source)
XLA Modules:
  0.0 141.5 jit_solution(15217053214092698200)
XLA Ops:
  0.6 1.0 shard_map.68.packed_ref
  1.7 1.3 collective-permute-start.1
  3.0 5.5 %collective-permute-start = (f32[9,8,8,128]{3,2,1,0:T(8,128)S(1)}, f32[9,8,8,128]{3,2,1,0:T(8,128)S(1)}, u32[]{:S(2)}, u32[]{:S(2)}) collective-permute-start(f32[9,8,8,128]{3,2,1,0:T(8,128)S(1)} %shard_map.68.packed_ref), channel_id=1, source_target_pairs={{0,1},{1,2},{2,3},{3,4},{4,5},{5,6},{6,7},{7,8},{8,9},{9,10},{10,1... | collective-permute-start | bytes 884744 | tf_op jit(solution)/shard_map/ppermute | solution.py:724
  8.5 2.2 %collective-permute-done.1 = f32[9,8,8,128]{3,2,1,0:T(8,128)S(1)} collective-permute-done((f32[9,8,8,128]{3,2,1,0:T(8,128)S(1)}, f32[9,8,8,128]{3,2,1,0:T(8,128)S(1)}, u32[]{:S(2)}, u32[]{:S(2)}) %collective-permute-start.1) | collective-permute-done | bytes 294944 | tf_op jit(solution)/shard_map/ppermute | solution.py:724
  10.6 1.5 %collective-permute-done = f32[9,8,8,128]{3,2,1,0:T(8,128)S(1)} collective-permute-done((f32[9,8,8,128]{3,2,1,0:T(8,128)S(1)}, f32[9,8,8,128]{3,2,1,0:T(8,128)S(1)}, u32[]{:S(2)}, u32[]{:S(2)}) %collective-permute-start) | collective-permute-done | bytes 294944 | tf_op jit(solution)/shard_map/ppermute | solution.py:724
  12.1 0.1 pad_maximum_fusion.own_ref
  12.2 12.1 %collective-permute-start.3 = (f32[9,8,24,128]{3,2,1,0:T(8,128)S(1)}, f32[9,8,24,128]{3,2,1,0:T(8,128)S(1)}, u32[]{:S(2)}, u32[]{:S(2)}) collective-permute-start(f32[9,8,24,128]{3,2,1,0:T(8,128)S(1)} %pad_maximum_fusion.own_ref), channel_id=1, source_target_pairs={{12,0},{24,12},{36,24},{48,36},{60,48},{72,60},{84,72},{96,84},{10... | collective-permute-start | bytes 2654216 | tf_op jit(solution)/shard_map/ppermute | solution.py:724
  24.3 1.9 %collective-permute-start.2 = (f32[9,8,24,128]{3,2,1,0:T(8,128)S(1)}, f32[9,8,24,128]{3,2,1,0:T(8,128)S(1)}, u32[]{:S(2)}, u32[]{:S(2)}) collective-permute-start(f32[9,8,24,128]{3,2,1,0:T(8,128)S(1)} %pad_maximum_fusion.own_ref), channel_id=1, source_target_pairs={{0,12},{12,24},{24,36},{36,48},{48,60},{60,72},{72,84},{84,96},{96... | collective-permute-start | bytes 2654216 | tf_op jit(solution)/shard_map/ppermute | solution.py:724
  26.2 3.3 %collective-permute-done.3.hi_ref = f32[9,8,24,128]{3,2,1,0:T(8,128)S(1)} collective-permute-done((f32[9,8,24,128]{3,2,1,0:T(8,128)S(1)}, f32[9,8,24,128]{3,2,1,0:T(8,128)S(1)}, u32[]{:S(2)}, u32[]{:S(2)}) %collective-permute-start.3) | collective-permute-done | bytes 884768 | tf_op jit(solution)/shard_map/ppermute | solution.py:724
  29.4 6.7 %collective-permute-done.2.lo_ref = f32[9,8,24,128]{3,2,1,0:T(8,128)S(1)} collective-permute-done((f32[9,8,24,128]{3,2,1,0:T(8,128)S(1)}, f32[9,8,24,128]{3,2,1,0:T(8,128)S(1)}, u32[]{:S(2)}, u32[]{:S(2)}) %collective-permute-start.2) | collective-permute-done | bytes 884768 | tf_op jit(solution)/shard_map/ppermute | solution.py:724
  36.1 5.0 %shard_map.69 = (f32[12,16,128]{2,1,0:T(8,128)S(1)}, f32[12,16,128]{2,1,0:T(8,128)S(1)}, f32[3,12,16,128]{3,2,1,0:T(8,128)S(1)}, f32[3,12,16,128]{3,2,1,0:T(8,12...) custom-call(f32[9,8,24,128]{3,2,1,0:T(8,128)S(1)} %collective-permut, ...), custom_call_target="tpu_custom_call" | custom-call | tf_op jit(solution)/shard_map/pallas_call | solution.py:387
  41.2 25.1 %all_to_all.27.pair_ref = f32[24,8,256]{2,1,0:T(8,128)S(1)} all-to-all(f32[24,8,256]{2,1,0:T(8,128)S(1)} %broadcast_in_dim.8), channel_id=1, replica_groups=mesh['chip'=32,'core'=2,'gy'=12] {'core','gy'}, dimensions={0} | all-to-all | bytes 393216 | tf_op jit(solution)/shard_map/all_to_all | solution.py:729
  66.3 4.4 %collective-permute-start.4 = (f32[12,8,256]{2,1,0:T(8,128)S(1)}, f32[12,8,256]{2,1,0:T(8,128)S(1)}, u32[]{:S(2)}, u32[]{:S(2)}) collective-permute-start(f32[12,8,256]{2,1,0:T(8,128)S(1)} %shard_map.70), channel_id=1, source_target_pairs={{12,24},{36,48},{60,72},{84,96},{108,120},{132,144},{156,168},{180... | collective-permute-start | bytes 294920 | tf_op jit(solution)/shard_map/ppermute | solution.py:754
  70.7 2.3 %collective-permute-done.4.far_ref = f32[12,8,256]{2,1,0:T(8,128)S(1)} collective-permute-done((f32[12,8,256]{2,1,0:T(8,128)S(1)}, f32[12,8,256]{2,1,0:T(8,128)S(1)}, u32[]{:S(2)}, u32[]{:S(2)}) %collective-permute-start.4) | collective-permute-done | bytes 98336 | tf_op jit(solution)/shard_map/ppermute | solution.py:754
  73.0 1.2 shard_map.71
  74.2 0.2 broadcast_in_dim.9
  74.4 30.1 %all_to_all.28 = f32[64,1,1408]{2,1,0:T(1,128)S(1)} all-to-all(f32[64,1,1408]{2,1,0:T(1,128)S(1)} %broadcast_in_dim.9), channel_id=1, replica_groups=mesh['chip'=32,'core'=2,'gy'=12] {'chip','core'}, dimensions={0} | all-to-all | bytes 720896 | tf_op jit(solution)/shard_map/all_to_all | solution.py:729
  104.6 9.1 %shard_map.72 = (f32[3,8,8,128]{3,2,1,0:T(8,128)S(1)}, f32[3,8,8,128]{3,2,1,0:T(8,128)S(1)}, f32[8,128]{1,0:T(8,128)S(1)}) custom-call(f32[64,1408]{1,0:T(8,128)S(1)} %bitcast.9, f32[8,7,32,128]{3,2,1,0:T(8,128)S(1)} %get-tuple-element.18.l2_ref, f32[9,16,128]{2,1,0:T(8,128)S(1)} %get-tuple-element.19.m1_ref, f32[9,16,128]{2,1,0:T(8,128)S(1)} %get-tuple-element.20.i1_ref, ...), custom_call_target="tpu_custom_call" | custom-call | tf_op jit(solution)/shard_map/pallas_call | solution.py:668
  113.7 14.6 %all_to_all.29 = f32[64,1,128]{2,1,0:T(1,128)S(1)} all-to-all(f32[64,1,128]{2,1,0:T(1,128)S(1)} %broadcast_in_dim.10), channel_id=1, replica_groups=mesh['chip'=32,'core'=2,'gy'=12] {'chip','core'}, dimensions={0} | all-to-all | bytes 65536 | tf_op jit(solution)/shard_map/all_to_all | solution.py:729
  128.4 12.3 %all_to_all.30 = f32[12,1,128]{2,1,0:T(1,128)S(1)} all-to-all(f32[12,1,128]{2,1,0:T(1,128)S(1)} %broadcast_in_dim.11), channel_id=1, replica_groups=mesh['chip'=32,'core'=2,'gy'=12] {'gy'}, dimensions={0} | all-to-all | bytes 12288 | tf_op jit(solution)/shard_map/all_to_all | solution.py:729
  140.7 0.8 shard_map.73
  (9 shorter events, 0.1 us)
Async XLA Ops:
  1.7 8.9 %collective-permute-start.1 = (f32[9,8,8,128]{3,2,1,0:T(8,128)S(1)}, f32[9,8,8,128]{3,2,1,0:T(8,128)S(1)}, u32[]{:S(2)}, u32[]{:S(2)}) collective-permute-start(f32[9,8,8,128]{3,2,1,0:T(8,128)S(1)} %shard_map.68.packed_ref), channel_id=1, source_target_pairs={{1,0},{2,1},{3,2},{4,3},{5,4},{6,5},{7,6},{8,7},{9,8},{10,9},{11,1... | collective-permute-start | bytes 884744 | tf_op jit(solution)/shard_map/ppermute | solution.py:724
  3.0 9.1 %collective-permute-start = (f32[9,8,8,128]{3,2,1,0:T(8,128)S(1)}, f32[9,8,8,128]{3,2,1,0:T(8,128)S(1)}, u32[]{:S(2)}, u32[]{:S(2)}) collective-permute-start(f32[9,8,8,128]{3,2,1,0:T(8,128)S(1)} %shard_map.68.packed_ref), channel_id=1, source_target_pairs={{0,1},{1,2},{2,3},{3,4},{4,5},{5,6},{6,7},{7,8},{8,9},{9,10},{10,1... | collective-permute-start | bytes 884744 | tf_op jit(solution)/shard_map/ppermute | solution.py:724
  12.2 17.3 %collective-permute-start.3 = (f32[9,8,24,128]{3,2,1,0:T(8,128)S(1)}, f32[9,8,24,128]{3,2,1,0:T(8,128)S(1)}, u32[]{:S(2)}, u32[]{:S(2)}) collective-permute-start(f32[9,8,24,128]{3,2,1,0:T(8,128)S(1)} %pad_maximum_fusion.own_ref), channel_id=1, source_target_pairs={{12,0},{24,12},{36,24},{48,36},{60,48},{72,60},{84,72},{96,84},{10... | collective-permute-start | bytes 2654216 | tf_op jit(solution)/shard_map/ppermute | solution.py:724
  24.3 11.9 %collective-permute-start.2 = (f32[9,8,24,128]{3,2,1,0:T(8,128)S(1)}, f32[9,8,24,128]{3,2,1,0:T(8,128)S(1)}, u32[]{:S(2)}, u32[]{:S(2)}) collective-permute-start(f32[9,8,24,128]{3,2,1,0:T(8,128)S(1)} %pad_maximum_fusion.own_ref), channel_id=1, source_target_pairs={{0,12},{12,24},{24,36},{36,48},{48,60},{60,72},{72,84},{84,96},{96... | collective-permute-start | bytes 2654216 | tf_op jit(solution)/shard_map/ppermute | solution.py:724
  66.3 6.7 %collective-permute-start.4 = (f32[12,8,256]{2,1,0:T(8,128)S(1)}, f32[12,8,256]{2,1,0:T(8,128)S(1)}, u32[]{:S(2)}, u32[]{:S(2)}) collective-permute-start(f32[12,8,256]{2,1,0:T(8,128)S(1)} %shard_map.70), channel_id=1, source_target_pairs={{12,24},{36,48},{60,72},{84,96},{108,120},{132,144},{156,168},{180... | collective-permute-start | bytes 294920 | tf_op jit(solution)/shard_map/ppermute | solution.py:754

commit v7 on v4

--- a/solution.py
+++ b/solution.py
@@ -728,8 +728,8 @@
             pltpu.VMEM(fixed.shape, jnp.int32),
             pltpu.SemaphoreType.DMA((5,)),
         ],
-        compiler_params=pltpu.CompilerParams(vmem_limit_bytes=60 * 1024 * 1024),
-    )(density, solid, void, fixed, residual)
+        compiler_params=PARAMS,
+    )(*[pltpu.with_memory_space_constraint(v, pltpu.HBM) for v in (density, solid, void, fixed, residual)])
     own = jnp.concatenate([from_peer(packed, "gy", -1), packed, from_peer(packed, "gy", 1)], axis=2)
     first = first_call(from_peer(own, "gx", -1), own, from_peer(own, "gx", 1))
     level0, level1, piece = (first[0:4], first[4:8], first[8])

time: 142 us -> 140 us (0.986)
  no operation moved by 1% of the time
where the time goes in v7:
time: 140 us
  blocking collectives  77.7 us (56%)
  starting transfers between devices  28.9 us (21%)
  Pallas kernels  17.1 us (12%)
  waiting for transfers between devices  15.2 us (11%)
    all_to_all x4, blocking collectives, spread_all(): lax.all_to_all(jnp.broadcast_to(row[None], (peers,) + row.shape), axis, 0...  77.7 us
    ppermute x6, starting transfers between devices, from_peer(): lax.ppermute(value, axis, [(i + step, i) for i in range(peers) if 0 <= i...  28.9 us
    ppermute x6, waiting for transfers between devices, from_peer(): lax.ppermute(value, axis, [(i + step, i) for i in range(peers) if 0 <= i...  15.2 us
    pallas_call x1, Pallas kernels, third_call(): pl.pallas_call(third_kernel, out_shape=[own, own, jax.ShapeDtypeStruct((8...  9.11 us
    pallas_call x1, Pallas kernels, first_call(): pl.pallas_call(first_kernel, out_shape=[big(12), big(12), big(3, 12), big...  4.99 us
  transfers between devices with their start and end apart: 6, of which 6 were waited for; matrix products, arithmetic and copies ran while one was open for 0% of the time, Pallas kernels for 0%

profile of v7, /device:TPU:1, one launch (start us, length us, event | category | flops | bytes accessed | tf_op | source)
XLA Modules:
  0.0 139.9 jit_solution(15867237958303602369)
XLA Ops:
  0.6 1.0 shard_map.68.packed_ref
  1.7 1.3 collective-permute-start.1
  3.0 5.5 %collective-permute-start = (f32[9,8,8,128]{3,2,1,0:T(8,128)S(1)}, f32[9,8,8,128]{3,2,1,0:T(8,128)S(1)}, u32[]{:S(2)}, u32[]{:S(2)}) collective-permute-start(f32[9,8,8,128]{3,2,1,0:T(8,128)S(1)} %shard_map.68.packed_ref), channel_id=1, source_target_pairs={{0,1},{1,2},{2,3},{3,4},{4,5},{5,6},{6,7},{7,8},{8,9},{9,10},{10,1... | collective-permute-start | bytes 884744 | tf_op jit(solution)/shard_map/ppermute | solution.py:711
  8.5 2.2 %collective-permute-done.1 = f32[9,8,8,128]{3,2,1,0:T(8,128)S(1)} collective-permute-done((f32[9,8,8,128]{3,2,1,0:T(8,128)S(1)}, f32[9,8,8,128]{3,2,1,0:T(8,128)S(1)}, u32[]{:S(2)}, u32[]{:S(2)}) %collective-permute-start.1) | collective-permute-done | bytes 294944 | tf_op jit(solution)/shard_map/ppermute | solution.py:711
  10.6 1.5 %collective-permute-done = f32[9,8,8,128]{3,2,1,0:T(8,128)S(1)} collective-permute-done((f32[9,8,8,128]{3,2,1,0:T(8,128)S(1)}, f32[9,8,8,128]{3,2,1,0:T(8,128)S(1)}, u32[]{:S(2)}, u32[]{:S(2)}) %collective-permute-start) | collective-permute-done | bytes 294944 | tf_op jit(solution)/shard_map/ppermute | solution.py:711
  12.1 0.1 pad_maximum_fusion.own_ref
  12.2 12.1 %collective-permute-start.3 = (f32[9,8,24,128]{3,2,1,0:T(8,128)S(1)}, f32[9,8,24,128]{3,2,1,0:T(8,128)S(1)}, u32[]{:S(2)}, u32[]{:S(2)}) collective-permute-start(f32[9,8,24,128]{3,2,1,0:T(8,128)S(1)} %pad_maximum_fusion.own_ref), channel_id=1, source_target_pairs={{12,0},{24,12},{36,24},{48,36},{60,48},{72,60},{84,72},{96,84},{10... | collective-permute-start | bytes 2654216 | tf_op jit(solution)/shard_map/ppermute | solution.py:711
  24.3 1.9 %collective-permute-start.2 = (f32[9,8,24,128]{3,2,1,0:T(8,128)S(1)}, f32[9,8,24,128]{3,2,1,0:T(8,128)S(1)}, u32[]{:S(2)}, u32[]{:S(2)}) collective-permute-start(f32[9,8,24,128]{3,2,1,0:T(8,128)S(1)} %pad_maximum_fusion.own_ref), channel_id=1, source_target_pairs={{0,12},{12,24},{24,36},{36,48},{48,60},{60,72},{72,84},{84,96},{96... | collective-permute-start | bytes 2654216 | tf_op jit(solution)/shard_map/ppermute | solution.py:711
  26.2 3.3 %collective-permute-done.3.hi_ref = f32[9,8,24,128]{3,2,1,0:T(8,128)S(1)} collective-permute-done((f32[9,8,24,128]{3,2,1,0:T(8,128)S(1)}, f32[9,8,24,128]{3,2,1,0:T(8,128)S(1)}, u32[]{:S(2)}, u32[]{:S(2)}) %collective-permute-start.3) | collective-permute-done | bytes 884768 | tf_op jit(solution)/shard_map/ppermute | solution.py:711
  29.4 6.7 %collective-permute-done.2.lo_ref = f32[9,8,24,128]{3,2,1,0:T(8,128)S(1)} collective-permute-done((f32[9,8,24,128]{3,2,1,0:T(8,128)S(1)}, f32[9,8,24,128]{3,2,1,0:T(8,128)S(1)}, u32[]{:S(2)}, u32[]{:S(2)}) %collective-permute-start.2) | collective-permute-done | bytes 884768 | tf_op jit(solution)/shard_map/ppermute | solution.py:711
  36.1 5.0 %shard_map.69 = (f32[12,16,128]{2,1,0:T(8,128)S(1)}, f32[12,16,128]{2,1,0:T(8,128)S(1)}, f32[3,12,16,128]{3,2,1,0:T(8,128)S(1)}, f32[3,12,16,128]{3,2,1,0:T(8,12...) custom-call(f32[9,8,24,128]{3,2,1,0:T(8,128)S(1)} %collective-permut, ...), custom_call_target="tpu_custom_call" | custom-call | tf_op jit(solution)/shard_map/pallas_call | solution.py:386
  41.2 20.9 %all_to_all.27.own_ref = f32[12,8,256]{2,1,0:T(8,128)S(1)} all-to-all(f32[12,8,256]{2,1,0:T(8,128)S(1)} %broadcast_in_dim.8), channel_id=1, replica_groups=mesh['gx'=64,'gy'=12] {'gy'}, dimensions={0} | all-to-all | bytes 196608 | tf_op jit(solution)/shard_map/all_to_all | solution.py:716
  62.0 1.9 %collective-permute-start.5 = (f32[12,8,256]{2,1,0:T(8,128)S(1)}, f32[12,8,256]{2,1,0:T(8,128)S(1)}, u32[]{:S(2)}, u32[]{:S(2)}) collective-permute-start(f32[12,8,256]{2,1,0:T(8,128)S(1)} %all_to_all.27.own_ref), channel_id=1, source_target_pairs={{12,0},{24,12},{36,24},{48,36},{60,48},{72,60},{84,72},{96,84},{10... | collective-permute-start | bytes 294920 | tf_op jit(solution)/shard_map/ppermute | solution.py:711
  63.9 6.2 %collective-permute-start.4 = (f32[12,8,256]{2,1,0:T(8,128)S(1)}, f32[12,8,256]{2,1,0:T(8,128)S(1)}, u32[]{:S(2)}, u32[]{:S(2)}) collective-permute-start(f32[12,8,256]{2,1,0:T(8,128)S(1)} %all_to_all.27.own_ref), channel_id=1, source_target_pairs={{0,12},{12,24},{24,36},{36,48},{48,60},{60,72},{72,84},{84,96},{96... | collective-permute-start | bytes 294920 | tf_op jit(solution)/shard_map/ppermute | solution.py:711
  70.1 0.4 collective-permute-done.5.hi_ref
  70.5 1.3 collective-permute-done.4.lo_ref
  71.7 1.1 shard_map.70
  72.9 0.2 broadcast_in_dim.9
  73.1 30.8 %all_to_all.28 = f32[64,1,1408]{2,1,0:T(1,128)S(1)} all-to-all(f32[64,1,1408]{2,1,0:T(1,128)S(1)} %broadcast_in_dim.9), channel_id=1, replica_groups=mesh['gx'=64,'gy'=12] {'gx'}, dimensions={0} | all-to-all | bytes 720896 | tf_op jit(solution)/shard_map/all_to_all | solution.py:716
  103.9 9.1 %shard_map.71 = (f32[3,8,8,128]{3,2,1,0:T(8,128)S(1)}, f32[3,8,8,128]{3,2,1,0:T(8,128)S(1)}, f32[8,128]{1,0:T(8,128)S(1)}) custom-call(f32[64,1408]{1,0:T(8,128)S(1)} %bitcast.9, f32[8,7,32,128]{3,2,1,0:T(8,128)S(1)} %get-tuple-element.18.l2_ref, f32[9,16,128]{2,1,0:T(8,128)S(1)} %get-tuple-element.19.m1_ref, f32[9,16,128]{2,1,0:T(8,128)S(1)} %get-tuple-element.20.i1_ref, ...), custom_call_target="tpu_custom_call" | custom-call | tf_op jit(solution)/shard_map/pallas_call | solution.py:660
  113.1 14.6 %all_to_all.29 = f32[64,1,128]{2,1,0:T(1,128)S(1)} all-to-all(f32[64,1,128]{2,1,0:T(1,128)S(1)} %broadcast_in_dim.10), channel_id=1, replica_groups=mesh['gx'=64,'gy'=12] {'gx'}, dimensions={0} | all-to-all | bytes 65536 | tf_op jit(solution)/shard_map/all_to_all | solution.py:716
  127.7 11.4 %all_to_all.30 = f32[12,1,128]{2,1,0:T(1,128)S(1)} all-to-all(f32[12,1,128]{2,1,0:T(1,128)S(1)} %broadcast_in_dim.11), channel_id=1, replica_groups=mesh['gx'=64,'gy'=12] {'gy'}, dimensions={0} | all-to-all | bytes 12288 | tf_op jit(solution)/shard_map/all_to_all | solution.py:716
  139.1 0.8 shard_map.72
  (8 shorter events, 0.1 us)
Async XLA Ops:
  1.7 8.9 %collective-permute-start.1 = (f32[9,8,8,128]{3,2,1,0:T(8,128)S(1)}, f32[9,8,8,128]{3,2,1,0:T(8,128)S(1)}, u32[]{:S(2)}, u32[]{:S(2)}) collective-permute-start(f32[9,8,8,128]{3,2,1,0:T(8,128)S(1)} %shard_map.68.packed_ref), channel_id=1, source_target_pairs={{1,0},{2,1},{3,2},{4,3},{5,4},{6,5},{7,6},{8,7},{9,8},{10,9},{11,1... | collective-permute-start | bytes 884744 | tf_op jit(solution)/shard_map/ppermute | solution.py:711
  3.0 9.1 %collective-permute-start = (f32[9,8,8,128]{3,2,1,0:T(8,128)S(1)}, f32[9,8,8,128]{3,2,1,0:T(8,128)S(1)}, u32[]{:S(2)}, u32[]{:S(2)}) collective-permute-start(f32[9,8,8,128]{3,2,1,0:T(8,128)S(1)} %shard_map.68.packed_ref), channel_id=1, source_target_pairs={{0,1},{1,2},{2,3},{3,4},{4,5},{5,6},{6,7},{7,8},{8,9},{9,10},{10,1... | collective-permute-start | bytes 884744 | tf_op jit(solution)/shard_map/ppermute | solution.py:711
  12.2 17.3 %collective-permute-start.3 = (f32[9,8,24,128]{3,2,1,0:T(8,128)S(1)}, f32[9,8,24,128]{3,2,1,0:T(8,128)S(1)}, u32[]{:S(2)}, u32[]{:S(2)}) collective-permute-start(f32[9,8,24,128]{3,2,1,0:T(8,128)S(1)} %pad_maximum_fusion.own_ref), channel_id=1, source_target_pairs={{12,0},{24,12},{36,24},{48,36},{60,48},{72,60},{84,72},{96,84},{10... | collective-permute-start | bytes 2654216 | tf_op jit(solution)/shard_map/ppermute | solution.py:711
  24.3 11.9 %collective-permute-start.2 = (f32[9,8,24,128]{3,2,1,0:T(8,128)S(1)}, f32[9,8,24,128]{3,2,1,0:T(8,128)S(1)}, u32[]{:S(2)}, u32[]{:S(2)}) collective-permute-start(f32[9,8,24,128]{3,2,1,0:T(8,128)S(1)} %pad_maximum_fusion.own_ref), channel_id=1, source_target_pairs={{0,12},{12,24},{24,36},{36,48},{48,60},{60,72},{72,84},{84,96},{96... | collective-permute-start | bytes 2654216 | tf_op jit(solution)/shard_map/ppermute | solution.py:711
  62.0 8.5 %collective-permute-start.5 = (f32[12,8,256]{2,1,0:T(8,128)S(1)}, f32[12,8,256]{2,1,0:T(8,128)S(1)}, u32[]{:S(2)}, u32[]{:S(2)}) collective-permute-start(f32[12,8,256]{2,1,0:T(8,128)S(1)} %all_to_all.27.own_ref), channel_id=1, source_target_pairs={{12,0},{24,12},{36,24},{48,36},{60,48},{72,60},{84,72},{96,84},{10... | collective-permute-start | bytes 294920 | tf_op jit(solution)/shard_map/ppermute | solution.py:711
  63.9 7.8 %collective-permute-start.4 = (f32[12,8,256]{2,1,0:T(8,128)S(1)}, f32[12,8,256]{2,1,0:T(8,128)S(1)}, u32[]{:S(2)}, u32[]{:S(2)}) collective-permute-start(f32[12,8,256]{2,1,0:T(8,128)S(1)} %all_to_all.27.own_ref), channel_id=1, source_target_pairs={{0,12},{12,24},{24,36},{36,48},{48,60},{60,72},{72,84},{84,96},{96... | collective-permute-start | bytes 294920 | tf_op jit(solution)/shard_map/ppermute | solution.py:711

commit v8 on v7

--- a/solution.py
+++ b/solution.py
@@ -218,12 +218,45 @@
     return jnp.where(free > 0.0, inverse, DAMPING)
 
 
+def low_slab(f):
+    return (0, 7, 14)[f] if f < 3 else 20 + 6 * (f - 3)
+
+
+def high_slab(f):
+    return 0 if f == 0 else 8 + 7 * (f - 1)
+
+
+def join_kernel(lo_ref, mid_ref, hi_ref, own_ref, up_ref, down_ref):
+    for r, ref in enumerate((lo_ref, mid_ref, hi_ref)):
+        rows = slice(8 * r, 8 * r + 8)
+        for f in range(9):
+            v = ref[f]
+            own_ref[f, :, rows, :] = v
+            first = min(f, 1) if f < 3 else 2
+            up_ref[low_slab(f) + first : low_slab(f) + 8, rows, :] = v[first:]
+            last = 8 if f == 0 else 7
+            down_ref[high_slab(f) : high_slab(f) + last, rows, :] = v[:last]
+
+
+def join_call(lo, mid, hi):
+    shapes = [(9, 8, 24, 128), (58, 24, 128), (64, 24, 128)]
+    return pl.pallas_call(
+        join_kernel,
+        out_shape=[jax.ShapeDtypeStruct(shape, F32) for shape in shapes],
+        compiler_params=PARAMS,
+    )(lo, mid, hi)
+
+
 def first_kernel(
     lo_ref, own_ref, hi_ref,
     m_out, i_out, f_out, r_out, m1_out, i1_out, f1_out, c1_out, pack_out,
     t_ref, b_ref, m_ref, i_ref, f_ref, r_ref, s_ref, u_ref, d_ref, v_ref, m1_ref, s1_ref, u1_ref, d1_ref, v2_ref,
 ):
-    pieces = (lo_ref, own_ref, hi_ref)
+    pieces = (
+        lambda f, i: lo_ref[low_slab(f) + i],
+        lambda f, i: own_ref[f, i],
+        lambda f, i: hi_ref[high_slab(f) + i],
+    )
     slab = (24, 128)
     z_up, z_down = z_shifts(True)
     gx, gy = (lax.axis_index("gx"), lax.axis_index("gy"))
@@ -231,13 +264,13 @@
     w0, w1, w2, w3 = [2.0 - math.sqrt(n) for n in range(4)]
 
     def each(first, last, body):
-        for p, ref in enumerate(pieces):
+        for p, get in enumerate(pieces):
             a, b = (max(first, 8 * p), min(last, 8 * p + 7))
             if a <= b:
-                lax.fori_loop(a - 8 * p, b - 8 * p + 1, lambda i, _, ref=ref, p=p: body(8 * p + i, ref, i), None, unroll=True)
-
-    def gather_flat(x, ref, i):
-        own = ref[0, i]
+                lax.fori_loop(a - 8 * p, b - 8 * p + 1, lambda i, _, get=get, p=p: body(8 * p + i, get, i), None, unroll=True)
+
+    def gather_flat(x, get, i):
+        own = get(0, i)
         ring = z_up(own) + z_down(own)
         c1 = y_up(own) + y_down(own) + ring
         c2 = y_up(ring) + y_down(ring)
@@ -254,12 +287,12 @@
     beside = w1 + w2 * (ring_y + ring_z) + w3 * ring_y * ring_z
     inverse_two, inverse_one = (1.0 / (plain + 2.0 * beside), 1.0 / (plain + beside))
 
-    def moduli_of(x, ref, i):
+    def moduli_of(x, get, i):
         at = 8 * gx - 8 + x
         edge = (at == 0) | (at == nodes_x - 1)
         inverse = jnp.where(edge, inverse_one, inverse_two)
         filtered = (b_ref[x] + (t_ref[x - 1] + t_ref[x + 1])) * inverse
-        solid, void = (ref[1, i], ref[2, i])
+        solid, void = (get(1, i), get(2, i))
         physical = (1.0 - void) * (solid + (1.0 - solid) * filtered)
         value = VOID_MODULUS + (1.0 - VOID_MODULUS) * (physical * physical * physical)
         mask = jnp.where((at >= 0) & (at < nodes_x), inside, 0.0)
@@ -267,12 +300,12 @@
 
     each(1, 22, moduli_of)
 
-    def smooth_of(x, ref, i):
+    def smooth_of(x, get, i):
         total = corner_sum(m_ref[x] + m_ref[x - 1], z_down)
         inverse = (DAMPING / DIAG) / total
         i_ref[x] = inverse
         for c in range(3):
-            free, r = (ref[3 + c, i], ref[6 + c, i])
+            free, r = (get(3 + c, i), get(6 + c, i))
             s = scaled(free, inverse) * r
             f_ref[c, x], r_ref[c, x], s_ref[c, x] = (free, r, s)
             u_ref[c, x] = free * s
@@ -730,8 +763,8 @@
         ],
         compiler_params=PARAMS,
     )(*[pltpu.with_memory_space_constraint(v, pltpu.HBM) for v in (density, solid, void, fixed, residual)])
-    own = jnp.concatenate([from_peer(packed, "gy", -1), packed, from_peer(packed, "gy", 1)], axis=2)
-    first = first_call(from_peer(own, "gx", -1), own, from_peer(own, "gx", 1))
+    own, up, down = join_call(from_peer(packed, "gy", -1), packed, from_peer(packed, "gy", 1))
+    first = first_call(from_peer(up, "gx", -1), own, from_peer(down, "gx", 1))
     level0, level1, piece = (first[0:4], first[4:8], first[8])
     columns = spread_all(piece, "gy")
     second = second_call(

time: 140 us -> 139 us (level)
  waiting for transfers between devices: 15.2 us -> 13.4 us
    ppermute x6, waiting for transfers between devices: 15.2 us -> 13.4 us  [from_peer(): lax.ppermute(value, axis, [(i + step, i) for i in range(peers) if 0 <= i...]
  transfers between devices with their start and end apart: 6 -> 6, of which waited for: 6 -> 5; matrix products, arithmetic and copies ran while one was open for 0% -> 0% of each run, Pallas kernels for 0% -> 0%
where the time goes in v8:
time: 139 us; the launch traced here: 138 us
  blocking collectives  77.7 us (56%)
  starting transfers between devices  28.9 us (21%)
  Pallas kernels  17.2 us (12%)
  waiting for transfers between devices  13.4 us (10%)
    all_to_all x4, blocking collectives, spread_all(): lax.all_to_all(jnp.broadcast_to(row[None], (peers,) + row.shape), axis, 0...  77.7 us
    ppermute x6, starting transfers between devices, from_peer(): lax.ppermute(value, axis, [(i + step, i) for i in range(peers) if 0 <= i...  28.9 us
    ppermute x6, waiting for transfers between devices, from_peer(): lax.ppermute(value, axis, [(i + step, i) for i in range(peers) if 0 <= i...  13.4 us
    pallas_call x1, Pallas kernels, third_call(): pl.pallas_call(third_kernel, out_shape=[own, own, jax.ShapeDtypeStruct((8...  9.11 us
    pallas_call x1, Pallas kernels, first_call(): pl.pallas_call(first_kernel, out_shape=[big(12), big(12), big(3, 12), big...  4.99 us
  transfers between devices with their start and end apart: 6, of which 5 were waited for; matrix products, arithmetic and copies ran while one was open for 0% of the time, Pallas kernels for 0%

profile of v8, /device:TPU:1, one launch (start us, length us, event | category | flops | bytes accessed | tf_op | source)
XLA Modules:
  0.0 138.2 jit_solution(16034824436180660805)
XLA Ops:
  0.6 1.0 shard_map.68.mid_ref.packed_ref
  1.7 1.3 collective-permute-start.1
  3.0 5.5 %collective-permute-start = (f32[9,8,8,128]{3,2,1,0:T(8,128)S(1)}, f32[9,8,8,128]{3,2,1,0:T(8,128)S(1)}, u32[]{:S(2)}, u32[]{:S(2)}) collective-permute-start(f32[9,8,8,128]{3,2,1,0:T(8,128)S(1)} %shard_map.68.mid_ref.packed_ref), channel_id=1, source_target_pairs={{0,1},{1,2},{2,3},{3,4},{4,5},{5,6},{6,7},{7,8},{8,9},{9,10},{10,1... | collective-permute-start | bytes 884744 | tf_op jit(solution)/shard_map/ppermute | solution.py:744
  8.5 2.2 %collective-permute-done.1.hi_ref = f32[9,8,8,128]{3,2,1,0:T(8,128)S(1)} collective-permute-done((f32[9,8,8,128]{3,2,1,0:T(8,128)S(1)}, f32[9,8,8,128]{3,2,1,0:T(8,128)S(1)}, u32[]{:S(2)}, u32[]{:S(2)}) %collective-permute-start.1) | collective-permute-done | bytes 294944 | tf_op jit(solution)/shard_map/ppermute | solution.py:744
  10.6 1.5 %collective-permute-done.lo_ref = f32[9,8,8,128]{3,2,1,0:T(8,128)S(1)} collective-permute-done((f32[9,8,8,128]{3,2,1,0:T(8,128)S(1)}, f32[9,8,8,128]{3,2,1,0:T(8,128)S(1)}, u32[]{:S(2)}, u32[]{:S(2)}) %collective-permute-start) | collective-permute-done | bytes 294944 | tf_op jit(solution)/shard_map/ppermute | solution.py:744
  12.1 0.2 shard_map.69
  12.3 12.1 %collective-permute-start.3 = (f32[64,24,128]{2,1,0:T(8,128)S(1)}, f32[64,24,128]{2,1,0:T(8,128)S(1)}, u32[]{:S(2)}, u32[]{:S(2)}) collective-permute-start(f32[64,24,128]{2,1,0:T(8,128)S(1)} %get-tuple-element.21), channel_id=1, source_target_pairs={{12,0},{24,12},{36,24},{48,36},{60,48},{72,60},{84,72},{96,84},{10... | collective-permute-start | bytes 2359304 | tf_op jit(solution)/shard_map/ppermute | solution.py:744
  24.4 1.9 %collective-permute-start.2 = (f32[58,24,128]{2,1,0:T(8,128)S(1)}, f32[58,24,128]{2,1,0:T(8,128)S(1)}, u32[]{:S(2)}, u32[]{:S(2)}) collective-permute-start(f32[58,24,128]{2,1,0:T(8,128)S(1)} %get-tuple-element.19), channel_id=1, source_target_pairs={{0,12},{12,24},{24,36},{36,48},{48,60},{60,72},{72,84},{84,96},{96... | collective-permute-start | bytes 2138120 | tf_op jit(solution)/shard_map/ppermute | solution.py:744
  26.3 8.1 %collective-permute-done.2.lo_ref = f32[58,24,128]{2,1,0:T(8,128)S(1)} collective-permute-done((f32[58,24,128]{2,1,0:T(8,128)S(1)}, f32[58,24,128]{2,1,0:T(8,128)S(1)}, u32[]{:S(2)}, u32[]{:S(2)}) %collective-permute-start.2) | collective-permute-done | bytes 712736 | tf_op jit(solution)/shard_map/ppermute | solution.py:744
  34.4 0.0 collective-permute-done.3.hi_ref
  34.4 5.0 %shard_map.70 = (f32[12,16,128]{2,1,0:T(8,128)S(1)}, f32[12,16,128]{2,1,0:T(8,128)S(1)}, f32[3,12,16,128]{3,2,1,0:T(8,128)S(1)}, f32[3,12,16,128]{3,2,1,0:T(8,12...) custom-call(f32[58,24,128]{2,1,0:T(8,128)S(1)} %collective-permute-d, ...), custom_call_target="tpu_custom_call" | custom-call | tf_op jit(solution)/shard_map/pallas_call | solution.py:419
  39.4 20.9 %all_to_all.27.own_ref = f32[12,8,256]{2,1,0:T(8,128)S(1)} all-to-all(f32[12,8,256]{2,1,0:T(8,128)S(1)} %broadcast_in_dim.8), channel_id=1, replica_groups=mesh['gx'=64,'gy'=12] {'gy'}, dimensions={0} | all-to-all | bytes 196608 | tf_op jit(solution)/shard_map/all_to_all | solution.py:749
  60.3 1.9 %collective-permute-start.5 = (f32[12,8,256]{2,1,0:T(8,128)S(1)}, f32[12,8,256]{2,1,0:T(8,128)S(1)}, u32[]{:S(2)}, u32[]{:S(2)}) collective-permute-start(f32[12,8,256]{2,1,0:T(8,128)S(1)} %all_to_all.27.own_ref), channel_id=1, source_target_pairs={{12,0},{24,12},{36,24},{48,36},{60,48},{72,60},{84,72},{96,84},{10... | collective-permute-start | bytes 294920 | tf_op jit(solution)/shard_map/ppermute | solution.py:744
  62.2 6.2 %collective-permute-start.4 = (f32[12,8,256]{2,1,0:T(8,128)S(1)}, f32[12,8,256]{2,1,0:T(8,128)S(1)}, u32[]{:S(2)}, u32[]{:S(2)}) collective-permute-start(f32[12,8,256]{2,1,0:T(8,128)S(1)} %all_to_all.27.own_ref), channel_id=1, source_target_pairs={{0,12},{12,24},{24,36},{36,48},{48,60},{60,72},{72,84},{84,96},{96... | collective-permute-start | bytes 294920 | tf_op jit(solution)/shard_map/ppermute | solution.py:744
  68.4 0.4 collective-permute-done.5.hi_ref
  68.7 1.3 collective-permute-done.4.lo_ref
  70.0 1.1 shard_map.71
  71.1 0.2 broadcast_in_dim.9
  71.3 30.8 %all_to_all.28 = f32[64,1,1408]{2,1,0:T(1,128)S(1)} all-to-all(f32[64,1,1408]{2,1,0:T(1,128)S(1)} %broadcast_in_dim.9), channel_id=1, replica_groups=mesh['gx'=64,'gy'=12] {'gx'}, dimensions={0} | all-to-all | bytes 720896 | tf_op jit(solution)/shard_map/all_to_all | solution.py:749
  102.2 9.1 %shard_map.72 = (f32[3,8,8,128]{3,2,1,0:T(8,128)S(1)}, f32[3,8,8,128]{3,2,1,0:T(8,128)S(1)}, f32[8,128]{1,0:T(8,128)S(1)}) custom-call(f32[64,1408]{1,0:T(8,128)S(1)} %bitcast.9, f32[8,7,32,128]{3,2,1,0:T(8,128)S(1)} %get-tuple-element.24.l2_ref, f32[9,16,128]{2,1,0:T(8,128)S(1)} %get-tuple-element.25.m1_ref, f32[9,16,128]{2,1,0:T(8,128)S(1)} %get-tuple-element.26.i1_ref, ...), custom_call_target="tpu_custom_call" | custom-call | tf_op jit(solution)/shard_map/pallas_call | solution.py:693
  111.3 14.6 %all_to_all.29 = f32[64,1,128]{2,1,0:T(1,128)S(1)} all-to-all(f32[64,1,128]{2,1,0:T(1,128)S(1)} %broadcast_in_dim.10), channel_id=1, replica_groups=mesh['gx'=64,'gy'=12] {'gx'}, dimensions={0} | all-to-all | bytes 65536 | tf_op jit(solution)/shard_map/all_to_all | solution.py:749
  126.0 11.4 %all_to_all.30 = f32[12,1,128]{2,1,0:T(1,128)S(1)} all-to-all(f32[12,1,128]{2,1,0:T(1,128)S(1)} %broadcast_in_dim.11), channel_id=1, replica_groups=mesh['gx'=64,'gy'=12] {'gy'}, dimensions={0} | all-to-all | bytes 12288 | tf_op jit(solution)/shard_map/all_to_all | solution.py:749
  137.4 0.8 shard_map.73
  (8 shorter events, 0.1 us)
Async XLA Ops:
  1.7 8.9 %collective-permute-start.1 = (f32[9,8,8,128]{3,2,1,0:T(8,128)S(1)}, f32[9,8,8,128]{3,2,1,0:T(8,128)S(1)}, u32[]{:S(2)}, u32[]{:S(2)}) collective-permute-start(f32[9,8,8,128]{3,2,1,0:T(8,128)S(1)} %shard_map.68.mid_ref.packed_ref), channel_id=1, source_target_pairs={{1,0},{2,1},{3,2},{4,3},{5,4},{6,5},{7,6},{8,7},{9,8},{10,9},{11,1... | collective-permute-start | bytes 884744 | tf_op jit(solution)/shard_map/ppermute | solution.py:744
  3.0 9.1 %collective-permute-start = (f32[9,8,8,128]{3,2,1,0:T(8,128)S(1)}, f32[9,8,8,128]{3,2,1,0:T(8,128)S(1)}, u32[]{:S(2)}, u32[]{:S(2)}) collective-permute-start(f32[9,8,8,128]{3,2,1,0:T(8,128)S(1)} %shard_map.68.mid_ref.packed_ref), channel_id=1, source_target_pairs={{0,1},{1,2},{2,3},{3,4},{4,5},{5,6},{6,7},{7,8},{8,9},{9,10},{10,1... | collective-permute-start | bytes 884744 | tf_op jit(solution)/shard_map/ppermute | solution.py:744
  12.3 22.2 %collective-permute-start.3 = (f32[64,24,128]{2,1,0:T(8,128)S(1)}, f32[64,24,128]{2,1,0:T(8,128)S(1)}, u32[]{:S(2)}, u32[]{:S(2)}) collective-permute-start(f32[64,24,128]{2,1,0:T(8,128)S(1)} %get-tuple-element.21), channel_id=1, source_target_pairs={{12,0},{24,12},{36,24},{48,36},{60,48},{72,60},{84,72},{96,84},{10... | collective-permute-start | bytes 2359304 | tf_op jit(solution)/shard_map/ppermute | solution.py:744
  24.4 10.1 %collective-permute-start.2 = (f32[58,24,128]{2,1,0:T(8,128)S(1)}, f32[58,24,128]{2,1,0:T(8,128)S(1)}, u32[]{:S(2)}, u32[]{:S(2)}) collective-permute-start(f32[58,24,128]{2,1,0:T(8,128)S(1)} %get-tuple-element.19), channel_id=1, source_target_pairs={{0,12},{12,24},{24,36},{36,48},{48,60},{60,72},{72,84},{84,96},{96... | collective-permute-start | bytes 2138120 | tf_op jit(solution)/shard_map/ppermute | solution.py:744
  60.3 8.5 %collective-permute-start.5 = (f32[12,8,256]{2,1,0:T(8,128)S(1)}, f32[12,8,256]{2,1,0:T(8,128)S(1)}, u32[]{:S(2)}, u32[]{:S(2)}) collective-permute-start(f32[12,8,256]{2,1,0:T(8,128)S(1)} %all_to_all.27.own_ref), channel_id=1, source_target_pairs={{12,0},{24,12},{36,24},{48,36},{60,48},{72,60},{84,72},{96,84},{10... | collective-permute-start | bytes 294920 | tf_op jit(solution)/shard_map/ppermute | solution.py:744
  62.2 7.8 %collective-permute-start.4 = (f32[12,8,256]{2,1,0:T(8,128)S(1)}, f32[12,8,256]{2,1,0:T(8,128)S(1)}, u32[]{:S(2)}, u32[]{:S(2)}) collective-permute-start(f32[12,8,256]{2,1,0:T(8,128)S(1)} %all_to_all.27.own_ref), channel_id=1, source_target_pairs={{0,12},{12,24},{24,36},{36,48},{48,60},{60,72},{72,84},{84,96},{96... | collective-permute-start | bytes 294920 | tf_op jit(solution)/shard_map/ppermute | solution.py:744

commit v9 on v8

--- a/solution.py
+++ b/solution.py
@@ -326,7 +326,7 @@
             f_out[c, x] = f_ref[c, x + 6, 4:20, :]
             r_out[c, x] = r_ref[c, x + 6, 4:20, :]
 
-    lax.fori_loop(0, 12, keep, None, unroll=2)
+    lax.fori_loop(0, 12, keep, None, unroll=True)
 
     v_ref[:, 24:32, :] = jnp.zeros((64, 8, 128), F32)
 
@@ -337,14 +337,14 @@
             v_ref[9 * c + n, 0:24, :] = smooth_rows(v)
             v_ref[27 + 9 * c + n, 0:24, :] = f_ref[c, x]
 
-    lax.fori_loop(0, 9, to_coarse, None, unroll=3)
+    lax.fori_loop(0, 9, to_coarse, None, unroll=True)
 
     def to_coarse_moduli(n, _):
         x = 2 * n + 2
         v = m_ref[x] + m_ref[x + 1]
         v_ref[54 + n, 0:24, :] = v + y_up(v)
 
-    lax.fori_loop(0, 10, to_coarse_moduli, None, unroll=5)
+    lax.fori_loop(0, 10, to_coarse_moduli, None, unroll=True)
 
     def half(first, count, matrix):
         v = v_ref[first : first + count, pl.ds(0, 16, stride=2), :]
@@ -772,11 +772,11 @@
     )
     rows = spread_all(second[1].reshape(-1), "gx")
     precond, image, sums = third_call(rows, second[0], level1, level0)
-    sums = jnp.sum(spread_all(sums[0], "gx"), axis=0)
+    sums = jnp.sum(spread_all(sums[0], "gy"), axis=0)
     block = jax.ShapeDtypeStruct(residual.shape, F32)
     return tuple(
         pl.pallas_call(last_kernel, out_shape=[block, block], compiler_params=PARAMS)(
-            spread_all(sums, "gy"), precond, image, packed
+            spread_all(sums, "gx"), precond, image, packed
         )
     )
 

time: 139 us -> 139 us (level)
  no operation moved by 1% of the time
where the time goes in v9:
time: 139 us; the launch traced here: 138 us
  blocking collectives  78.8 us (57%)
  starting transfers between devices  28.9 us (21%)
  Pallas kernels  16.3 us (12%)
  waiting for transfers between devices  13.4 us (10%)
    all_to_all x4, blocking collectives, spread_all(): lax.all_to_all(jnp.broadcast_to(row[None], (peers,) + row.shape), axis, 0...  78.8 us
    ppermute x6, starting transfers between devices, from_peer(): lax.ppermute(value, axis, [(i + step, i) for i in range(peers) if 0 <= i...  28.9 us
    ppermute x6, waiting for transfers between devices, from_peer(): lax.ppermute(value, axis, [(i + step, i) for i in range(peers) if 0 <= i...  13.4 us
    pallas_call x1, Pallas kernels, third_call(): pl.pallas_call(third_kernel, out_shape=[own, own, jax.ShapeDtypeStruct((8...  9.11 us
    pallas_call x1, Pallas kernels, first_call(): pl.pallas_call(first_kernel, out_shape=[big(12), big(12), big(3, 12), big...  4.1 us
  transfers between devices with their start and end apart: 6, of which 5 were waited for; matrix products, arithmetic and copies ran while one was open for 0% of the time, Pallas kernels for 0%

profile of v9, /device:TPU:1, one launch (start us, length us, event | category | flops | bytes accessed | tf_op | source)
XLA Modules:
  0.0 138.5 jit_solution(9811575563682793122)
XLA Ops:
  0.6 1.0 shard_map.68.mid_ref.packed_ref
  1.7 1.3 collective-permute-start.1
  3.0 5.5 %collective-permute-start = (f32[9,8,8,128]{3,2,1,0:T(8,128)S(1)}, f32[9,8,8,128]{3,2,1,0:T(8,128)S(1)}, u32[]{:S(2)}, u32[]{:S(2)}) collective-permute-start(f32[9,8,8,128]{3,2,1,0:T(8,128)S(1)} %shard_map.68.mid_ref.packed_ref), channel_id=1, source_target_pairs={{0,1},{1,2},{2,3},{3,4},{4,5},{5,6},{6,7},{7,8},{8,9},{9,10},{10,1... | collective-permute-start | bytes 884744 | tf_op jit(solution)/shard_map/ppermute | solution.py:744
  8.5 2.2 %collective-permute-done.1.hi_ref = f32[9,8,8,128]{3,2,1,0:T(8,128)S(1)} collective-permute-done((f32[9,8,8,128]{3,2,1,0:T(8,128)S(1)}, f32[9,8,8,128]{3,2,1,0:T(8,128)S(1)}, u32[]{:S(2)}, u32[]{:S(2)}) %collective-permute-start.1) | collective-permute-done | bytes 294944 | tf_op jit(solution)/shard_map/ppermute | solution.py:744
  10.6 1.5 %collective-permute-done.lo_ref = f32[9,8,8,128]{3,2,1,0:T(8,128)S(1)} collective-permute-done((f32[9,8,8,128]{3,2,1,0:T(8,128)S(1)}, f32[9,8,8,128]{3,2,1,0:T(8,128)S(1)}, u32[]{:S(2)}, u32[]{:S(2)}) %collective-permute-start) | collective-permute-done | bytes 294944 | tf_op jit(solution)/shard_map/ppermute | solution.py:744
  12.1 0.2 shard_map.69
  12.3 12.1 %collective-permute-start.3 = (f32[64,24,128]{2,1,0:T(8,128)S(1)}, f32[64,24,128]{2,1,0:T(8,128)S(1)}, u32[]{:S(2)}, u32[]{:S(2)}) collective-permute-start(f32[64,24,128]{2,1,0:T(8,128)S(1)} %get-tuple-element.21), channel_id=1, source_target_pairs={{12,0},{24,12},{36,24},{48,36},{60,48},{72,60},{84,72},{96,84},{10... | collective-permute-start | bytes 2359304 | tf_op jit(solution)/shard_map/ppermute | solution.py:744
  24.4 1.9 %collective-permute-start.2 = (f32[58,24,128]{2,1,0:T(8,128)S(1)}, f32[58,24,128]{2,1,0:T(8,128)S(1)}, u32[]{:S(2)}, u32[]{:S(2)}) collective-permute-start(f32[58,24,128]{2,1,0:T(8,128)S(1)} %get-tuple-element.19), channel_id=1, source_target_pairs={{0,12},{12,24},{24,36},{36,48},{48,60},{60,72},{72,84},{84,96},{96... | collective-permute-start | bytes 2138120 | tf_op jit(solution)/shard_map/ppermute | solution.py:744
  26.3 8.1 %collective-permute-done.2.lo_ref = f32[58,24,128]{2,1,0:T(8,128)S(1)} collective-permute-done((f32[58,24,128]{2,1,0:T(8,128)S(1)}, f32[58,24,128]{2,1,0:T(8,128)S(1)}, u32[]{:S(2)}, u32[]{:S(2)}) %collective-permute-start.2) | collective-permute-done | bytes 712736 | tf_op jit(solution)/shard_map/ppermute | solution.py:744
  34.4 0.0 collective-permute-done.3.hi_ref
  34.4 4.1 %shard_map.70 = (f32[12,16,128]{2,1,0:T(8,128)S(1)}, f32[12,16,128]{2,1,0:T(8,128)S(1)}, f32[3,12,16,128]{3,2,1,0:T(8,128)S(1)}, f32[3,12,16,128]{3,2,1,0:T(8,12...) custom-call(f32[58,24,128]{2,1,0:T(8,128)S(1)} %collective-permute-d, ...), custom_call_target="tpu_custom_call" | custom-call | tf_op jit(solution)/shard_map/pallas_call | solution.py:419
  38.5 20.9 %all_to_all.27.own_ref = f32[12,8,256]{2,1,0:T(8,128)S(1)} all-to-all(f32[12,8,256]{2,1,0:T(8,128)S(1)} %broadcast_in_dim.8), channel_id=1, replica_groups=mesh['gx'=64,'gy'=12] {'gy'}, dimensions={0} | all-to-all | bytes 196608 | tf_op jit(solution)/shard_map/all_to_all | solution.py:749
  59.4 1.9 %collective-permute-start.5 = (f32[12,8,256]{2,1,0:T(8,128)S(1)}, f32[12,8,256]{2,1,0:T(8,128)S(1)}, u32[]{:S(2)}, u32[]{:S(2)}) collective-permute-start(f32[12,8,256]{2,1,0:T(8,128)S(1)} %all_to_all.27.own_ref), channel_id=1, source_target_pairs={{12,0},{24,12},{36,24},{48,36},{60,48},{72,60},{84,72},{96,84},{10... | collective-permute-start | bytes 294920 | tf_op jit(solution)/shard_map/ppermute | solution.py:744
  61.3 6.2 %collective-permute-start.4 = (f32[12,8,256]{2,1,0:T(8,128)S(1)}, f32[12,8,256]{2,1,0:T(8,128)S(1)}, u32[]{:S(2)}, u32[]{:S(2)}) collective-permute-start(f32[12,8,256]{2,1,0:T(8,128)S(1)} %all_to_all.27.own_ref), channel_id=1, source_target_pairs={{0,12},{12,24},{24,36},{36,48},{48,60},{60,72},{72,84},{84,96},{96... | collective-permute-start | bytes 294920 | tf_op jit(solution)/shard_map/ppermute | solution.py:744
  67.5 0.4 collective-permute-done.5.hi_ref
  67.8 1.3 collective-permute-done.4.lo_ref
  69.1 1.1 shard_map.71
  70.3 0.2 broadcast_in_dim.9
  70.4 30.8 %all_to_all.28 = f32[64,1,1408]{2,1,0:T(1,128)S(1)} all-to-all(f32[64,1,1408]{2,1,0:T(1,128)S(1)} %broadcast_in_dim.9), channel_id=1, replica_groups=mesh['gx'=64,'gy'=12] {'gx'}, dimensions={0} | all-to-all | bytes 720896 | tf_op jit(solution)/shard_map/all_to_all | solution.py:749
  101.3 9.1 %shard_map.72 = (f32[3,8,8,128]{3,2,1,0:T(8,128)S(1)}, f32[3,8,8,128]{3,2,1,0:T(8,128)S(1)}, f32[8,128]{1,0:T(8,128)S(1)}) custom-call(f32[64,1408]{1,0:T(8,128)S(1)} %bitcast.6, f32[8,7,32,128]{3,2,1,0:T(8,128)S(1)} %get-tuple-element.24.l2_ref, f32[9,16,128]{2,1,0:T(8,128)S(1)} %get-tuple-element.25.m1_ref, f32[9,16,128]{2,1,0:T(8,128)S(1)} %get-tuple-element.26.i1_ref, ...), custom_call_target="tpu_custom_call" | custom-call | tf_op jit(solution)/shard_map/pallas_call | solution.py:693
  110.4 11.4 %all_to_all.29 = f32[12,1,128]{2,1,0:T(1,128)S(1)} all-to-all(f32[12,1,128]{2,1,0:T(1,128)S(1)} %broadcast_in_dim.10), channel_id=1, replica_groups=mesh['gx'=64,'gy'=12] {'gy'}, dimensions={0} | all-to-all | bytes 12288 | tf_op jit(solution)/shard_map/all_to_all | solution.py:749
  121.9 15.8 %all_to_all.30 = f32[64,1,128]{2,1,0:T(1,128)S(1)} all-to-all(f32[64,1,128]{2,1,0:T(1,128)S(1)} %broadcast_in_dim.11), channel_id=1, replica_groups=mesh['gx'=64,'gy'=12] {'gx'}, dimensions={0} | all-to-all | bytes 65536 | tf_op jit(solution)/shard_map/all_to_all | solution.py:749
  137.6 0.8 shard_map.73
  (7 shorter events, 0.1 us)
Async XLA Ops:
  1.7 8.9 %collective-permute-start.1 = (f32[9,8,8,128]{3,2,1,0:T(8,128)S(1)}, f32[9,8,8,128]{3,2,1,0:T(8,128)S(1)}, u32[]{:S(2)}, u32[]{:S(2)}) collective-permute-start(f32[9,8,8,128]{3,2,1,0:T(8,128)S(1)} %shard_map.68.mid_ref.packed_ref), channel_id=1, source_target_pairs={{1,0},{2,1},{3,2},{4,3},{5,4},{6,5},{7,6},{8,7},{9,8},{10,9},{11,1... | collective-permute-start | bytes 884744 | tf_op jit(solution)/shard_map/ppermute | solution.py:744
  3.0 9.1 %collective-permute-start = (f32[9,8,8,128]{3,2,1,0:T(8,128)S(1)}, f32[9,8,8,128]{3,2,1,0:T(8,128)S(1)}, u32[]{:S(2)}, u32[]{:S(2)}) collective-permute-start(f32[9,8,8,128]{3,2,1,0:T(8,128)S(1)} %shard_map.68.mid_ref.packed_ref), channel_id=1, source_target_pairs={{0,1},{1,2},{2,3},{3,4},{4,5},{5,6},{6,7},{7,8},{8,9},{9,10},{10,1... | collective-permute-start | bytes 884744 | tf_op jit(solution)/shard_map/ppermute | solution.py:744
  12.3 22.2 %collective-permute-start.3 = (f32[64,24,128]{2,1,0:T(8,128)S(1)}, f32[64,24,128]{2,1,0:T(8,128)S(1)}, u32[]{:S(2)}, u32[]{:S(2)}) collective-permute-start(f32[64,24,128]{2,1,0:T(8,128)S(1)} %get-tuple-element.21), channel_id=1, source_target_pairs={{12,0},{24,12},{36,24},{48,36},{60,48},{72,60},{84,72},{96,84},{10... | collective-permute-start | bytes 2359304 | tf_op jit(solution)/shard_map/ppermute | solution.py:744
  24.4 10.1 %collective-permute-start.2 = (f32[58,24,128]{2,1,0:T(8,128)S(1)}, f32[58,24,128]{2,1,0:T(8,128)S(1)}, u32[]{:S(2)}, u32[]{:S(2)}) collective-permute-start(f32[58,24,128]{2,1,0:T(8,128)S(1)} %get-tuple-element.19), channel_id=1, source_target_pairs={{0,12},{12,24},{24,36},{36,48},{48,60},{60,72},{72,84},{84,96},{96... | collective-permute-start | bytes 2138120 | tf_op jit(solution)/shard_map/ppermute | solution.py:744
  59.4 8.5 %collective-permute-start.5 = (f32[12,8,256]{2,1,0:T(8,128)S(1)}, f32[12,8,256]{2,1,0:T(8,128)S(1)}, u32[]{:S(2)}, u32[]{:S(2)}) collective-permute-start(f32[12,8,256]{2,1,0:T(8,128)S(1)} %all_to_all.27.own_ref), channel_id=1, source_target_pairs={{12,0},{24,12},{36,24},{48,36},{60,48},{72,60},{84,72},{96,84},{10... | collective-permute-start | bytes 294920 | tf_op jit(solution)/shard_map/ppermute | solution.py:744
  61.3 7.8 %collective-permute-start.4 = (f32[12,8,256]{2,1,0:T(8,128)S(1)}, f32[12,8,256]{2,1,0:T(8,128)S(1)}, u32[]{:S(2)}, u32[]{:S(2)}) collective-permute-start(f32[12,8,256]{2,1,0:T(8,128)S(1)} %all_to_all.27.own_ref), channel_id=1, source_target_pairs={{0,12},{12,24},{24,36},{36,48},{48,60},{60,72},{72,84},{84,96},{96... | collective-permute-start | bytes 294920 | tf_op jit(solution)/shard_map/ppermute | solution.py:744
